TPU v7x, 128 devices: a whole 4x4x4 slice. The times are simulated.
128 devices in a mesh: section: 2 (over x_lo), dp: 64 (over x_hi, z, y, core).
Axes of the slice: x: 4 (x_hi: 2, x_lo: 2; x = x_hi * 2 + x_lo), y: 4, z: 4, core: 2. Of those that a mesh axis runs over, the one named last changes fastest.
Arguments:
- tokens: bfloat16 [8192, 1024], P('dp'), may hold values from -6 to 6
- segment_ids: int32 [8192], P('dp'), may hold values from 0 to 255, never falling along the last dimension, each value on 1 to 64 neighbouring positions
- gains: bfloat16 [2, 2, 1024], P('section', None, 'dp'), may hold values from 0.5 to 1.5
- biases: bfloat16 [2, 10, 1024], P('section', None, 'dp'), may hold values from -4 to 4
- w_qkv: bfloat16 [2, 1024, 3072], P('section', None, 'dp'), may hold values from -0.1875 to 0.1875
- w_proj: bfloat16 [2, 1024, 1024], P('section', None, 'dp'), may hold values from -0.375 to 0.375
- w_fc: bfloat16 [2, 1024, 4096], P('section', None, 'dp'), may hold values from -0.1875 to 0.1875
- w_out: bfloat16 [2, 4096, 1024], P('section', None, 'dp'), may hold values from -0.09375 to 0.09375
- cotangent: bfloat16 [8192, 1024], P('dp'), may hold values from -16 to 16
Outputs:
- activations: bfloat16 [2, 8192, 1024], P('section', 'dp')
- input_grads: bfloat16 [2, 8192, 1024], P('section', 'dp')
- grad_gains: float32 [2, 2, 1024], P('section', None, 'dp')
- grad_biases: float32 [2, 10, 1024], P('section', None, 'dp')
- grad_qkv: float32 [2, 1024, 3072], P('section', None, 'dp')
- grad_proj: float32 [2, 1024, 1024], P('section', None, 'dp')
- grad_fc: float32 [2, 1024, 4096], P('section', None, 'dp')
- grad_out: float32 [2, 4096, 1024], P('section', None, 'dp')
Inputs may be any that keep to these rules, and one draw needn't show every extreme that they name: `segment_ids`: document numbers never fall along the tokens; each document has 1 to 64 tokens and one has exactly 64.
All inputs are finite; a program needn't handle non-finite values.
Results may differ from a plain program's by a relative error of at most 0.015.
Values may be sent and summed in bfloat16 or wider, within the bound.
A program may use at most 256 MiB of HBM per device.

v0:
```python
import jax
import jax.numpy as jnp
from jax import lax
from jax.sharding import PartitionSpec as P

HEAD = 64
MB_TOK = 64
MICRO = 2


EPS = 1e-05


def shifted(value, axis, steps):
    count = lax.axis_size(axis)
    first, last = (max(0, -steps), min(count, count - steps))
    return lax.ppermute(value, axis, [(source, source + steps) for source in range(first, last)])


def norm_rows(values, gain, shift):
    centre = values - jnp.mean(values, axis=-1, keepdims=True)
    spread = jnp.mean(centre * centre, axis=-1, keepdims=True)
    return centre * lax.rsqrt(spread + EPS) * gain + shift


def gelu_tanh(values):
    return jax.nn.gelu(values, approximate=True)


def score_mask(seg):
    order = jnp.arange(seg.shape[0])
    return (seg[:, None] == seg[None, :]) & (order[None, :] <= order[:, None])


def forward_block(inp, seg, weights):
    gains_low, biases_low, w_qkv, w_proj, w_fc, w_out = weights
    rows, width = inp.shape
    heads = width // HEAD
    gains = gains_low.astype(jnp.float32)
    biases = biases_low.astype(jnp.float32)
    first = norm_rows(inp, gains[0], biases[0]).astype(jnp.bfloat16)
    mixed = jnp.dot(first, w_qkv, preferred_element_type=jnp.float32)
    query = (mixed[:, :width] + biases[1]).astype(jnp.bfloat16).reshape(rows, heads, HEAD)
    keys = mixed[:, width : 2 * width].astype(jnp.bfloat16).reshape(rows, heads, HEAD)
    values = (mixed[:, 2 * width :] + biases[2]).astype(jnp.bfloat16).reshape(rows, heads, HEAD)
    scores = jnp.einsum("qhd,khd->hqk", query, keys, preferred_element_type=jnp.float32) * HEAD ** (
        -0.5
    )
    scores = jnp.where(score_mask(seg)[None], scores, -1e30)
    probs = jax.nn.softmax(scores, axis=-1)
    probs_low = probs.astype(jnp.bfloat16)
    attended = jnp.einsum("hqk,khd->qhd", probs_low, values, preferred_element_type=jnp.float32)
    attended = attended.reshape(rows, width).astype(jnp.bfloat16)
    middle = inp + (jnp.dot(attended, w_proj, preferred_element_type=jnp.float32) + biases[3])
    second = norm_rows(middle, gains[1], biases[4]).astype(jnp.bfloat16)
    pre = jnp.dot(second, w_fc, preferred_element_type=jnp.float32) + biases[5:9].reshape(-1)
    act = gelu_tanh(pre).astype(jnp.bfloat16)
    result = middle + (jnp.dot(act, w_out, preferred_element_type=jnp.float32) + biases[9])
    saved = (first, query, keys, values, probs, probs_low, attended, middle, second, pre, act)
    return (result, saved)


def backward_block(inp, seg, weights, d_result):
    gains_low, biases_low, w_qkv, w_proj, w_fc, w_out = weights
    rows, width = inp.shape
    heads = width // HEAD
    gains = gains_low.astype(jnp.float32)
    biases = biases_low.astype(jnp.float32)
    ignored, saved = forward_block(inp, seg, weights)
    first, query, keys, values, probs, probs_low, attended, middle, second, pre, act = saved
    d_final = d_result.astype(jnp.bfloat16)
    g_wout = jnp.dot(act.T, d_final, preferred_element_type=jnp.float32)
    g_bout = jnp.sum(d_final.astype(jnp.float32), axis=0)
    d_act = jnp.dot(d_final, w_out.T, preferred_element_type=jnp.float32)
    unused, gelu_pull = jax.vjp(gelu_tanh, pre)
    d_pre = gelu_pull(d_act)[0].astype(jnp.bfloat16)
    g_wfc = jnp.dot(second.T, d_pre, preferred_element_type=jnp.float32)
    g_bfc = jnp.sum(d_pre.astype(jnp.float32), axis=0)
    d_second = jnp.dot(d_pre, w_fc.T, preferred_element_type=jnp.float32)
    unused, second_pull = jax.vjp(norm_rows, middle, gains[1], biases[4])
    d_mid_norm, g_gain_two, g_shift_two = second_pull(d_second)
    d_middle = d_result + d_mid_norm
    d_branch = d_middle.astype(jnp.bfloat16)
    g_wproj = jnp.dot(attended.T, d_branch, preferred_element_type=jnp.float32)
    g_bproj = jnp.sum(d_branch.astype(jnp.float32), axis=0)
    d_att = jnp.dot(d_branch, w_proj.T, preferred_element_type=jnp.float32).astype(jnp.bfloat16)
    d_att = d_att.reshape(rows, heads, HEAD)
    d_values = jnp.einsum("hqk,qhd->khd", probs_low, d_att, preferred_element_type=jnp.float32)
    d_probs = jnp.einsum("qhd,khd->hqk", d_att, values, preferred_element_type=jnp.float32)
    d_scores = (probs * (d_probs - jnp.sum(d_probs * probs, axis=-1, keepdims=True))).astype(
        jnp.bfloat16
    )
    d_query = jnp.einsum(
        "hqk,khd->qhd", d_scores, keys, preferred_element_type=jnp.float32
    ) * HEAD ** (-0.5)
    d_keys = jnp.einsum(
        "hqk,qhd->khd", d_scores, query, preferred_element_type=jnp.float32
    ) * HEAD ** (-0.5)
    d_mixed = jnp.concatenate(
        [d_query.reshape(rows, width), d_keys.reshape(rows, width), d_values.reshape(rows, width)],
        axis=1,
    ).astype(jnp.bfloat16)
    g_wqkv = jnp.dot(first.T, d_mixed, preferred_element_type=jnp.float32)
    column_sums = jnp.sum(d_mixed.astype(jnp.float32), axis=0)
    d_first = jnp.dot(d_mixed, w_qkv.T, preferred_element_type=jnp.float32)
    unused, first_pull = jax.vjp(norm_rows, inp, gains[0], biases[0])
    d_inp_norm, g_gain_one, g_shift_one = first_pull(d_first)
    d_inp = d_middle + d_inp_norm
    g_gains = jnp.stack([g_gain_one, g_gain_two])
    g_biases = jnp.concatenate(
        [
            jnp.stack(
                [g_shift_one, column_sums[:width], column_sums[2 * width :], g_bproj, g_shift_two]
            ),
            g_bfc.reshape(4, width),
            g_bout[None],
        ],
        axis=0,
    )
    return ((g_gains, g_biases, g_wqkv, g_wproj, g_wfc, g_wout), d_inp)


def pick(array, index):
    return lax.dynamic_index_in_dim(array, index, 0, keepdims=False)


def place(array, index, valid, update):
    kept = pick(array, index)
    return lax.dynamic_update_index_in_dim(array, jnp.where(valid, update, kept), index, 0)


def local(tokens, segment_ids, gains, biases, w_qkv, w_proj, w_fc, w_out, cotangent):
    section = lax.axis_index("section")
    tok_rows, width = tokens.shape
    token_parts = tokens.reshape(MICRO, MB_TOK, width)
    seg_parts = segment_ids.reshape(MICRO, MB_TOK)
    cot_parts = cotangent.reshape(MICRO, MB_TOK, width)
    gathered = (
        lax.all_gather(gains, "dp", axis=2, tiled=True),
        lax.all_gather(biases, "dp", axis=2, tiled=True),
        lax.all_gather(w_qkv, "dp", axis=2, tiled=True),
        lax.all_gather(w_proj, "dp", axis=2, tiled=True),
        lax.all_gather(w_fc, "dp", axis=2, tiled=True),
        lax.all_gather(w_out, "dp", axis=2, tiled=True),
    )
    weights = tuple((member[0] for member in gathered))
    inputs = jnp.zeros((MICRO, MB_TOK, width), jnp.bfloat16)
    results = jnp.zeros((MICRO, MB_TOK, width), jnp.bfloat16)
    arriving = jnp.zeros((MB_TOK, width), jnp.bfloat16)
    for tick in range(MICRO + 1):
        index = tick - section
        valid = (index >= 0) & (index < MICRO)
        safe = jnp.clip(index, 0, MICRO - 1)
        source = jnp.where(section == 0, token_parts[min(tick, MICRO - 1)], arriving)
        result, unused = forward_block(source.astype(jnp.float32), pick(seg_parts, safe), weights)
        result_low = result.astype(jnp.bfloat16)
        inputs = place(inputs, safe, valid, source)
        results = place(results, safe, valid, result_low)
        if tick < MICRO:
            arriving = shifted(result_low, "section", 1)
    again = (
        lax.all_gather(gains, "dp", axis=2, tiled=True),
        lax.all_gather(biases, "dp", axis=2, tiled=True),
        lax.all_gather(w_qkv, "dp", axis=2, tiled=True),
        lax.all_gather(w_proj, "dp", axis=2, tiled=True),
        lax.all_gather(w_fc, "dp", axis=2, tiled=True),
        lax.all_gather(w_out, "dp", axis=2, tiled=True),
    )
    weights_back = tuple((member[0] for member in again))
    totals = tuple((jnp.zeros(member.shape, jnp.float32) for member in weights_back))
    input_parts = jnp.zeros((MICRO, MB_TOK, width), jnp.bfloat16)
    coming = jnp.zeros((MB_TOK, width), jnp.bfloat16)
    for tick in range(MICRO + 1):
        index = MICRO - 1 - tick + (1 - section)
        valid = (index >= 0) & (index < MICRO)
        safe = jnp.clip(index, 0, MICRO - 1)
        d_result = jnp.where(section == 1, pick(cot_parts, safe), coming).astype(jnp.float32)
        tick_grads, d_inp = backward_block(
            pick(inputs, safe).astype(jnp.float32), pick(seg_parts, safe), weights_back, d_result
        )
        totals = tuple(
            (total + jnp.where(valid, term, 0.0) for total, term in zip(totals, tick_grads))
        )
        d_send = d_inp.astype(jnp.bfloat16)
        input_parts = place(input_parts, safe, valid, d_send)
        if tick < MICRO:
            coming = shifted(d_send, "section", -1)
    summed = (
        lax.psum_scatter(totals[0][None], "dp", scatter_dimension=2, tiled=True),
        lax.psum_scatter(totals[1][None], "dp", scatter_dimension=2, tiled=True),
        lax.psum_scatter(totals[2][None], "dp", scatter_dimension=2, tiled=True),
        lax.psum_scatter(totals[3][None], "dp", scatter_dimension=2, tiled=True),
        lax.psum_scatter(totals[4][None], "dp", scatter_dimension=2, tiled=True),
        lax.psum_scatter(totals[5][None], "dp", scatter_dimension=2, tiled=True),
    )
    activations = results.reshape(1, tok_rows, width)
    input_grads = input_parts.reshape(1, tok_rows, width)
    return (
        activations,
        input_grads,
        summed[0],
        summed[1],
        summed[2],
        summed[3],
        summed[4],
        summed[5],
    )


def solution(mesh):
    placed = (
        P("dp", None),
        P("dp"),
        P("section", None, "dp"),
        P("section", None, "dp"),
        P("section", None, "dp"),
        P("section", None, "dp"),
        P("section", None, "dp"),
        P("section", None, "dp"),
        P("dp", None),
    )
    return jax.shard_map(
        local,
        mesh=mesh,
        in_specs=placed,
        out_specs=(
            P("section", "dp", None),
            P("section", "dp", None),
            P("section", None, "dp"),
            P("section", None, "dp"),
            P("section", None, "dp"),
            P("section", None, "dp"),
            P("section", None, "dp"),
            P("section", None, "dp"),
        ),
        check_vma=False,
    )
```

profile of v0, /device:TPU:0, one launch (start us, length us, event | category | flops | bytes accessed | tf_op | source)
XLA Modules:
  0.0 3959.4 jit_solution(4963835163743567331)
XLA Ops:
  10.8 99.2 %all_gather.25 = bf16[1,10,1024]{1,0,2:T(2,128)(2,1)S(1)} all-gather(bf16[1,10,16]{1,0,2:T(2,128)(2,1)S(1)} %copy.216), channel_id=1, replica_groups=mesh['section'=2,'dp'=64] {'dp'}, dimensions={2}, use_global_device_ids=true | all-gather | bytes 20800 | tf_op jit(solution)/shard_map/all_gather | solution.py:140
  113.2 90.3 %all_gather.24 = bf16[1,2,1024]{1,0,2:T(2,128)(2,1)S(1)} all-gather(bf16[1,2,16]{1,0,2:T(2,128)(2,1)S(1)} %copy.215), channel_id=1, replica_groups=mesh['section'=2,'dp'=64] {'dp'}, dimensions={2}, use_global_device_ids=true | all-gather | bytes 4160 | tf_op jit(solution)/shard_map/all_gather | solution.py:139
  213.8 18.0 slice_reduce_fusion.1
  242.6 83.6 %all-gather.11.cloned.1.call-done = bf16[1,4096,1024]{1,2,0:T(8,128)(2,1)} async-done(((bf16[1,4096,16]{1,2,0:T(8,128)(2,1)}), bf16[1,4096,1024]{1,2,0:T(8,128)(2,1)}) %all-gather.11.cloned.1.call-update) | async-done | bytes 8388624 | tf_op jit(solution)/shard_map/all_gather | solution.py:144
  326.2 11.1 bitcast_dynamic-update-slice_fusion.6
  359.2 11.7 bitcast_dynamic-update-slice_fusion.5
  393.4 6.2 fusion.63
  399.7 6.7 convert_reduce_fusion.2
  475.8 6.5 convert_reduce_fusion.1
  535.0 6.2 fusion.69
  544.1 6.5 convert_reduce_fusion
  598.4 6.5 copy.315
  604.9 6.5 bitcast_reduce_fusion
  616.6 11.0 copy.282
  630.8 6.5 fusion.411
  637.3 9.1 add_bitcast_fusion.2
  646.4 27.1 copy.281
  674.0 9.4 fusion.270
  683.4 8.1 fusion.271
  691.5 11.0 add_bitcast_fusion
  702.5 37.4 copy.284
  740.5 9.2 fusion.544
  749.7 8.2 fusion.545
  757.9 11.2 add_bitcast_fusion.1
  769.1 37.1 copy.283
  820.8 11.1 fusion.198
  832.3 89.0 %reduce-scatter.7.cloned.1.call-done = f32[16,2]{1,0:T(8,128)} async-done(((f32[1024,2]{1,0:T(8,128)}), f32[16,2]{1,0:T(8,128)}) %reduce-scatter.7.cloned.1.call-update) | async-done | bytes 144
  922.6 328.2 %reduce-scatter.9.cloned.1.call-done = f32[16,10]{1,0:T(8,128)} async-done(((f32[1024,10]{1,0:T(8,128)}), f32[16,10]{1,0:T(8,128)}) %reduce-scatter.9.cloned.1.call-update) | async-done | bytes 656
  1252.3 642.8 %all-reduce.11.cloned.1.call-done = f32[1,1024,1024]{1,0,2:T(1,128)} async-done(((f32[1,1024,1024]{1,0,2:T(1,128)}), f32[1,1024,1024]{1,0,2:T(1,128)}) %all-reduce.11.cloned.1.call-update) | async-done | bytes 4194320
  1896.6 675.4 %all-reduce.9.cloned.1.call-done = f32[1,1024,3072]{1,0,2:T(1,128)} async-done(((f32[1,1024,3072]{1,0,2:T(1,128)}), f32[1,1024,3072]{1,0,2:T(1,128)}) %all-reduce.9.cloned.1.call-update) | async-done | bytes 12582928
  2573.6 687.7 %all-reduce.15.cloned.1.call-done = f32[1,4096,1024]{1,0,2:T(1,128)} async-done(((f32[1,4096,1024]{1,0,2:T(1,128)}), f32[1,4096,1024]{1,0,2:T(1,128)}) %all-reduce.15.cloned.1.call-update) | async-done | bytes 16777232
  3263.1 687.5 %all-reduce.13.cloned.1.call-done = f32[1,1024,4096]{1,0,2:T(1,128)} async-done(((f32[1,1024,4096]{1,0,2:T(1,128)}), f32[1,1024,4096]{1,0,2:T(1,128)}) %all-reduce.13.cloned.1.call-update) | async-done | bytes 16777232
  (540 shorter events, 275.2 us)
Async XLA Ops:
  7.2 224.7 %copy-start.14 = (bf16[128,1024]{1,0:T(8,128)(2,1)S(1)}, bf16[128,1024]{1,0:T(8,128)(2,1)}, u32[]{:S(2)}) copy-start(bf16[128,1024]{1,0:T(8,128)(2,1)} %param.9) | copy-start | bytes 786436
  7.2 224.7 %all-gather.5.cloned.1.call-start = ((), (), s32[]{:S(2)}) async-start(), calls=%async_computation.2 | async-start | bytes 6389760 | tf_op jit(solution)/shard_map/all_gather | solution.py:141
  7.9 230.5 %all-gather.7.cloned.1.call-start = ((), (), s32[]{:S(2)}) async-start(), calls=%async_computation.3 | async-start | bytes 2129920 | tf_op jit(solution)/shard_map/all_gather | solution.py:142
  8.7 234.0 %all-gather.9.cloned.1.call-start = ((), (), s32[]{:S(2)}) async-start(), calls=%async_computation.4 | async-start | bytes 8519680 | tf_op jit(solution)/shard_map/all_gather | solution.py:143
  9.4 316.8 %all-gather.11.cloned.1.call-start = ((), (), s32[]{:S(2)}) async-start(), calls=%async_computation.5 | async-start | bytes 8519680 | tf_op jit(solution)/shard_map/all_gather | solution.py:144
  10.0 911.3 %reduce-scatter.7.cloned.1.call-start = ((), (), s32[]{:S(2)}) async-start(), calls=%async_computation.6 | async-start | bytes 532480
  204.3 189.1 %copy-start.58 = (f32[1,8,4,128]{3,1,2,0:T(8,128)}, f32[1,8,4,128]{3,1,2,0:T(8,128)S(1)}, u32[]{:S(2)}) copy-start(f32[1,8,4,128]{3,1,2,0:T(8,128)S(1)} %copy.358) | copy-start | bytes 49156
  206.6 31.8 copy-start.78
  231.8 127.4 %copy-start.73 = (f32[1024]{0:T(1024)}, f32[1024]{0:T(1024)S(1)}, u32[]{:S(2)}) copy-start(f32[1024]{0:T(1024)S(1)} %get-tuple-element.55) | copy-start | bytes 12292
  231.8 152.8 %copy-start.67 = (f32[1024]{0:T(1024)}, f32[1024]{0:T(1024)S(1)}, u32[]{:S(2)}) copy-start(f32[1024]{0:T(1024)S(1)} %get-tuple-element.57) | copy-start | bytes 12292
  231.8 152.8 %copy-start.70 = (f32[1024]{0:T(1024)}, f32[1024]{0:T(1024)S(1)}, u32[]{:S(2)}) copy-start(f32[1024]{0:T(1024)S(1)} %get-tuple-element.58) | copy-start | bytes 12292
  231.8 159.5 %copy-start.65 = (f32[1024]{0:T(1024)}, f32[1024]{0:T(1024)S(1)}, u32[]{:S(2)}) copy-start(f32[1024]{0:T(1024)S(1)} %get-tuple-element.56) | copy-start | bytes 12292
  337.3 5.8 collective-permute-start
  340.2 46.7 %copy-start.76 = (pred[64,64]{0,1:T(8,128)(4,1)}, pred[64,64]{0,1:T(8,128)(4,1)S(1)}, u32[]{:S(2)}) copy-start(pred[64,64]{0,1:T(8,128)(4,1)S(1)} %get-tuple-element.164) | copy-start | bytes 12292
  370.9 7.2 collective-permute-start.1
  378.2 83.2 %copy-start.12 = (bf16[64,1024]{1,0:T(8,128)(2,1)}, bf16[64,1024]{1,0:T(8,128)(2,1)S(1)}, u32[]{:S(2)}) copy-start(bf16[64,1024]{1,0:T(8,128)(2,1)S(1)} %get-tuple-element.95) | copy-start | bytes 393220
  446.5 27.7 collective-permute-start.2
  459.8 24.8 copy-start.91
  460.0 24.6 copy-start.102
  495.0 26.2 slice-start.6
  520.0 22.6 collective-permute-start.3
  526.8 23.8 copy-start.81
  527.1 23.5 copy-start.57
  529.7 23.2 copy-start.104
  529.9 23.0 copy-start.109
  587.9 662.9 %reduce-scatter.9.cloned.1.call-start = ((), (), s32[]{:S(2)}) async-start(), calls=%async_computation.7 | async-start | bytes 532480
  611.4 1283.7 %all-reduce.11.cloned.1.call-start = ((), (), s32[]{:S(2)}) async-start(), calls=%async_computation.9 | async-start | bytes 8388608
  627.6 1944.4 %all-reduce.9.cloned.1.call-start = ((), (), s32[]{:S(2)}) async-start(), calls=%async_computation.8 | async-start | bytes 25165824
  673.5 2587.8 %all-reduce.15.cloned.1.call-start = ((), (), s32[]{:S(2)}) async-start(), calls=%async_computation.11 | async-start | bytes 33554432
  739.9 3210.7 %all-reduce.13.cloned.1.call-start = ((), (), s32[]{:S(2)}) async-start(), calls=%async_computation.10 | async-start | bytes 33554432
  832.0 3120.4 %copy-start.51 = (bf16[2,64,1024]{2,1,0:T(8,128)(2,1)}, bf16[2,64,1024]{2,1,0:T(8,128)(2,1)S(1)}, u32[]{:S(2)}) copy-start(bf16[2,64,1024]{2,1,0:T(8,128)(2,1)S(1)} %fusion.198) | copy-start | bytes 786436
  832.3 3120.0 %copy-start.56 = (bf16[2,64,1024]{2,1,0:T(8,128)(2,1)}, bf16[2,64,1024]{2,1,0:T(8,128)(2,1)S(1)}, u32[]{:S(2)}) copy-start(bf16[2,64,1024]{2,1,0:T(8,128)(2,1)S(1)} %fusion.400) | copy-start | bytes 786436
  (117 other events, 1107.7 us)
Sparse Core Ops, SparseCore 0:
  11.2 78.9 all-gather.4
  93.5 67.2 all-gather.6
  164.0 78.5 all-gather.8
  245.8 80.3 all-gather.10
  588.0 333.2 reduce-scatter.6
  923.6 327.1 reduce-scatter.8
  1253.2 641.8 all-reduce.10
  1897.8 674.1 all-reduce.8
  2574.6 686.6 all-reduce.14
  3263.8 686.7 all-reduce.12
where the time goes:
time: 3970 us; the launch traced here: 3960 us
  waiting for transfers between devices  3200 us (81%)
  matrix products  259 us (7%)
  local copies, waits for them, and re-layouts  241 us (6%)
  blocking collectives  189 us (5%)
    unnamed x16, waiting for transfers between devices  3110 us
    all_gather x1, blocking collectives, local(): lax.all_gather(biases, 'dp', axis=2, tiled=True)  99.2 us
    all_gather x1, blocking collectives, local(): lax.all_gather(gains, 'dp', axis=2, tiled=True)  90.3 us
    all_gather x1, waiting for transfers between devices, local(): lax.all_gather(w_out, 'dp', axis=2, tiled=True)  83.6 us
  transfers between devices with their start and end apart: 14, of which 10 were waited for; matrix products, arithmetic and copies ran while one was open for 8% of the time, Pallas kernels for 0%

commit v1 on v0

v1 whole, which is shorter than its diff:
```python
import jax
import jax.numpy as jnp
from jax import lax
from jax.experimental import pallas as pl
from jax.experimental.pallas import tpu as pltpu
from jax.sharding import PartitionSpec as P

MESH = pl.DeviceIdType.MESH
F32 = jnp.float32
BF16 = jnp.bfloat16
EPS = 1e-05
ROWS = 128
WIDTH = 1024
HEAD = 64
GC = 0.7978845608028654
NT = (((1,), (1,)), ((), ()))

PARTS = {"B": (0, 4), "C": (4, 4), "A1": (8, 2), "A2": (10, 2)}
INNER_IS_Y = {"B": False, "C": True, "A1": True, "A2": False}


def remote(src, dst, ssem, rsem, target):
    return pltpu.make_async_remote_copy(
        src_ref=src, dst_ref=dst, send_sem=ssem, recv_sem=rsem, device_id=target, device_id_type=MESH
    )


class Ring:
    def __init__(self, view, pos, left, right, ssem, rsem):
        self.view, self.pos, self.left, self.right = view, pos, left, right
        self.ssem, self.rsem = ssem, rsem

    def at(self, off):
        return lax.rem(self.pos + off, 4)

    def cp(self, off, half, slot, target):
        ref = self.view(self.at(off), half)
        return remote(ref, ref, self.ssem(slot), self.rsem(slot), target)

    def start(self):
        self.cp(0, None, 0, self.right).start()
        self.cp(0, None, 1, self.left).start()

    def mid(self):
        self.cp(3, None, 0, self.right).wait_recv()
        self.cp(3, 0, 2, self.right).start()
        self.cp(1, None, 1, self.left).wait_recv()
        self.cp(1, 1, 3, self.left).start()

    def end(self):
        self.cp(2, 0, 2, self.right).wait_recv()
        self.cp(2, 1, 3, self.left).wait_recv()

    def sent(self):
        self.cp(0, None, 0, self.right).wait_send()
        self.cp(0, None, 1, self.left).wait_send()
        self.cp(3, 0, 2, self.right).wait_send()
        self.cp(1, 1, 3, self.left).wait_send()


class SumRing:
    def __init__(self, view, pos, left, right, bufs, ssem, rsem, add):
        self.view, self.pos, self.left, self.right = view, pos, left, right
        self.half_l, self.half_r, self.full_l, self.full_r = bufs
        self.ssem, self.rsem, self.add = ssem, rsem, add

    def at(self, off):
        return lax.rem(self.pos + off, 4)

    def cp(self, k):
        off, half, buf, target = (
            (2, 0, self.half_l, self.right),
            (2, 1, self.half_r, self.left),
            (1, None, self.full_l, self.right),
            (3, None, self.full_r, self.left),
        )[k]
        return remote(self.view(self.at(off), half), buf, self.ssem(k), self.rsem(k), target)

    def start(self):
        self.cp(0).start()
        self.cp(1).start()

    def mid(self):
        self.cp(0).wait_recv()
        self.add(self.view(self.at(1), 0), (self.half_l,))
        self.cp(2).start()
        self.cp(1).wait_recv()
        self.add(self.view(self.at(3), 1), (self.half_r,))
        self.cp(3).start()

    def end(self):
        self.cp(2).wait_recv()
        self.cp(3).wait_recv()
        self.add(self.view(self.pos, None), (self.full_l, self.full_r))

    def sent(self):
        for k in range(4):
            self.cp(k).wait_send()


def add_into(view, terms):
    lead = view.shape[:-2]
    count = 1
    for size in lead:
        count *= size

    def body(step, carry):
        index, rest = [], step
        for size in reversed(lead):
            index.append(lax.rem(rest, size))
            rest = lax.div(rest, size)
        index = tuple(reversed(index))
        total = view[index].astype(F32)
        for term in terms:
            total = total + term[index].astype(F32)
        view[index] = total.astype(BF16)
        return carry

    lax.fori_loop(0, count, body, 0)


def kernel(
    tok_ref, seg_ref, gains_ref, bias_ref, qkv_ref, proj_ref, fc_ref, wout_ref, cot_ref,
    act_out, grad_out, ggain_out, gbias_out, gqkv_out, gproj_out, gfc_out, gwout_out,
    w, rb_outer, rb_half, rb_inner, rb_ihalf, rb_x, ra_x, ra_outer, ra_half, ra_inner, ra_ihalf,
    xin, x1, x2, x3, x4, qkv, probs, xh1, xh2, rs1, rs2, dgel, gf, dpre, dbr, datt, dmix, dmid, mask, qbias,
    bf, sgb, sb_y, sb_c, sb_x, sbw, sr, sr_c, sr_x, sr_z, sr_y,
    s_out, s_fc, s_proj, s_qkv, t_out, t_fc, t_proj, t_qkv, hb,
    loc_sem, ag_s, ag_r, agx_s, agx_r, sib_s, sib_r, rs_s, rs_r, rsx_s, rsx_r, ex_s, ex_r, sm_s, sm_r, sec_s, sec_r,
):
    sec = lax.axis_index("section")
    dp = lax.axis_index("dp")
    c = lax.rem(dp, 2)
    y = lax.rem(lax.div(dp, 2), 4)
    z = lax.rem(lax.div(dp, 8), 4)
    x = lax.div(dp, 32)
    ox, oc = 1 - x, 1 - c

    def at(px, pz, py, pc):
        return (sec, ((px * 4 + pz) * 4 + py) * 2 + pc)

    ys = [at(x, z, lax.rem(y + k, 4), c) for k in range(4)]
    zs = [at(x, lax.rem(z + k, 4), y, c) for k in range(4)]
    xp = at(ox, z, y, c)
    sib = at(x, z, y, oc)
    other_section = (1 - sec, dp)

    own = w.at[x, z, y, c]
    local = [
        pltpu.make_async_copy(qkv_ref, own.at[pl.ds(0, 3)], loc_sem.at[0]),
        pltpu.make_async_copy(proj_ref, own.at[pl.ds(3, 1)], loc_sem.at[1]),
        pltpu.make_async_copy(fc_ref, own.at[pl.ds(4, 4)], loc_sem.at[2]),
    ] + [
        pltpu.make_async_copy(wout_ref.at[:, pl.ds(1024 * j, 1024)], own.at[8 + j], loc_sem.at[3 + j]) for j in range(4)
    ]
    for cp in local:
        cp.start()
    barrier = pltpu.get_barrier_semaphore()
    partners = ys[1:] + zs[1:] + [xp, sib, other_section]
    for target in partners:
        pl.semaphore_signal(barrier, 1, device_id=target, device_id_type=MESH)
    pl.semaphore_wait(barrier, len(partners))
    for cp in local:
        cp.wait()

    def line(part, xx, o, half=None, core=None):
        base, size = PARTS[part]
        core = c if core is None else core
        inner = slice(None) if half is None else pl.ds(2 * half, 2)
        if INNER_IS_Y[part]:
            return w.at[xx, o, inner, core, pl.ds(base, size)]
        return w.at[xx, inner, o, core, pl.ds(base, size)]

    def single(part, xx, i, half=None):
        base, size = PARTS[part]
        if half is not None:
            size = size // 2
            base = base + half * size
        if INNER_IS_Y[part]:
            return w.at[xx, z, i, c, pl.ds(base, size)]
        return w.at[xx, i, y, c, pl.ds(base, size)]

    def axes(part):
        yy, zz = (y, ys[3], ys[1]), (z, zs[3], zs[1])
        return (yy, zz) if INNER_IS_Y[part] else (zz, yy)

    names = ("B", "C", "A1", "A2")

    def xside(other):
        return ox if other else x

    def gather_rings(part, other):
        inner, outer = axes(part)
        slot = names.index(part) * 2 + other
        xx = xside(other)
        first = Ring(lambda i, h: single(part, xx, i, h), *inner,
                     lambda k: ag_s.at[slot, 0, k], lambda k: ag_r.at[slot, 0, k])
        second = Ring(lambda o, h: line(part, xx, o, h), *outer,
                      lambda k: ag_s.at[slot, 1, k], lambda k: ag_r.at[slot, 1, k])
        return first, second

    rings = {(part, other): gather_rings(part, other) for part in ("B", "C") for other in (0, 1)}
    rings.update({(part, 0): gather_rings(part, 0) for part in ("A1", "A2")})

    def outer_pos(part):
        return z if INNER_IS_Y[part] else y

    def to_sibling(part, other, off, core=None):
        o = lax.rem(outer_pos(part) + off, 4)
        ref = line(part, xside(other), o, None, core)
        k = names.index(part)
        return remote(ref, ref, sib_s.at[k, other, off], sib_r.at[k, other, off], sib)

    def x_line(part, other, off):
        o = lax.rem(outer_pos(part) + off, 4)
        ref = line(part, xside(other), o)
        k = names.index(part) - 2
        return remote(ref, ref, agx_s.at[2 + k * 4 + off], agx_r.at[2 + k * 4 + off], xp)

    def x_single(part, other):
        k = names.index(part)
        ref = single(part, xside(other), z if not INNER_IS_Y[part] else y)
        return remote(ref, ref, agx_s.at[k], agx_r.at[k], xp)

    ring_a1, ring_a2 = rings["A1", 0], rings["A2", 0]
    x_single("B", 0).start()
    x_single("C", 0).start()
    ring_a1[0].start()
    ring_a2[0].start()
    rings["B", 0][0].start()
    rings["C", 0][0].start()

    sgb[...] = jnp.zeros_like(sgb)
    sgb[0:2, :] = gains_ref[...].astype(F32)
    sgb[2:12, :] = bias_ref[...].astype(F32)
    spread = (
        lax.broadcasted_iota(jnp.int32, (16, 128), 1)
        == lax.broadcasted_iota(jnp.int32, (16, 128), 0) + 16 * (y * 2 + c)
    ).astype(F32)
    sb_y[0] = jnp.dot(sgb[...].astype(BF16), spread.astype(BF16), preferred_element_type=F32)

    def small(slot, src, dst, target):
        return remote(src, dst, sm_s.at[slot], sm_r.at[slot], target)

    small_y = [small(k - 1, sb_y.at[0], sb_y.at[k], ys[k]) for k in (1, 2, 3)]
    for cp in small_y:
        cp.start()

    ring_a1[0].mid()
    ring_a2[0].mid()
    rings["B", 0][0].mid()
    rings["C", 0][0].mid()
    ring_a1[0].end()
    ring_a1[1].start()
    x_line("A1", 0, 0).start()
    ring_a2[0].end()
    ring_a2[1].start()
    x_line("A2", 0, 0).start()
    to_sibling("A1", 0, 0).start()
    to_sibling("A2", 0, 0).start()
    x_single("B", 1).wait_recv()
    rings["B", 1][0].start()
    x_single("C", 1).wait_recv()
    rings["C", 1][0].start()

    for cp in small_y:
        cp.wait_recv()
    sb_c[0] = sb_y[0] + sb_y[1] + sb_y[2] + sb_y[3]
    small_c = small(3, sb_c.at[0], sb_c.at[1], sib)
    small_c.start()

    for part in ("B", "C"):
        rings[part, 0][0].end()
        rings[part, 0][1].start()
        to_sibling(part, 0, 0).start()

    seg_col = jnp.broadcast_to(seg_ref[...].astype(F32), (ROWS, ROWS))
    qi = lax.broadcasted_iota(jnp.int32, (ROWS, ROWS), 0)
    ki = lax.broadcasted_iota(jnp.int32, (ROWS, ROWS), 1)
    allowed = (seg_col == seg_col.T) & (ki <= qi) & (lax.div(qi, 64) == lax.div(ki, 64))
    mask[...] = allowed.astype(F32)

    small_c.wait_recv()
    sb_x[x, z] = sb_c[0] + sb_c[1]
    small_z = [small(3 + k, sb_x.at[x, z], sb_x.at[x, z], zs[k]) for k in (1, 2, 3)]
    for cp in small_z:
        cp.start()

    def a_mid(part, ring):
        ring[1].mid()
        for off in (3, 1):
            x_line(part, 0, off).start()
            to_sibling(part, 0, off).start()

    a_mid("A1", ring_a1)
    a_mid("A2", ring_a2)
    rings["B", 1][0].mid()
    rings["C", 1][0].mid()
    for part in ("B", "C"):
        rings[part, 1][0].end()
        rings[part, 1][1].start()
        to_sibling(part, 1, 0).start()
    for part, ring in (("A1", ring_a1), ("A2", ring_a2)):
        ring[1].end()
        x_line(part, 0, 2).start()
        to_sibling(part, 0, 2).start()

    for k in (1, 2, 3):
        from_z = lax.rem(z + 4 - k, 4)
        small(3 + k, sb_x.at[x, from_z], sb_x.at[x, from_z], zs[k]).wait_recv()
    small_x = small(7, sb_x.at[x], sb_x.at[x], xp)
    small_x.start()

    def bulk_mid(part, other):
        rings[part, other][1].mid()
        for off in (3, 1):
            to_sibling(part, other, off).start()

    def bulk_end(part, other):
        rings[part, other][1].end()
        to_sibling(part, other, 2).start()

    bulk_mid("B", 0)
    bulk_mid("C", 0)
    small(7, sb_x.at[ox], sb_x.at[ox], xp).wait_recv()
    for g in range(8):
        bf[:, g * 128 : (g + 1) * 128] = sb_x[g // 4, g % 4]
    qbias[:, 0:WIDTH] = bf[3:4, :]
    qbias[:, WIDTH : 2 * WIDTH] = jnp.zeros((1, WIDTH), F32)
    qbias[:, 2 * WIDTH :] = bf[4:5, :]

    def row(k):
        return bf[k : k + 1, :]

    bulk_end("B", 0)
    bulk_mid("B", 1)
    bulk_end("C", 0)
    bulk_mid("C", 1)

    def a_pass_on(off):
        for part in ("A1", "A2"):
            x_line(part, 1, off).wait_recv()
            to_sibling(part, 1, off).start()

    a_pass_on(0)
    bulk_end("B", 1)
    bulk_end("C", 1)

    def from_sibling(part):
        for other in (0, 1):
            for off in (0, 3, 1, 2):
                to_sibling(part, other, off, oc).wait_recv()

    handed_on = remote(act_out, hb, sec_s, sec_r, other_section)
    handed_back = remote(grad_out, hb, sec_s, sec_r, other_section)

    @pl.when(sec == 0)
    def _():
        xin[...] = tok_ref[...].astype(F32)

    @pl.when(sec == 1)
    def _():
        handed_on.wait_recv()
        xin[...] = hb[...].astype(F32)

    def norm(values, gain, shift):
        centre = values - jnp.mean(values, axis=-1, keepdims=True)
        rs = lax.rsqrt(jnp.mean(centre * centre, axis=-1, keepdims=True) + EPS)
        hat = centre * rs
        return hat, rs, (hat * gain + shift).astype(BF16)

    def exchange(slot, src, dst):
        return remote(src, dst, ex_s.at[slot], ex_r.at[slot], sib)

    xh1[...], rs1[...], x1[0] = norm(xin[...], row(0), row(2))
    ex_first = exchange(0, x1.at[0], x1.at[1])
    ex_first.start()
    from_sibling("B")

    def qkv_weights(k):
        return w[k, :, :, :, 0:3].reshape(1536, WIDTH)

    for k in range(2):
        cols = slice(1536 * k, 1536 * (k + 1))
        mixed = lax.dot_general(x1[0], qkv_weights(k), NT, preferred_element_type=F32)
        qkv[:, cols] = (mixed + qbias[:, cols]).astype(BF16)

    low_lanes = lax.broadcasted_iota(jnp.int32, (ROWS, 128), 1) < HEAD
    zero = jnp.zeros((ROWS, 128), BF16)

    def pair(base, hp):
        return pl.ds(pl.multiple_of(base + hp * 128, 128), 128)

    def attend(hp, carry):
        q, k, v = (qkv[:, pair(base, hp)] for base in (0, WIDTH, 2 * WIDTH))
        parts = []
        for e in range(2):
            qm = jnp.where(low_lanes if e == 0 else ~low_lanes, q, zero)
            scores = lax.dot_general(qm, k, NT, preferred_element_type=F32) * 0.125
            scores = jnp.where(mask[...] > 0.5, scores, -1e30)
            top = jnp.max(scores, axis=-1, keepdims=True)
            ex = jnp.exp(scores - top)
            p = ex / jnp.sum(ex, axis=-1, keepdims=True)
            probs[2 * hp + e] = p
            parts.append(jnp.dot(p.astype(BF16), v, preferred_element_type=F32))
        x2[0, :, pair(0, hp)] = jnp.where(low_lanes, parts[0], parts[1]).astype(BF16)
        return carry

    lax.fori_loop(0, 8, attend, 0)
    ex_att = exchange(1, x2.at[0], x2.at[1])
    ex_att.start()

    a_pass_on(3)
    proj_w = w[:, :, :, :, 3].reshape(WIDTH, WIDTH)
    xin[...] = xin[...] + (lax.dot_general(x2[0], proj_w, NT, preferred_element_type=F32) + row(5))
    xh2[...], rs2[...], x3[0] = norm(xin[...], row(1), row(6))
    ex_second = exchange(2, x3.at[0], x3.at[1])
    ex_second.start()
    from_sibling("C")
    a_pass_on(1)

    def fc_weights(j):
        return w[lax.div(j, 2), pl.ds(2 * lax.rem(j, 2), 2), :, :, 4:8].reshape(WIDTH, WIDTH)

    def up(j, carry):
        pre = lax.dot_general(x3[0], fc_weights(j), NT, preferred_element_type=F32) + bf[pl.ds(7 + j, 1), :]
        square = pre * pre
        t = jnp.tanh(GC * (pre + 0.044715 * (square * pre)))
        half = 0.5 * (1.0 + t)
        x4[0, j] = (pre * half).astype(BF16)
        dgel[j] = half + (0.5 * GC) * pre * (1.0 - t * t) * (1.0 + 0.134145 * square)
        return carry

    lax.fori_loop(0, 4, up, 0)
    ex_act = exchange(3, x4.at[0], x4.at[1])
    ex_act.start()
    a_pass_on(2)
    from_sibling("A1")
    from_sibling("A2")

    def wout_weights(j):
        return w[:, :, :, :, 8 + j].reshape(WIDTH, WIDTH)

    xin[...] = xin[...] + row(11)

    def down(j, carry):
        xin[...] += lax.dot_general(x4[0, j], wout_weights(j), NT, preferred_element_type=F32)
        return carry

    lax.fori_loop(0, 4, down, 0)
    act_out[...] = xin[...].astype(BF16)

    @pl.when(sec == 0)
    def _():
        handed_on.start()

    for key in rings:
        rings[key][0].sent()
        rings[key][1].sent()
    for part in ("B", "C"):
        x_single(part, 0).wait_send()
    for part in names:
        for other in (0, 1):
            for off in range(4):
                to_sibling(part, other, off).wait_send()
                if part in ("A1", "A2") and other == 0:
                    x_line(part, 0, off).wait_send()
    for cp in small_y + [small_c] + small_z + [small_x]:
        cp.wait_send()

    sbw[...] = jnp.zeros_like(sbw)

    @pl.when(sec == 0)
    def _():
        handed_back.wait_recv()
        gf[...] = hb[...]

    @pl.when(sec == 1)
    def _():
        gf[...] = cot_ref[...]

    def column_sum(values):
        return jnp.sum(values.astype(F32), axis=0, keepdims=True)

    sbw[11:12, :] = column_sum(gf[...])
    s_out[...] = gf[...].T.reshape(2, 4, 4, 2, 1, 16, ROWS)

    def swap(slot, src, dst):
        return exchange(slot, src.at[:, :, :, oc], dst)

    ex_gf = swap(4, s_out, t_out)
    ex_gf.start()

    def back_act(j, carry):
        d_act = jnp.dot(gf[...], wout_weights(j), preferred_element_type=F32)
        d_pre = (dgel[j] * d_act).astype(BF16)
        dpre[j] = d_pre
        sbw[pl.ds(7 + j, 1), :] = column_sum(d_pre)
        s_fc[lax.div(j, 2), pl.ds(2 * lax.rem(j, 2), 2)] = d_pre.T.reshape(2, 4, 2, 4, 16, ROWS)
        return carry

    lax.fori_loop(0, 4, back_act, 0)
    ex_dpre = swap(5, s_fc, t_fc)
    ex_dpre.start()

    def lhs(mine, theirs, rows):
        return jnp.concatenate([mine.reshape(rows, ROWS), theirs.reshape(rows, ROWS)], axis=1)

    def sum_rings(part, other):
        inner, outer = axes(part)
        slot = names.index(part) * 2 + other
        xx = xside(other)
        if part in ("B", "C"):
            k = names.index(part) * 2 + other
            ibufs = (rb_ihalf.at[k, 0], rb_ihalf.at[k, 1], rb_inner.at[k, 0], rb_inner.at[k, 1])
            obufs = (rb_half.at[k, 0], rb_half.at[k, 1], rb_outer.at[k, 0], rb_outer.at[k, 1])
        else:
            k = names.index(part) - 2
            ibufs = (ra_ihalf.at[k, 0], ra_ihalf.at[k, 1], ra_inner.at[k, 0], ra_inner.at[k, 1])
            obufs = (ra_half.at[k, 0], ra_half.at[k, 1], ra_outer.at[k, 0], ra_outer.at[k, 1])
        first = SumRing(lambda o, h: line(part, xx, o, h), *outer, obufs,
                        lambda k: rs_s.at[slot, 0, k], lambda k: rs_r.at[slot, 0, k], add_into)
        second = SumRing(lambda i, h: single(part, xx, i, h), *inner, ibufs,
                         lambda k: rs_s.at[slot, 1, k], lambda k: rs_r.at[slot, 1, k], add_into)
        return first, second

    sums = {(part, other): sum_rings(part, other) for part in ("B", "C") for other in (0, 1)}
    sums.update({(part, 0): sum_rings(part, 0) for part in ("A1", "A2")})

    def x_sum(part, off):
        k = names.index(part) - 2
        o = lax.rem(outer_pos(part) + off, 4)
        return remote(line(part, ox, o), ra_x.at[k, off], rsx_s.at[2 + k * 4 + off], rsx_r.at[2 + k * 4 + off], xp)

    def x_last(part):
        k = names.index(part)
        return remote(single(part, ox, y if INNER_IS_Y[part] else z), rb_x.at[k], rsx_s.at[k], rsx_r.at[k], xp)

    def grads_out():
        ex_gf.wait_recv()
        ex_act.wait_recv()
        for other in (1, 0):
            xx = xside(other)
            left = lhs(s_out[xx, :, :, c], t_out[xx], 256)

            def body(j, carry):
                right = x4[:, j].reshape(2 * ROWS, WIDTH)
                w[xx, :, :, c, 8 + j] = (
                    jnp.dot(left, right, preferred_element_type=F32).astype(BF16).reshape(4, 4, 16, WIDTH)
                )
                return carry

            lax.fori_loop(0, 4, body, 0)
            if other:
                for off in (2, 1, 3, 0):
                    for part in ("A1", "A2"):
                        x_sum(part, off).start()

    def grads_fc():
        ex_dpre.wait_recv()
        ex_second.wait_recv()
        right = x3[...].reshape(2 * ROWS, WIDTH)
        for other in (1, 0):
            xx = xside(other)

            def body(k, carry):
                zz = pl.ds(2 * k, 2)
                left = lhs(s_fc[xx, zz, :, c], t_fc[xx, zz], 512)
                w[xx, zz, :, c, 4:8] = (
                    jnp.dot(left, right, preferred_element_type=F32).astype(BF16).reshape(2, 4, 4, 16, WIDTH)
                )
                return carry

            lax.fori_loop(0, 2, body, 0)
            sums["C", other][0].start()

    @pl.when(sec == 0)
    def _():
        grads_out()

    def back_second(j, carry):
        dmid[...] += jnp.dot(dpre[j], fc_weights(j), preferred_element_type=F32)
        return carry

    dmid[...] = jnp.zeros_like(dmid)
    lax.fori_loop(0, 4, back_second, 0)

    def norm_back(d_out, hat, rs, gain):
        d_hat = d_out * gain
        mean_one = jnp.mean(d_hat, axis=-1, keepdims=True)
        mean_two = jnp.mean(d_hat * hat, axis=-1, keepdims=True)
        return rs * (d_hat - mean_one - hat * mean_two)

    d_second = dmid[...]
    sbw[1:2, :] = column_sum(d_second * xh2[...])
    sbw[6:7, :] = column_sum(d_second)
    dmid[...] = gf[...].astype(F32) + norm_back(d_second, xh2[...], rs2[...], row(1))
    dbr[...] = dmid[...].astype(BF16)
    sbw[5:6, :] = column_sum(dbr[...])
    s_proj[...] = dbr[...].T.reshape(2, 4, 4, 2, 1, 16, ROWS)
    ex_dbr = swap(6, s_proj, t_proj)
    ex_dbr.start()

    @pl.when(sec == 0)
    def _():
        grads_fc()

    datt[...] = jnp.dot(dbr[...], proj_back(w), preferred_element_type=F32).astype(BF16)

    def attend_back(hp, carry):
        q, k, v = (qkv[:, pair(base, hp)] for base in (0, WIDTH, 2 * WIDTH))
        da = datt[:, pair(0, hp)]
        dq, dk, dv = [], [], []
        for e in range(2):
            lanes = low_lanes if e == 0 else ~low_lanes
            dam = jnp.where(lanes, da, zero)
            qm = jnp.where(lanes, q, zero)
            p = probs[2 * hp + e]
            dv.append(jnp.dot(p.astype(BF16).T, dam, preferred_element_type=F32))
            dp_ = lax.dot_general(dam, v, NT, preferred_element_type=F32)
            ds = (p * (dp_ - jnp.sum(dp_ * p, axis=-1, keepdims=True))).astype(BF16)
            dq.append(jnp.dot(ds, k, preferred_element_type=F32))
            dk.append(jnp.dot(ds.T, qm, preferred_element_type=F32))
        dmix[:, pair(0, hp)] = (jnp.where(low_lanes, dq[0], dq[1]) * 0.125).astype(BF16)
        dmix[:, pair(WIDTH, hp)] = ((dk[0] + dk[1]) * 0.125).astype(BF16)
        dmix[:, pair(2 * WIDTH, hp)] = (dv[0] + dv[1]).astype(BF16)
        return carry

    lax.fori_loop(0, 8, attend_back, 0)
    for k in range(2):
        s_qkv[k] = dmix[:, 1536 * k : 1536 * (k + 1)].T.reshape(4, 4, 2, 3, 16, ROWS)
    ex_dmix = swap(7, s_qkv, t_qkv)
    ex_dmix.start()
    sbw[3:4, :] = column_sum(dmix[:, 0:WIDTH])
    sbw[4:5, :] = column_sum(dmix[:, 2 * WIDTH :])
    d_first = jnp.dot(dmix[:, 0:1536], qkv_weights(0), preferred_element_type=F32)
    d_first = d_first + jnp.dot(dmix[:, 1536:], qkv_weights(1), preferred_element_type=F32)
    sbw[0:1, :] = column_sum(d_first * xh1[...])
    sbw[2:3, :] = column_sum(d_first)
    grad_out[...] = (dmid[...] + norm_back(d_first, xh1[...], rs1[...], row(0))).astype(BF16)

    @pl.when(sec == 1)
    def _():
        handed_back.start()
        grads_out()
        grads_fc()

    ex_first.wait_recv()
    ex_att.wait_recv()
    ex_dbr.wait_recv()
    ex_dmix.wait_recv()
    first_rows = x1[...].reshape(2 * ROWS, WIDTH)
    att_rows = x2[...].reshape(2 * ROWS, WIDTH)
    for other in (1, 0):
        xx = xside(other)
        left = lhs(s_proj[xx, :, :, c], t_proj[xx], 256)
        w[xx, :, :, c, 3] = jnp.dot(left, att_rows, preferred_element_type=F32).astype(BF16).reshape(4, 4, 16, WIDTH)

        def body(k, carry):
            zz = pl.ds(2 * k, 2)
            left = lhs(s_qkv[xx, zz, :, c], t_qkv[xx, zz], 384)
            w[xx, zz, :, c, 0:3] = (
                jnp.dot(left, first_rows, preferred_element_type=F32).astype(BF16).reshape(2, 4, 3, 16, WIDTH)
            )
            return carry

        lax.fori_loop(0, 2, body, 0)
        sums["B", other][0].start()

    for g in range(8):
        sr[g // 4, g % 4] = sbw[:, g * 128 : (g + 1) * 128]
    sm_core = small(8, sr, sr_c, sib)
    sm_core.start()

    def a_arrive(off):
        for part in ("A1", "A2"):
            x_sum(part, off).wait_recv()
            k = names.index(part) - 2
            add_into(line(part, x, lax.rem(outer_pos(part) + off, 4)), (ra_x.at[k, off],))

    sums["C", 1][0].mid()
    sums["C", 0][0].mid()
    a_arrive(2)
    sums["A1", 0][0].start()
    sums["A2", 0][0].start()
    sm_core.wait_recv()
    sm_core.wait_send()
    sr[...] = sr[...] + sr_c[...]
    sm_xs = small(9, sr.at[ox], sr_x, xp)
    sm_xs.start()
    sums["B", 1][0].mid()
    sums["B", 0][0].mid()
    a_arrive(1)
    a_arrive(3)
    sums["A1", 0][0].mid()
    sums["A2", 0][0].mid()
    sums["C", 1][0].end()
    sums["C", 1][1].start()
    sums["C", 0][0].end()
    sums["C", 0][1].start()
    sm_xs.wait_recv()
    sr[x] = sr[x] + sr_x[...]
    sm_zs = [small(9 + k, sr.at[x, lax.rem(z + k, 4)], sr_z.at[k - 1], zs[k]) for k in (1, 2, 3)]
    for cp in sm_zs:
        cp.start()
    sums["C", 1][1].mid()
    sums["C", 0][1].mid()
    sums["C", 1][1].end()
    x_last("C").start()
    sums["C", 0][1].end()
    for cp in sm_zs:
        cp.wait_recv()
    sr_y[0] = sr[x, z] + sr_z[0] + sr_z[1] + sr_z[2]
    sm_ys = [small(12 + k, sr_y.at[0], sr_y.at[k], ys[k]) for k in (1, 2, 3)]
    for cp in sm_ys:
        cp.start()
    sums["B", 1][0].end()
    sums["B", 1][1].start()
    sums["B", 0][0].end()
    sums["B", 0][1].start()
    a_arrive(0)
    sums["A1", 0][0].end()
    sums["A1", 0][1].start()
    sums["A2", 0][0].end()
    sums["A2", 0][1].start()
    sums["B", 1][1].mid()
    sums["B", 0][1].mid()
    sums["A1", 0][1].mid()
    sums["A2", 0][1].mid()
    sums["B", 1][1].end()
    x_last("B").start()
    sums["B", 0][1].end()
    for cp in sm_ys:
        cp.wait_recv()
    total = sr_y[0] + sr_y[1] + sr_y[2] + sr_y[3]
    picked = lax.dot_general(total, spread, NT, preferred_element_type=F32, precision=lax.Precision.HIGHEST)
    ggain_out[...] = picked[0:2, :]
    gbias_out[...] = picked[2:12, :]
    sums["A1", 0][1].end()
    sums["A2", 0][1].end()
    mine = w.at[x, z, y, c]
    for j in range(4):
        gwout_out[:, 1024 * j : 1024 * (j + 1)] = mine[8 + j].astype(F32)
    x_last("C").wait_recv()
    gfc_out[...] = mine[4:8].astype(F32) + rb_x[1].astype(F32)
    x_last("B").wait_recv()
    gqkv_out[...] = mine[0:3].astype(F32) + rb_x[0, 0:3].astype(F32)
    gproj_out[...] = mine[3:4].astype(F32) + rb_x[0, 3:4].astype(F32)

    for key in sums:
        sums[key][0].sent()
        sums[key][1].sent()
    for part in ("A1", "A2"):
        for off in range(4):
            x_sum(part, off).wait_send()
    for part in ("B", "C"):
        x_last(part).wait_send()
    for cp in [ex_first, ex_att, ex_second, ex_act, ex_gf, ex_dpre, ex_dbr, ex_dmix, sm_xs] + sm_zs + sm_ys:
        cp.wait_send()

    @pl.when(sec == 0)
    def _():
        handed_on.wait_send()

    @pl.when(sec == 1)
    def _():
        handed_back.wait_send()


def proj_back(w):
    return w[:, :, :, :, 3].reshape(WIDTH, WIDTH)


def local(tokens, segment_ids, gains, biases, w_qkv, w_proj, w_fc, w_out, cotangent):
    vmem = pl.BlockSpec(memory_space=pltpu.VMEM)
    hbm = pl.BlockSpec(memory_space=pl.ANY)

    def shape(*dims, dtype=F32):
        return jax.ShapeDtypeStruct(dims, dtype)

    def v(*dims, dtype=BF16):
        return pltpu.VMEM(dims, dtype)

    def dma(*dims):
        return pltpu.SemaphoreType.DMA(dims)

    scratch = [
        v(2, 4, 4, 2, 12, 16, WIDTH),
        v(4, 2, 4, 4, 16, WIDTH), v(4, 2, 2, 4, 16, WIDTH), v(4, 2, 4, 16, WIDTH), v(4, 2, 2, 16, WIDTH),
        v(2, 4, 16, WIDTH),
        v(2, 4, 4, 2, 16, WIDTH), v(2, 2, 4, 2, 16, WIDTH), v(2, 2, 2, 2, 16, WIDTH), v(2, 2, 2, 16, WIDTH),
        v(2, 2, 1, 16, WIDTH),
        v(ROWS, WIDTH, dtype=F32), v(2, ROWS, WIDTH), v(2, ROWS, WIDTH), v(2, ROWS, WIDTH), v(2, 4, ROWS, WIDTH),
        v(ROWS, 3 * WIDTH), v(16, ROWS, ROWS, dtype=F32), v(ROWS, WIDTH, dtype=F32), v(ROWS, WIDTH, dtype=F32),
        v(ROWS, 1, dtype=F32), v(ROWS, 1, dtype=F32), v(4, ROWS, WIDTH, dtype=F32), v(ROWS, WIDTH),
        v(4, ROWS, WIDTH), v(ROWS, WIDTH), v(ROWS, WIDTH), v(ROWS, 3 * WIDTH), v(ROWS, WIDTH, dtype=F32),
        v(ROWS, ROWS, dtype=F32), v(1, 3 * WIDTH, dtype=F32),
        v(16, WIDTH, dtype=F32), v(16, 16, dtype=F32), v(4, 16, 128, dtype=F32), v(2, 16, 128, dtype=F32),
        v(2, 4, 16, 128, dtype=F32), v(16, WIDTH, dtype=F32), v(2, 4, 16, 128, dtype=F32),
        v(2, 4, 16, 128, dtype=F32), v(4, 16, 128, dtype=F32), v(3, 16, 128, dtype=F32), v(4, 16, 128, dtype=F32),
        v(2, 4, 4, 2, 1, 16, ROWS), v(2, 4, 4, 2, 4, 16, ROWS), v(2, 4, 4, 2, 1, 16, ROWS), v(2, 4, 4, 2, 3, 16, ROWS),
        v(2, 4, 4, 1, 16, ROWS), v(2, 4, 4, 4, 16, ROWS), v(2, 4, 4, 1, 16, ROWS), v(2, 4, 4, 3, 16, ROWS),
        v(ROWS, WIDTH),
        dma(7), dma(8, 2, 4), dma(8, 2, 4), dma(10), dma(10), dma(4, 2, 4), dma(4, 2, 4),
        dma(8, 2, 4), dma(8, 2, 4), dma(10), dma(10), dma(8), dma(8), dma(16), dma(16),
        pltpu.SemaphoreType.DMA, pltpu.SemaphoreType.DMA,
    ]
    out = pl.pallas_call(
        kernel,
        out_shape=(
            shape(ROWS, WIDTH, dtype=BF16), shape(ROWS, WIDTH, dtype=BF16), shape(2, 16), shape(10, 16),
            shape(3, 16, WIDTH), shape(1, 16, WIDTH), shape(4, 16, WIDTH), shape(16, 4 * WIDTH),
        ),
        in_specs=[vmem, vmem, vmem, vmem, hbm, hbm, hbm, hbm, vmem],
        out_specs=(vmem,) * 8,
        scratch_shapes=scratch,
        compiler_params=pltpu.CompilerParams(
            collective_id=0, has_side_effects=True, vmem_limit_bytes=63 * 2**20
        ),
        name="relay",
    )(
        tokens,
        segment_ids.reshape(ROWS, 1),
        gains[0],
        biases[0],
        w_qkv[0].T.reshape(3, 16, WIDTH),
        w_proj[0].T.reshape(1, 16, WIDTH),
        w_fc[0].T.reshape(4, 16, WIDTH),
        w_out[0].T,
        cotangent,
    )
    activations, input_grads, g_gains, g_biases, g_qkv, g_proj, g_fc, g_out = out
    return (
        activations[None],
        input_grads[None],
        g_gains[None],
        g_biases[None],
        g_qkv.reshape(48, WIDTH).T[None],
        g_proj.reshape(16, WIDTH).T[None],
        g_fc.reshape(64, WIDTH).T[None],
        g_out.T[None],
    )


def solution(mesh):
    weight = P("section", None, "dp")
    rows = P("section", "dp", None)
    return jax.shard_map(
        local,
        mesh=mesh,
        in_specs=(P("dp", None), P("dp")) + (weight,) * 6 + (P("dp", None),),
        out_specs=(rows, rows) + (weight,) * 6,
        check_vma=False,
    )
```

time: 3970 us -> 238 us (0.06)
  waiting for transfers between devices: 3200 us -> 0 us
  matrix products: 259 us -> 0 us
  local copies, waits for them, and re-layouts: 241 us -> 8.9 us
  Pallas kernels: 0 us -> 228 us
  blocking collectives: 189 us -> 0 us
    unnamed x16 -> x0, waiting for transfers between devices: 3110 us -> none
    dot_general x66 -> x0, matrix products: 259 us -> none  [the longest x3 33.9 us: forward_block(): jnp.dot(act, w_out, preferred_element_type=jnp.float32) + biases[9]]
    pallas_call x0 -> x1, Pallas kernels: none -> 228 us  [local(): pl.pallas_call(kernel, out_shape=(shape(ROWS, WIDTH, dtype=BF16), shape(R...]
    all_gather x2 -> x0, blocking collectives: 189 us -> none  [the longest x1 99.2 us: local(): lax.all_gather(biases, 'dp', axis=2, tiled=True)]
    broadcast_in_dim x4 -> x0, local copies, waits for them, and re-layouts: 113 us -> none  [the longest x1 37.4 us: local(): totals[5][None]]
    all_gather x4 -> x0, waiting for transfers between devices: 85 us -> none  [the longest x1 83.6 us: local(): lax.all_gather(w_out, 'dp', axis=2, tiled=True)]
    unnamed x306 -> x24, local copies, waits for them, and re-layouts: 48.4 us -> 8.16 us
  transfers between devices with their start and end apart: 14 -> 0, of which waited for: 10 -> 0; matrix products, arithmetic and copies ran while one was open for 8% -> 0% of each run, Pallas kernels for 0% -> 0%
where the time goes in v1:
time: 238 us; the launch traced here: 237 us
  Pallas kernels  228 us (96%)
  local copies, waits for them, and re-layouts  8.9 us (4%)
    pallas_call x1, Pallas kernels, local(): pl.pallas_call(kernel, out_shape=(shape(ROWS, WIDTH, dtype=BF16), shape(R...  228 us
    unnamed x24, local copies, waits for them, and re-layouts  8.16 us

profile of v1, /device:TPU:0, one launch (start us, length us, event | category | flops | bytes accessed | tf_op | source)
XLA Modules:
  0.0 237.3 jit_solution(9574192685514086992)
XLA Ops:
  0.6 0.0 copy-start.7
  0.6 0.6 copy-done.7
  1.3 0.7 copy.17.seg_ref
  2.0 227.7 %relay.1 = (bf16[128,1024]{1,0:T(8,128)(2,1)}, bf16[128,1024]{1,0:T(8,128)(2,1)}, f32[2,16]{1,0:T(2,128)}, f32[10,16]{1,0:T(8,128)}, f32[3,16,1024]{2,1,0:T(8,12...) custom-call(bf16[128,1024]{1,0:T(8,128)(2,1)} %tok_ref.1, s32[128,1]{1,0:T(8,128)} %copy.17.seg_ref, ...), custom_call_target="tpu_custom_call" | custom-call | tf_op jit(solution)/shard_map/relay/pallas_call | solution.py:808
  229.8 0.0 copy-start.5
  229.8 0.7 copy-done.5
  230.5 0.6 copy.18
  231.1 0.0 copy-start.2
  231.1 1.7 copy.26
  232.8 0.0 copy-done.2
  232.8 0.0 copy-start.6
  232.8 0.0 copy-start.3
  232.8 0.7 copy.27
  233.5 0.0 copy-done.6
  233.5 0.6 copy.28
  234.0 0.0 copy-done.3
  234.0 0.0 copy-start.4
  234.0 0.0 copy-start.1
  234.0 0.7 copy.29
  234.7 0.2 copy-done.4
  234.9 0.6 copy.30
  235.5 0.0 copy-done.1
  235.5 0.0 copy-start
  235.5 0.7 copy.31
  236.2 0.3 copy-done
  236.6 0.7 copy.32
Async XLA Ops:
  0.6 0.7 copy-start.7
  229.8 0.7 copy-start.5
  231.1 1.7 copy-start.2
  232.8 0.7 copy-start.6
  232.8 1.3 copy-start.3
  234.0 0.9 copy-start.4
  234.0 1.5 copy-start.1
  235.5 1.0 copy-start

commit v2 on v1

--- a/solution.py
+++ b/solution.py
@@ -389,24 +389,29 @@
     zero = jnp.zeros((ROWS, 128), BF16)
 
     def pair(base, hp):
-        return pl.ds(pl.multiple_of(base + hp * 128, 128), 128)
-
-    def attend(hp, carry):
-        q, k, v = (qkv[:, pair(base, hp)] for base in (0, WIDTH, 2 * WIDTH))
+        return slice(base + hp * 128, base + hp * 128 + 128)
+
+    def lanes_of(e):
+        return low_lanes if e == 0 else ~low_lanes
+
+    raw = []
+    for hp in range(8):
+        q, k = qkv[:, pair(0, hp)], qkv[:, pair(WIDTH, hp)]
+        for e in range(2):
+            raw.append(lax.dot_general(jnp.where(lanes_of(e), q, zero), k, NT, preferred_element_type=F32))
+    seen = mask[...] > 0.5
+    soft = []
+    for scores in raw:
+        scores = jnp.where(seen, scores * 0.125, -1e30)
+        ex = jnp.exp(scores - jnp.max(scores, axis=-1, keepdims=True))
+        soft.append(ex * (1.0 / jnp.sum(ex, axis=-1, keepdims=True)))
+    for hp in range(8):
+        v = qkv[:, pair(2 * WIDTH, hp)]
         parts = []
         for e in range(2):
-            qm = jnp.where(low_lanes if e == 0 else ~low_lanes, q, zero)
-            scores = lax.dot_general(qm, k, NT, preferred_element_type=F32) * 0.125
-            scores = jnp.where(mask[...] > 0.5, scores, -1e30)
-            top = jnp.max(scores, axis=-1, keepdims=True)
-            ex = jnp.exp(scores - top)
-            p = ex / jnp.sum(ex, axis=-1, keepdims=True)
-            probs[2 * hp + e] = p
-            parts.append(jnp.dot(p.astype(BF16), v, preferred_element_type=F32))
+            probs[2 * hp + e] = soft[2 * hp + e]
+            parts.append(jnp.dot(soft[2 * hp + e].astype(BF16), v, preferred_element_type=F32))
         x2[0, :, pair(0, hp)] = jnp.where(low_lanes, parts[0], parts[1]).astype(BF16)
-        return carry
-
-    lax.fori_loop(0, 8, attend, 0)
     ex_att = exchange(1, x2.at[0], x2.at[1])
     ex_att.start()
 
@@ -420,18 +425,15 @@
     a_pass_on(1)
 
     def fc_weights(j):
-        return w[lax.div(j, 2), pl.ds(2 * lax.rem(j, 2), 2), :, :, 4:8].reshape(WIDTH, WIDTH)
-
-    def up(j, carry):
-        pre = lax.dot_general(x3[0], fc_weights(j), NT, preferred_element_type=F32) + bf[pl.ds(7 + j, 1), :]
+        return w[j // 2, 2 * (j % 2) : 2 * (j % 2) + 2, :, :, 4:8].reshape(WIDTH, WIDTH)
+
+    for j in range(4):
+        pre = lax.dot_general(x3[0], fc_weights(j), NT, preferred_element_type=F32) + row(7 + j)
         square = pre * pre
         t = jnp.tanh(GC * (pre + 0.044715 * (square * pre)))
         half = 0.5 * (1.0 + t)
         x4[0, j] = (pre * half).astype(BF16)
         dgel[j] = half + (0.5 * GC) * pre * (1.0 - t * t) * (1.0 + 0.134145 * square)
-        return carry
-
-    lax.fori_loop(0, 4, up, 0)
     ex_act = exchange(3, x4.at[0], x4.at[1])
     ex_act.start()
     a_pass_on(2)
@@ -441,14 +443,10 @@
     def wout_weights(j):
         return w[:, :, :, :, 8 + j].reshape(WIDTH, WIDTH)
 
-    xin[...] = xin[...] + row(11)
-
-    def down(j, carry):
-        xin[...] += lax.dot_general(x4[0, j], wout_weights(j), NT, preferred_element_type=F32)
-        return carry
-
-    lax.fori_loop(0, 4, down, 0)
-    act_out[...] = xin[...].astype(BF16)
+    result = xin[...] + row(11)
+    for j in range(4):
+        result = result + lax.dot_general(x4[0, j], wout_weights(j), NT, preferred_element_type=F32)
+    act_out[...] = result.astype(BF16)
 
     @pl.when(sec == 0)
     def _():
@@ -491,15 +489,12 @@
     ex_gf = swap(4, s_out, t_out)
     ex_gf.start()
 
-    def back_act(j, carry):
+    for j in range(4):
         d_act = jnp.dot(gf[...], wout_weights(j), preferred_element_type=F32)
         d_pre = (dgel[j] * d_act).astype(BF16)
         dpre[j] = d_pre
-        sbw[pl.ds(7 + j, 1), :] = column_sum(d_pre)
-        s_fc[lax.div(j, 2), pl.ds(2 * lax.rem(j, 2), 2)] = d_pre.T.reshape(2, 4, 2, 4, 16, ROWS)
-        return carry
-
-    lax.fori_loop(0, 4, back_act, 0)
+        sbw[7 + j : 8 + j, :] = column_sum(d_pre)
+        s_fc[j // 2, 2 * (j % 2) : 2 * (j % 2) + 2] = d_pre.T.reshape(2, 4, 2, 4, 16, ROWS)
     ex_dpre = swap(5, s_fc, t_fc)
     ex_dpre.start()
 
@@ -543,14 +538,11 @@
             xx = xside(other)
             left = lhs(s_out[xx, :, :, c], t_out[xx], 256)
 
-            def body(j, carry):
+            for j in range(4):
                 right = x4[:, j].reshape(2 * ROWS, WIDTH)
                 w[xx, :, :, c, 8 + j] = (
                     jnp.dot(left, right, preferred_element_type=F32).astype(BF16).reshape(4, 4, 16, WIDTH)
                 )
-                return carry
-
-            lax.fori_loop(0, 4, body, 0)
             if other:
                 for off in (2, 1, 3, 0):
                     for part in ("A1", "A2"):
@@ -563,27 +555,21 @@
         for other in (1, 0):
             xx = xside(other)
 
-            def body(k, carry):
-                zz = pl.ds(2 * k, 2)
+            for k in range(2):
+                zz = slice(2 * k, 2 * k + 2)
                 left = lhs(s_fc[xx, zz, :, c], t_fc[xx, zz], 512)
                 w[xx, zz, :, c, 4:8] = (
                     jnp.dot(left, right, preferred_element_type=F32).astype(BF16).reshape(2, 4, 4, 16, WIDTH)
                 )
-                return carry
-
-            lax.fori_loop(0, 2, body, 0)
             sums["C", other][0].start()
 
     @pl.when(sec == 0)
     def _():
         grads_out()
 
-    def back_second(j, carry):
-        dmid[...] += jnp.dot(dpre[j], fc_weights(j), preferred_element_type=F32)
-        return carry
-
-    dmid[...] = jnp.zeros_like(dmid)
-    lax.fori_loop(0, 4, back_second, 0)
+    d_second = jnp.zeros((ROWS, WIDTH), F32)
+    for j in range(4):
+        d_second = d_second + jnp.dot(dpre[j], fc_weights(j), preferred_element_type=F32)
 
     def norm_back(d_out, hat, rs, gain):
         d_hat = d_out * gain
@@ -591,7 +577,6 @@
         mean_two = jnp.mean(d_hat * hat, axis=-1, keepdims=True)
         return rs * (d_hat - mean_one - hat * mean_two)
 
-    d_second = dmid[...]
     sbw[1:2, :] = column_sum(d_second * xh2[...])
     sbw[6:7, :] = column_sum(d_second)
     dmid[...] = gf[...].astype(F32) + norm_back(d_second, xh2[...], rs2[...], row(1))
@@ -607,26 +592,27 @@
 
     datt[...] = jnp.dot(dbr[...], proj_back(w), preferred_element_type=F32).astype(BF16)
 
-    def attend_back(hp, carry):
-        q, k, v = (qkv[:, pair(base, hp)] for base in (0, WIDTH, 2 * WIDTH))
-        da = datt[:, pair(0, hp)]
+    d_probs, masked_da = [], []
+    for hp in range(8):
+        da, v = datt[:, pair(0, hp)], qkv[:, pair(2 * WIDTH, hp)]
+        for e in range(2):
+            masked_da.append(jnp.where(lanes_of(e), da, zero))
+            d_probs.append(lax.dot_general(masked_da[-1], v, NT, preferred_element_type=F32))
+    d_scores = []
+    for h in range(16):
+        p, dp_ = probs[h], d_probs[h]
+        d_scores.append((p * (dp_ - jnp.sum(dp_ * p, axis=-1, keepdims=True))).astype(BF16))
+    for hp in range(8):
+        q, k = qkv[:, pair(0, hp)], qkv[:, pair(WIDTH, hp)]
         dq, dk, dv = [], [], []
         for e in range(2):
-            lanes = low_lanes if e == 0 else ~low_lanes
-            dam = jnp.where(lanes, da, zero)
-            qm = jnp.where(lanes, q, zero)
-            p = probs[2 * hp + e]
-            dv.append(jnp.dot(p.astype(BF16).T, dam, preferred_element_type=F32))
-            dp_ = lax.dot_general(dam, v, NT, preferred_element_type=F32)
-            ds = (p * (dp_ - jnp.sum(dp_ * p, axis=-1, keepdims=True))).astype(BF16)
-            dq.append(jnp.dot(ds, k, preferred_element_type=F32))
-            dk.append(jnp.dot(ds.T, qm, preferred_element_type=F32))
+            h = 2 * hp + e
+            dv.append(jnp.dot(probs[h].astype(BF16).T, masked_da[h], preferred_element_type=F32))
+            dq.append(jnp.dot(d_scores[h], k, preferred_element_type=F32))
+            dk.append(jnp.dot(d_scores[h].T, jnp.where(lanes_of(e), q, zero), preferred_element_type=F32))
         dmix[:, pair(0, hp)] = (jnp.where(low_lanes, dq[0], dq[1]) * 0.125).astype(BF16)
         dmix[:, pair(WIDTH, hp)] = ((dk[0] + dk[1]) * 0.125).astype(BF16)
         dmix[:, pair(2 * WIDTH, hp)] = (dv[0] + dv[1]).astype(BF16)
-        return carry
-
-    lax.fori_loop(0, 8, attend_back, 0)
     for k in range(2):
         s_qkv[k] = dmix[:, 1536 * k : 1536 * (k + 1)].T.reshape(4, 4, 2, 3, 16, ROWS)
     ex_dmix = swap(7, s_qkv, t_qkv)
@@ -656,15 +642,12 @@
         left = lhs(s_proj[xx, :, :, c], t_proj[xx], 256)
         w[xx, :, :, c, 3] = jnp.dot(left, att_rows, preferred_element_type=F32).astype(BF16).reshape(4, 4, 16, WIDTH)
 
-        def body(k, carry):
-            zz = pl.ds(2 * k, 2)
+        for k in range(2):
+            zz = slice(2 * k, 2 * k + 2)
             left = lhs(s_qkv[xx, zz, :, c], t_qkv[xx, zz], 384)
             w[xx, zz, :, c, 0:3] = (
                 jnp.dot(left, first_rows, preferred_element_type=F32).astype(BF16).reshape(2, 4, 3, 16, WIDTH)
             )
-            return carry
-
-        lax.fori_loop(0, 2, body, 0)
         sums["B", other][0].start()
 
     for g in range(8):

time: 238 us -> 211 us (0.89)
  Pallas kernels: 228 us -> 201 us
    pallas_call x1, Pallas kernels: 228 us -> 201 us  [local(): pl.pallas_call(kernel, out_shape=(shape(ROWS, WIDTH, dtype=BF16), shape(R...]
where the time goes in v2:
time: 211 us
  Pallas kernels  201 us (95%)
  local copies, waits for them, and re-layouts  8.9 us (4%)
    pallas_call x1, Pallas kernels, local(): pl.pallas_call(kernel, out_shape=(shape(ROWS, WIDTH, dtype=BF16), shape(R...  201 us
    unnamed x24, local copies, waits for them, and re-layouts  8.16 us

profile of v2, /device:TPU:0, one launch (start us, length us, event | category | flops | bytes accessed | tf_op | source)
XLA Modules:
  0.0 210.8 jit_solution(8539567292715540532)
XLA Ops:
  0.6 0.0 copy-start.7
  0.6 0.6 copy-done.7
  1.3 0.7 copy.17.seg_ref
  2.0 201.2 %relay.1 = (bf16[128,1024]{1,0:T(8,128)(2,1)}, bf16[128,1024]{1,0:T(8,128)(2,1)}, f32[2,16]{1,0:T(2,128)}, f32[10,16]{1,0:T(8,128)}, f32[3,16,1024]{2,1,0:T(8,12...) custom-call(bf16[128,1024]{1,0:T(8,128)(2,1)} %tok_ref.1, s32[128,1]{1,0:T(8,128)} %copy.17.seg_ref, ...), custom_call_target="tpu_custom_call" | custom-call | tf_op jit(solution)/shard_map/relay/pallas_call | solution.py:791
  203.3 0.0 copy-start.5
  203.3 0.7 copy-done.5
  204.0 0.6 copy.18
  204.5 0.0 copy-start.2
  204.6 1.7 copy.26
  206.3 0.0 copy-done.2
  206.3 0.0 copy-start.6
  206.3 0.0 copy-start.3
  206.3 0.7 copy.27
  207.0 0.0 copy-done.6
  207.0 0.6 copy.28
  207.5 0.0 copy-done.3
  207.5 0.0 copy-start.4
  207.5 0.0 copy-start.1
  207.5 0.7 copy.29
  208.2 0.2 copy-done.4
  208.4 0.6 copy.30
  209.0 0.0 copy-done.1
  209.0 0.0 copy-start
  209.0 0.7 copy.31
  209.7 0.3 copy-done
  210.1 0.7 copy.32
Async XLA Ops:
  0.6 0.7 copy-start.7
  203.3 0.7 copy-start.5
  204.5 1.7 copy-start.2
  206.3 0.7 copy-start.6
  206.3 1.3 copy-start.3
  207.5 0.9 copy-start.4
  207.5 1.5 copy-start.1
  209.0 1.0 copy-start

commit v3 on v0

v3 whole, which is shorter than its diff:
```python
import jax
import jax.numpy as jnp
from jax import lax
from jax.experimental import pallas as pl
from jax.experimental.pallas import tpu as pltpu
from jax.sharding import PartitionSpec as P

MESH = pl.DeviceIdType.MESH
F32 = jnp.float32
BF16 = jnp.bfloat16
EPS = 1e-05
ROWS = 128
WIDTH = 1024
HEAD = 64
GC = 0.7978845608028654
NT = (((1,), (1,)), ((), ()))

PARTS = ("Be", "Ce", "A1", "A2", "Bl", "Cl")
FIRST = {"Be": 0, "Ce": 2, "A1": 4, "A2": 6, "Bl": 8, "Cl": 10}
INNER_IS_Y = {"Be": False, "Ce": True, "A1": True, "A2": False, "Bl": False, "Cl": True}
X_FIRST = {"Be": True, "Ce": True, "A1": False, "A2": False, "Bl": True, "Cl": True}
GROUPS = ((0, (0,)), (1, (0,)), (0, (1, 3)), (0, (2,)), (1, (1, 3)), (1, (2,)))
STAGES = ((0,), (1, 3), (2,))
SUM_AT = {"Be": (0, 4), "Ce": (0, 6), "A1": (0, 8), "A2": (0, 10), "Bl": (1, 8), "Cl": (1, 10)}

GATHER_ONE = [
    "Be.x.s", "A2.in0.start", "Ce.x.s", "A1.in0.start", "A1.g0.start", "Bl.in0.start", "Ce.in0.start", "Cl.in0.start",
    "A1.X.0.0", "A2.in0.mid", "Be.x.r", "A1.in0.mid", "A2.g0.start", "Ce.g0.start", "small.1", "Bl.x.s", "Ce.x.r",
    "A2.X.2.0", "Be.g0.start", "Cl.x.s", "A2.X.0.0", "A2.g2.start", "Ce.in0.mid", "A1.X.2.0", "Be.in0.start",
    "A1.in0.end", "A1.g0.mid", "A1.g3.start", "Bl.in0.mid", "Cl.g0.start", "Be.in0.mid", "A1.X.3.0", "Be.g2.start",
    "Cl.x.r", "Cl.in0.mid", "Cl.g2.start", "A2.in0.end", "A2.X.3.0", "Be.in1.start", "A2.g3.start", "Ce.in1.start",
    "Cl.in1.start", "A1.X.0.1", "Bl.in0.end", "A2.g2.mid", "Cl.g0.mid", "A1.sib.0.0", "A1.g3.mid", "Ce.g1.start",
    "Bl.x.r", "Bl.in1.start", "A2.g0.mid", "Be.g2.mid", "Cl.in0.end", "Cl.sib.0.0", "Be.in1.mid", "A2.X.2.1",
    "Ce.in0.end", "Be.in0.end", "Be.g3.start", "small.2", "A1.g2.start", "A2.g3.mid", "A2.X.3.1", "Ce.g2.start",
    "Be.g0.mid", "A2.X.0.1", "Be.g1.start", "A2.g2.end", "A2.g0.end", "Ce.sib.0.0", "Cl.g3.start", "A2.sib.0.1",
    "Ce.in1.mid", "Be.g4.start", "A2.g3.end", "Cl.g2.mid", "Bl.g0.start", "A2.sib.0.2", "Be.g3.mid", "Bl.in1.mid",
    "A2.sib.0.0", "Be.in1.end", "Bl.sib.0.0", "A2.XR.0", "Ce.g2.mid", "Cl.in1.mid", "A1.X.3.1", "Be.sib.0.1",
    "Be.sib.0.0", "A2.X.2.2", "small.3", "Ce.g3.start", "A1.g2.mid", "Ce.in1.end", "Ce.g0.mid", "A2.sib.1.0",
    "Ce.g5.start", "Cl.g3.mid", "A1.sib.0.1", "Cl.sib.0.1", "A1.X.2.1", "A2.X.3.2", "Be.g4.mid", "A2.XR.1",
    "A1.g3.end", "Be.g5.start", "Ce.g1.mid", "Bl.in1.end", "Bl.g5.start", "Ce.g3.mid", "Cl.g2.end", "Bl.g1.start",
    "A1.XR.0", "Ce.sib.1.0", "Cl.g0.end", "Ce.g4.start", "Be.g4.end", "A1.X.3.2", "Be.sib.1.0", "Be.g2.end",
    "Bl.g0.mid", "small.4", "A1.g0.end", "Cl.in1.end", "A2.sib.1.1", "A2.X.0.2", "Bl.g2.start", "Ce.g2.end",
    "Be.g0.end", "Be.g5.mid", "A1.X.0.2", "A1.g2.end", "Be.g1.mid", "Ce.sib.0.1", "Ce.g5.mid", "Cl.g5.start",
    "Cl.sib.1.0", "Bl.sib.1.0", "Ce.g3.end", "Be.sib.1.1", "A1.sib.0.2", "Be.g3.end", "Ce.g0.end", "Cl.g3.end",
    "Ce.sib.0.2", "Bl.g3.start", "Cl.sib.0.2", "Ce.g4.mid", "Ce.sib.1.1", "Bl.g4.start", "A1.XR.1", "Ce.g5.end",
    "small.5", "Cl.g4.start", "Be.g5.end", "A1.X.2.2", "Ce.g1.end", "Bl.g2.mid", "Bl.g1.mid", "Be.g1.end",
    "Bl.g0.end", "A1.sib.1.1", "Be.sib.0.2", "A1.sib.1.0", "Ce.g4.end", "Ce.sib.1.2", "Bl.g3.mid", "Cl.g1.start",
    "Bl.g5.mid", "Be.sib.1.2", "A2.XR.2", "A2.sib.1.2", "Cl.g4.mid", "Bl.sib.0.1", "Bl.g4.mid", "Bl.sib.1.1",
    "Cl.g5.mid", "Bl.g2.end", "Cl.g1.mid", "Bl.g1.end", "Cl.sib.1.1", "A1.XR.2", "A1.sib.1.2", "small.6",
]

GATHER_TWO = [
    "Cl.g4.end", "Bl.g3.end", "Cl.g1.end", "Cl.g5.end", "Cl.sib.1.2", "Bl.g5.end", "Bl.g4.end", "Bl.sib.1.2",
    "Bl.sib.0.2",
]

SUM_ONE = [
    "comp.gout1", "Cl.g5.start", "Bl.g1.start", "comp.gout0", "Bl.g5.start", "Cl.g2.start", "Bl.g4.start",
    "comp.gfc1", "A2.X.2", "Cl.g4.start", "Bl.g2.start", "Bl.g5.mid", "Bl.g3.start", "Cl.g3.start", "A1.X.2",
    "Cl.g1.start", "Bl.g1.mid", "Bl.g4.mid", "Cl.g0.start", "Cl.g2.mid",
]

SUM_TWO = [
    "Bl.g0.start", "Cl.g0.mid", "Bl.g2.mid", "Cl.g3.mid", "Cl.g4.mid",
]

SUM_THREE = [
    "A2.X.1", "Bl.g3.mid", "Cl.g3.end", "Cl.g5.mid", "Bl.g1.end", "Cl.g2.end", "Bl.g0.mid", "Bl.g4.end",
    "Cl.in0.start", "Cl.g1.mid", "comp.gatt1", "Ce.g5.start", "comp.gatt0", "Be.g5.start", "Ce.g1.start",
    "Be.g1.start", "Bl.g5.end", "Be.g2.start", "Ce.g3.start", "Cl.g5.end", "Be.g3.start", "Ce.g4.start",
    "Be.g4.start", "Ce.g0.start", "Ce.g5.mid", "Be.g0.start", "comp.gfc0", "Ce.g1.mid", "Bl.g2.end", "A2.XR.2",
    "A1.X.1", "A2.X.0", "Be.g5.mid", "Be.g3.mid", "Ce.g3.mid", "Be.g4.mid", "Cl.g4.end", "Be.g1.mid", "Ce.g4.mid",
    "Ce.g2.start", "Bl.g3.end", "comp.first", "small.7", "A2.g3.start", "Ce.g5.end", "Ce.g3.end", "Cl.g0.end",
    "Bl.in1.start", "Bl.in0.start", "Ce.g0.mid", "Be.g5.end", "Cl.in1.start", "A2.g2.start", "A2.XR.1", "Cl.g1.end",
    "A1.XR.2", "Bl.g0.end", "Ce.in1.start", "small.8", "Ce.g4.end", "A2.g0.start", "A1.g0.start", "A1.g2.start",
    "Ce.g2.mid", "Be.g2.mid", "Ce.in1.mid", "Be.g4.end", "A2.g3.mid", "Be.g3.end", "Ce.in0.start", "Cl.in0.mid",
    "Be.in1.start", "Ce.g1.end", "Be.in0.start", "A1.XR.1", "small.9", "Bl.in0.mid", "A1.X.0", "Bl.in1.mid",
    "A1.g3.start", "Cl.in1.mid", "Be.g0.mid", "A1.g2.mid", "Be.g1.end", "Ce.g2.end", "A2.g2.mid", "Be.g2.end",
    "A1.g3.mid", "A2.XR.0", "Bl.in0.end", "Cl.in0.end", "Ce.in1.end", "small.10", "Ce.in0.mid", "Ce.g0.end",
    "A2.g3.end", "Cl.in1.end", "A2.in0.start", "Be.in1.mid", "Be.in0.mid", "Ce.x.s", "Cl.x.s", "A1.XR.0", "A1.g3.end",
    "A1.in0.start", "Bl.in1.end", "Bl.x.s", "A1.g0.mid", "A2.g0.mid", "small.11", "Be.in1.end", "A2.g2.end", "Be.x.s",
    "Be.g0.end", "A2.in0.mid", "A1.g2.end", "A1.in0.mid", "Cl.x.r", "A1.g0.end", "Be.in0.end", "A2.g0.end",
    "Ce.in0.end", "Ce.x.r", "Bl.x.r", "Be.x.r", "A2.in0.end", "A1.in0.end",
]


def remote(src, dst, ssem, rsem, target):
    return pltpu.make_async_remote_copy(
        src_ref=src, dst_ref=dst, send_sem=ssem, recv_sem=rsem, device_id=target, device_id_type=MESH
    )


def kernel(
    seg_ref, gains_ref, bias_ref, tok_ref, qkv_ref, proj_ref, fc_ref, wout_ref, cot_ref,
    act_hbm, grad_hbm, ggain_hbm, gbias_hbm, gqkv_hbm, gproj_hbm, gfc_hbm, gwout_hbm,
    w, rbuf, act_out, grad_out, gsum, ggain_out, gbias_out, tokv, cotv,
    xin, x1, x2, x3, x4, qkv, probs, xh1, xh2, rs1, rs2, dgel, gf, dpre, dbr, datt, dmix, dmid, mask, qbias,
    bf, sgb, sb_y, sb_c, sb_x, sbw, sr, sr_c, sr_x, sr_z, sr_y,
    s_out, s_fc, s_proj, s_qkv, t_out, t_fc, t_proj, t_qkv, hb, sems,
):
    sec = lax.axis_index("section")
    dp = lax.axis_index("dp")
    c = lax.rem(dp, 2)
    y = lax.rem(lax.div(dp, 2), 4)
    z = lax.rem(lax.div(dp, 8), 4)
    x = lax.div(dp, 32)
    ox, oc = 1 - x, 1 - c
    yp = [lax.rem(y + k, 4) for k in range(4)]
    zp = [lax.rem(z + k, 4) for k in range(4)]

    def at(px, pz, py, pc):
        return (sec, ((px * 4 + pz) * 4 + py) * 2 + pc)

    ys = [at(x, z, yp[k], c) for k in range(4)]
    zs = [at(x, zp[k], y, c) for k in range(4)]
    xp = at(ox, z, y, c)
    sib = at(x, z, y, oc)
    other_section = (1 - sec, dp)

    taken = [0, 0]

    def sem():
        taken[0] += 1
        return sems.at[taken[0] - 1]

    def arrivals(pieces):
        taken[1] += pieces
        return taken[1] - pieces

    own = w.at[x, z, y, c]
    own_sem, tok_sem, cot_sem = sem(), sem(), sem()
    pltpu.make_async_copy(qkv_ref, own.at[pl.ds(0, 3)], own_sem).start()
    pltpu.make_async_copy(proj_ref, own.at[pl.ds(3, 1)], own_sem).start()
    pltpu.make_async_copy(fc_ref, own.at[pl.ds(4, 4)], own_sem).start()
    for j in range(4):
        pltpu.make_async_copy(wout_ref.at[:, pl.ds(1024 * j, 1024)], own.at[8 + j], own_sem).start()
    tok_in = pltpu.make_async_copy(tok_ref, tokv, tok_sem)
    cot_in = pltpu.make_async_copy(cot_ref, cotv, cot_sem)
    tok_in.start()
    cot_in.start()
    barrier = pltpu.get_barrier_semaphore()
    partners = ys[1:] + zs[1:] + [xp, sib, other_section]
    for target in partners:
        pl.semaphore_signal(barrier, 1, device_id=target, device_id_type=MESH)
    pl.semaphore_wait(barrier, len(partners))
    pltpu.make_async_copy(own, own, own_sem).wait()

    def slab(part, xx, i, o, half=None, summing=False):
        core, base = c, FIRST[part]
        if summing:
            core, base = (oc if SUM_AT[part][0] else c), SUM_AT[part][1]
        pieces = pl.ds(base, 2) if half is None else pl.ds(base + half, 1)
        pz, py = (o, i) if INNER_IS_Y[part] else (i, o)
        return w.at[xx, pz, py, core, pieces]

    def bytes_of(count):
        two = pl.ds(0, 2)
        return {
            1: w.at[0, 0, 0, 0, two],
            2: w.at[0, 0, two, 0, two],
            4: w.at[0, 0, :, 0, two],
            8: w.at[0, two, :, 0, two],
            15: w.at[0, 0, pl.ds(0, 3), 0, pl.ds(0, 10)],
            16: w.at[0, :, :, 0, two],
            30: w.at[0, two, pl.ds(0, 3), 0, pl.ds(0, 10)],
            32: w.at[:, :, :, 0, two],
        }[count]

    def await_arrival(which, count):
        ref = bytes_of(count)
        remote(ref, ref, which, which, sib).wait_recv()

    def await_sent(which, count):
        ref = bytes_of(count)
        remote(ref, ref, which, which, sib).wait_send()

    def axes(part):
        return (yp, zp, ys, zs) if INNER_IS_Y[part] else (zp, yp, zs, ys)

    def rings_of(part, summing):
        ip, op, idev, odev = axes(part)
        found = {}

        def along_inner(xx):
            return lambda j, half=None: slab(part, xx, ip[j], op[0], half, summing)

        def along_outer(xx, i):
            return lambda j, half=None: slab(part, xx, ip[i], op[j], half, summing)

        for other in (0, 1) if X_FIRST[part] else (0,):
            found[f"in{other}"] = ([along_inner(ox if other else x)], idev[3], idev[1])
        for g, (other, offsets) in enumerate(GROUPS):
            if X_FIRST[part] or not other:
                found[f"g{g}"] = ([along_outer(ox if other else x, i) for i in offsets], odev[3], odev[1])
        return found

    def small(src, dst, sems_of, target):
        return remote(src, dst, sems_of[0], sems_of[1], target)

    ag_rings = {part: rings_of(part, False) for part in PARTS}
    ag_sem = {(part, name): (sem(), sem()) for part in PARTS for name in ag_rings[part]}
    ag_sent = {part: (sem(), sem(), sem()) for part in PARTS}
    ag_x = {part: (sem(),) if X_FIRST[part] else (sem(), sem(), sem()) for part in PARTS}
    ag_sib = {part: sem() for part in PARTS}

    def line(part, xx, o):
        core, base = c, FIRST[part]
        if INNER_IS_Y[part]:
            return w.at[xx, o, :, core, pl.ds(base, 2)]
        return w.at[xx, :, o, core, pl.ds(base, 2)]

    def gather(step):
        part, name, *rest = step.split(".")
        if part == "small":
            small_steps[int(name)]()
            return
        ip, op, _, _ = axes(part)
        if name == "x" and rest[0] == "s":
            ref = slab(part, x, ip[0], op[0])
            remote(ref, ref, ag_sent[part][1], ag_x[part][0], xp).start()
        elif name == "x":
            await_arrival(ag_x[part][0], 1)
        elif name == "X":
            for i in GROUPS[int(rest[0])][1]:
                for o in STAGES[int(rest[1])]:
                    ref = slab(part, x, ip[i], op[o])
                    remote(ref, ref, ag_sent[part][1], ag_x[part][int(rest[1])], xp).start()
        elif name == "XR":
            await_arrival(ag_x[part][int(rest[0])], 4 * len(STAGES[int(rest[0])]))
        elif name == "sib":
            for o in STAGES[int(rest[1])]:
                ref = line(part, ox if int(rest[0]) else x, op[o])
                remote(ref, ref, ag_sent[part][2], ag_sib[part], sib).start()
        else:
            views, left, right = ag_rings[part][name]
            full, half = ag_sem[part, name]
            sent = ag_sent[part][0]
            if rest[0] == "start":
                for view in views:
                    remote(view(0), view(0), sent, full, right).start()
                    remote(view(0), view(0), sent, full, left).start()
            elif rest[0] == "mid":
                await_arrival(full, 2 * len(views))
                for view in views:
                    remote(view(3, 0), view(3, 0), sent, half, right).start()
                    remote(view(1, 1), view(1, 1), sent, half, left).start()
            else:
                await_arrival(half, len(views))

    spread = (
        lax.broadcasted_iota(jnp.int32, (16, 128), 1)
        == lax.broadcasted_iota(jnp.int32, (16, 128), 0) + 16 * (y * 2 + c)
    ).astype(F32)
    sm_y, sm_c, sm_z, sm_x = [(sem(), sem()) for _ in range(4)]

    def small_one():
        sgb[...] = jnp.zeros_like(sgb)
        sgb[0:2, :] = gains_ref[...].astype(F32)
        sgb[2:12, :] = bias_ref[...].astype(F32)
        sb_y[0] = jnp.dot(sgb[...].astype(BF16), spread.astype(BF16), preferred_element_type=F32)
        for k in (1, 2, 3):
            small(sb_y.at[0], sb_y.at[k], sm_y, ys[k]).start()

    def small_two():
        rows = sb_y.at[pl.ds(1, 3)]
        small(rows, rows, sm_y, sib).wait_recv()
        sb_c[0] = sb_y[0] + sb_y[1] + sb_y[2] + sb_y[3]
        small(sb_c.at[0], sb_c.at[1], sm_c, sib).start()

    def small_three():
        small(sb_c.at[0], sb_c.at[1], sm_c, sib).wait_recv()
        sb_x[x, z] = sb_c[0] + sb_c[1]
        for k in (1, 2, 3):
            small(sb_x.at[x, z], sb_x.at[x, z], sm_z, zs[k]).start()

    def small_four():
        rows = sb_x.at[0, pl.ds(0, 3)]
        small(rows, rows, sm_z, sib).wait_recv()
        small(sb_x.at[x], sb_x.at[x], sm_x, xp).start()

    def small_five():
        small(sb_x.at[ox], sb_x.at[ox], sm_x, xp).wait_recv()
        for g in range(8):
            bf[:, g * 128 : (g + 1) * 128] = sb_x[g // 4, g % 4]
        qbias[:, 0:WIDTH] = bf[3:4, :]
        qbias[:, WIDTH : 2 * WIDTH] = jnp.zeros((1, WIDTH), F32)
        qbias[:, 2 * WIDTH :] = bf[4:5, :]

    def row(k):
        return bf[k : k + 1, :]

    def small_six():
        seg = jnp.broadcast_to(seg_ref[...].astype(F32), (ROWS, ROWS))
        qi = lax.broadcasted_iota(jnp.int32, (ROWS, ROWS), 0)
        ki = lax.broadcasted_iota(jnp.int32, (ROWS, ROWS), 1)
        allowed = (seg == seg.T) & (ki <= qi) & (lax.div(qi, 64) == lax.div(ki, 64))
        mask[...] = allowed.astype(F32)

    small_steps = {1: small_one, 2: small_two, 3: small_three, 4: small_four, 5: small_five, 6: small_six}

    for step in GATHER_ONE:
        gather(step)

    handed = (sem(), sem())
    handed_on = remote(act_out, hb, *handed, other_section)
    handed_back = remote(grad_out, hb, *handed, other_section)
    tok_in.wait()
    cot_in.wait()

    @pl.when(sec == 0)
    def _():
        xin[...] = tokv[...].astype(F32)

    @pl.when(sec == 1)
    def _():
        for step in GATHER_TWO:
            gather(step)
        handed_on.wait_recv()
        xin[...] = hb[...].astype(F32)

    def norm(values, gain, shift):
        centre = values - jnp.mean(values, axis=-1, keepdims=True)
        rs = lax.rsqrt(jnp.mean(centre * centre, axis=-1, keepdims=True) + EPS)
        hat = centre * rs
        return hat, rs, (hat * gain + shift).astype(BF16)

    ex_sems = [(sem(), sem()) for _ in range(8)]

    def exchange(slot, src, dst):
        return remote(src, dst, *ex_sems[slot], sib)

    def from_sibling(part):
        await_arrival(ag_sib[part], 32)

    xh1[...], rs1[...], x1[0] = norm(xin[...], row(0), row(2))
    ex_first = exchange(0, x1.at[0], x1.at[1])
    ex_first.start()
    from_sibling("Be")
    from_sibling("Ce")

    def qkv_weights(k):
        return w[k, :, :, :, 0:3].reshape(1536, WIDTH)

    for k in range(2):
        cols = slice(1536 * k, 1536 * (k + 1))
        mixed = lax.dot_general(x1[0], qkv_weights(k), NT, preferred_element_type=F32)
        qkv[:, cols] = (mixed + qbias[:, cols]).astype(BF16)

    low_lanes = lax.broadcasted_iota(jnp.int32, (ROWS, 128), 1) < HEAD
    zero = jnp.zeros((ROWS, 128), BF16)

    def pair(base, hp):
        return slice(base + hp * 128, base + hp * 128 + 128)

    def lanes_of(e):
        return low_lanes if e == 0 else ~low_lanes

    raw = []
    for hp in range(8):
        q, k = qkv[:, pair(0, hp)], qkv[:, pair(WIDTH, hp)]
        for e in range(2):
            raw.append(lax.dot_general(jnp.where(lanes_of(e), q, zero), k, NT, preferred_element_type=F32))
    seen = mask[...] > 0.5
    soft = []
    for scores in raw:
        scores = jnp.where(seen, scores * 0.125, -1e30)
        ex = jnp.exp(scores - jnp.max(scores, axis=-1, keepdims=True))
        soft.append(ex * (1.0 / jnp.sum(ex, axis=-1, keepdims=True)))
    for hp in range(8):
        v = qkv[:, pair(2 * WIDTH, hp)]
        parts = []
        for e in range(2):
            probs[2 * hp + e] = soft[2 * hp + e]
            parts.append(jnp.dot(soft[2 * hp + e].astype(BF16), v, preferred_element_type=F32))
        x2[0, :, pair(0, hp)] = jnp.where(low_lanes, parts[0], parts[1]).astype(BF16)
    ex_att = exchange(1, x2.at[0], x2.at[1])
    ex_att.start()

    def proj_weights():
        return w[:, :, :, :, 3].reshape(WIDTH, WIDTH)

    xin[...] = xin[...] + (lax.dot_general(x2[0], proj_weights(), NT, preferred_element_type=F32) + row(5))
    xh2[...], rs2[...], x3[0] = norm(xin[...], row(1), row(6))
    ex_second = exchange(2, x3.at[0], x3.at[1])
    ex_second.start()

    @pl.when(sec == 0)
    def _():
        for step in GATHER_TWO:
            gather(step)

    from_sibling("A1")
    from_sibling("A2")

    def fc_weights(j):
        return w[j // 2, 2 * (j % 2) : 2 * (j % 2) + 2, :, :, 4:8].reshape(WIDTH, WIDTH)

    for j in range(4):
        pre = lax.dot_general(x3[0], fc_weights(j), NT, preferred_element_type=F32) + row(7 + j)
        square = pre * pre
        t = jnp.tanh(GC * (pre + 0.044715 * (square * pre)))
        half = 0.5 * (1.0 + t)
        x4[0, j] = (pre * half).astype(BF16)
        dgel[j] = half + (0.5 * GC) * pre * (1.0 - t * t) * (1.0 + 0.134145 * square)
    ex_act = exchange(3, x4.at[0], x4.at[1])
    ex_act.start()
    from_sibling("Bl")
    from_sibling("Cl")

    def wout_weights(j):
        return w[:, :, :, :, 8 + j].reshape(WIDTH, WIDTH)

    result = xin[...] + row(11)
    for j in range(4):
        result = result + lax.dot_general(x4[0, j], wout_weights(j), NT, preferred_element_type=F32)
    act_out[...] = result.astype(BF16)

    @pl.when(sec == 0)
    def _():
        handed_on.start()

    act_done = pltpu.make_async_copy(act_out, act_hbm, tok_sem)
    act_done.start()

    for part in PARTS:
        await_sent(ag_sent[part][0], 30 if X_FIRST[part] else 15)
        await_sent(ag_sent[part][1], 1 if X_FIRST[part] else 16)
        await_sent(ag_sent[part][2], 32)
    rows = sb_y.at[pl.ds(1, 3)]
    small(rows, rows, sm_y, sib).wait_send()
    small(sb_c.at[0], sb_c.at[1], sm_c, sib).wait_send()
    small(rows, rows, sm_z, sib).wait_send()
    small(sb_x.at[x], sb_x.at[x], sm_x, xp).wait_send()

    @pl.when(sec == 0)
    def _():
        handed_back.wait_recv()
        gf[...] = hb[...]

    @pl.when(sec == 1)
    def _():
        gf[...] = cotv[...]

    def column_sum(values):
        return jnp.sum(values.astype(F32), axis=0, keepdims=True)

    sbw[...] = jnp.zeros_like(sbw)
    sbw[11:12, :] = column_sum(gf[...])
    s_out[...] = gf[...].T.reshape(2, 4, 4, 2, 1, 16, ROWS)

    def swap(slot, src, dst):
        return exchange(slot, src.at[:, :, :, oc], dst)

    ex_gf = swap(4, s_out, t_out)
    ex_gf.start()
    for j in range(4):
        d_act = jnp.dot(gf[...], wout_weights(j), preferred_element_type=F32)
        d_pre = (dgel[j] * d_act).astype(BF16)
        dpre[j] = d_pre
        sbw[7 + j : 8 + j, :] = column_sum(d_pre)
        s_fc[j // 2, 2 * (j % 2) : 2 * (j % 2) + 2] = d_pre.T.reshape(2, 4, 2, 4, 16, ROWS)
    ex_dpre = swap(5, s_fc, t_fc)
    ex_dpre.start()
    ex_dbr = swap(6, s_proj, t_proj)
    ex_dmix = swap(7, s_qkv, t_qkv)

    def lhs(mine, theirs, rows):
        return jnp.concatenate([mine.reshape(rows, ROWS), theirs.reshape(rows, ROWS)], axis=1)

    def product(left, right):
        return jnp.dot(left, right, preferred_element_type=F32).astype(BF16)

    def grads_out(xx):
        left = lhs(s_out[xx, :, :, c], t_out[xx], 256)
        for j in range(4):
            w[xx, :, :, oc, 8 + j] = product(left, x4[:, j].reshape(2 * ROWS, WIDTH)).reshape(4, 4, 16, WIDTH)

    def grads_fc(xx):
        for k in range(2):
            zz = slice(2 * k, 2 * k + 2)
            left = lhs(s_fc[xx, zz, :, c], t_fc[xx, zz], 512)
            w[xx, zz, :, c, 8:12] = product(left, x3[...].reshape(2 * ROWS, WIDTH)).reshape(2, 4, 4, 16, WIDTH)

    def grads_att(xx):
        left = lhs(s_proj[xx, :, :, c], t_proj[xx], 256)
        w[xx, :, :, c, 7] = product(left, x2[...].reshape(2 * ROWS, WIDTH)).reshape(4, 4, 16, WIDTH)
        for k in range(2):
            zz = slice(2 * k, 2 * k + 2)
            left = lhs(s_qkv[xx, zz, :, c], t_qkv[xx, zz], 384)
            w[xx, zz, :, c, 4:7] = product(left, x1[...].reshape(2 * ROWS, WIDTH)).reshape(2, 4, 3, 16, WIDTH)

    def compute(name):
        if name == "gout1":
            ex_gf.wait_recv()
            ex_act.wait_recv()
            grads_out(ox)
        elif name == "gout0":
            grads_out(x)
        elif name == "gfc1":
            ex_dpre.wait_recv()
            ex_second.wait_recv()
            grads_fc(ox)
        elif name == "gfc0":
            grads_fc(x)
        elif name == "gatt1":
            ex_first.wait_recv()
            ex_att.wait_recv()
            ex_dbr.wait_recv()
            ex_dmix.wait_recv()
            grads_att(ox)
        elif name == "gatt0":
            grads_att(x)
        elif name == "first":
            pl.when(sec == 0)(back_first)

    rs_rings = {part: rings_of(part, True) for part in PARTS}
    rs_sem = {(part, name): (sem(), sem()) for part in PARTS for name in rs_rings[part]}
    rs_sent = {part: (sem(), sem()) for part in PARTS}
    rs_x = {part: (sem(),) if X_FIRST[part] else (sem(), sem(), sem()) for part in PARTS}
    rs_at = {(part, name): arrivals(6 * len(rs_rings[part][name][0])) for part in PARTS for name in rs_rings[part]}
    rs_x_at = {part: arrivals(2 if X_FIRST[part] else 32) for part in PARTS}

    def add(view, *terms, out=None):
        total = view[...].astype(F32)
        for term in terms:
            total = total + term[...].astype(F32)
        if out is None:
            view[...] = total.astype(BF16)
        else:
            out[...] = total

    def own_sum(part):
        return gsum.at[pl.ds(FIRST[part], 2)]

    def summing(step):
        part, name, *rest = step.split(".")
        if part == "small":
            small_steps[int(name)]()
            return
        if part == "comp":
            compute(name)
            return
        ip, op, _, _ = axes(part)
        if name == "x" and rest[0] == "s":
            buf = rbuf.at[pl.ds(rs_x_at[part], 2)]
            remote(slab(part, ox, ip[0], op[0], None, True), buf, rs_sent[part][1], rs_x[part][0], xp).start()
        elif name == "x":
            await_arrival(rs_x[part][0], 1)
            add(slab(part, x, ip[0], op[0], None, True), rbuf.at[pl.ds(rs_x_at[part], 2)], out=own_sum(part))
        elif name in ("X", "XR"):
            stage = int(rest[0])
            if name == "XR":
                await_arrival(rs_x[part][stage], 4 * len(STAGES[stage]))
            for o in STAGES[stage]:
                for i in range(4):
                    buf = rbuf.at[pl.ds(rs_x_at[part] + (o * 4 + i) * 2, 2)]
                    if name == "X":
                        ref = slab(part, ox, ip[i], op[o], None, True)
                        remote(ref, buf, rs_sent[part][1], rs_x[part][stage], xp).start()
                    else:
                        add(slab(part, x, ip[i], op[o], None, True), buf)
        else:
            views, left, right = rs_rings[part][name]
            half, full = rs_sem[part, name]
            sent = rs_sent[part][0]

            def buf(k, offset, size):
                return rbuf.at[pl.ds(rs_at[part, name] + 6 * k + offset, size)]

            if rest[0] == "start":
                for k, view in enumerate(views):
                    remote(view(2, 0), buf(k, 0, 1), sent, half, right).start()
                    remote(view(2, 1), buf(k, 1, 1), sent, half, left).start()
            elif rest[0] == "mid":
                await_arrival(half, len(views))
                for k, view in enumerate(views):
                    add(view(1, 0), buf(k, 0, 1))
                    remote(view(1), buf(k, 2, 2), sent, full, right).start()
                    add(view(3, 1), buf(k, 1, 1))
                    remote(view(3), buf(k, 4, 2), sent, full, left).start()
            else:
                await_arrival(full, 2 * len(views))
                last = name == "in0" and not X_FIRST[part]
                for k, view in enumerate(views):
                    add(view(0), buf(k, 2, 2), buf(k, 4, 2), out=own_sum(part) if last else None)

    sm_core, sm_xs, sm_zs, sm_ys = [(sem(), sem()) for _ in range(4)]

    def small_seven():
        for g in range(8):
            sr[g // 4, g % 4] = sbw[:, g * 128 : (g + 1) * 128]
        small(sr, sr_c, sm_core, sib).start()

    def small_eight():
        small(sr, sr_c, sm_core, sib).wait()
        sr[...] = sr[...] + sr_c[...]
        small(sr.at[ox], sr_x, sm_xs, xp).start()

    def small_nine():
        small(sr.at[ox], sr_x, sm_xs, xp).wait_recv()
        sr[x] = sr[x] + sr_x[...]
        for k in (1, 2, 3):
            small(sr.at[x, zp[k]], sr_z.at[k - 1], sm_zs, zs[k]).start()

    def small_ten():
        small(sr_z, sr_z, sm_zs, sib).wait_recv()
        sr_y[0] = sr[x, z] + sr_z[0] + sr_z[1] + sr_z[2]
        for k in (1, 2, 3):
            small(sr_y.at[0], sr_y.at[k], sm_ys, ys[k]).start()

    def small_eleven():
        rows = sr_y.at[pl.ds(1, 3)]
        small(rows, rows, sm_ys, sib).wait_recv()
        total = sr_y[0] + sr_y[1] + sr_y[2] + sr_y[3]
        picked = lax.dot_general(total, spread, NT, preferred_element_type=F32, precision=lax.Precision.HIGHEST)
        ggain_out[...] = picked[0:2, :]
        for k in range(10):
            gbias_out[k] = picked[2 + k : 3 + k, :]

    small_steps.update({7: small_seven, 8: small_eight, 9: small_nine, 10: small_ten, 11: small_eleven})

    @pl.when(sec == 0)
    def _():
        for step in SUM_ONE:
            summing(step)

    d_second = jnp.zeros((ROWS, WIDTH), F32)
    for j in range(4):
        d_second = d_second + jnp.dot(dpre[j], fc_weights(j), preferred_element_type=F32)

    def norm_back(d_out, hat, rs, gain):
        d_hat = d_out * gain
        mean_one = jnp.mean(d_hat, axis=-1, keepdims=True)
        mean_two = jnp.mean(d_hat * hat, axis=-1, keepdims=True)
        return rs * (d_hat - mean_one - hat * mean_two)

    sbw[1:2, :] = column_sum(d_second * xh2[...])
    sbw[6:7, :] = column_sum(d_second)
    dmid[...] = gf[...].astype(F32) + norm_back(d_second, xh2[...], rs2[...], row(1))
    dbr[...] = dmid[...].astype(BF16)
    sbw[5:6, :] = column_sum(dbr[...])
    s_proj[...] = dbr[...].T.reshape(2, 4, 4, 2, 1, 16, ROWS)
    ex_dbr.start()

    @pl.when(sec == 0)
    def _():
        for step in SUM_TWO:
            summing(step)

    datt[...] = jnp.dot(dbr[...], proj_weights(), preferred_element_type=F32).astype(BF16)
    d_probs, masked_da = [], []
    for hp in range(8):
        da, v = datt[:, pair(0, hp)], qkv[:, pair(2 * WIDTH, hp)]
        for e in range(2):
            masked_da.append(jnp.where(lanes_of(e), da, zero))
            d_probs.append(lax.dot_general(masked_da[-1], v, NT, preferred_element_type=F32))
    d_scores = []
    for h in range(16):
        p, dp_ = probs[h], d_probs[h]
        d_scores.append((p * (dp_ - jnp.sum(dp_ * p, axis=-1, keepdims=True))).astype(BF16))
    for hp in range(8):
        q, k = qkv[:, pair(0, hp)], qkv[:, pair(WIDTH, hp)]
        dq, dk, dv = [], [], []
        for e in range(2):
            h = 2 * hp + e
            dv.append(jnp.dot(probs[h].astype(BF16).T, masked_da[h], preferred_element_type=F32))
            dq.append(jnp.dot(d_scores[h], k, preferred_element_type=F32))
            dk.append(jnp.dot(d_scores[h].T, jnp.where(lanes_of(e), q, zero), preferred_element_type=F32))
        dmix[:, pair(0, hp)] = (jnp.where(low_lanes, dq[0], dq[1]) * 0.125).astype(BF16)
        dmix[:, pair(WIDTH, hp)] = ((dk[0] + dk[1]) * 0.125).astype(BF16)
        dmix[:, pair(2 * WIDTH, hp)] = (dv[0] + dv[1]).astype(BF16)
    for k in range(2):
        s_qkv[k] = dmix[:, 1536 * k : 1536 * (k + 1)].T.reshape(4, 4, 2, 3, 16, ROWS)
    ex_dmix.start()
    sbw[3:4, :] = column_sum(dmix[:, 0:WIDTH])
    sbw[4:5, :] = column_sum(dmix[:, 2 * WIDTH :])

    def back_first():
        d_first = jnp.dot(dmix[:, 0:1536], qkv_weights(0), preferred_element_type=F32)
        d_first = d_first + jnp.dot(dmix[:, 1536:], qkv_weights(1), preferred_element_type=F32)
        sbw[0:1, :] = column_sum(d_first * xh1[...])
        sbw[2:3, :] = column_sum(d_first)
        grad_out[...] = (dmid[...] + norm_back(d_first, xh1[...], rs1[...], row(0))).astype(BF16)
        pltpu.make_async_copy(grad_out, grad_hbm, cot_sem).start()

    @pl.when(sec == 1)
    def _():
        back_first()
        handed_back.start()
        for step in SUM_ONE + SUM_TWO:
            summing(step)

    for step in SUM_THREE:
        summing(step)

    done = [
        pltpu.make_async_copy(gsum.at[pl.ds(0, 3)], gqkv_hbm, own_sem),
        pltpu.make_async_copy(gsum.at[pl.ds(3, 1)], gproj_hbm, own_sem),
        pltpu.make_async_copy(gsum.at[pl.ds(4, 4)], gfc_hbm, own_sem),
    ] + [
        pltpu.make_async_copy(gsum.at[8 + j], gwout_hbm.at[:, pl.ds(1024 * j, 1024)], own_sem) for j in range(4)
    ]
    for cp in done:
        cp.start()
    small_done = [
        pltpu.make_async_copy(ggain_out, ggain_hbm, sem()),
        pltpu.make_async_copy(gbias_out, gbias_hbm, sem()),
    ]
    for cp in small_done:
        cp.start()

    for part in PARTS:
        await_sent(rs_sent[part][0], 30 if X_FIRST[part] else 15)
        await_sent(rs_sent[part][1], 1 if X_FIRST[part] else 16)
    for cp in (ex_first, ex_att, ex_second, ex_act, ex_gf, ex_dpre, ex_dbr, ex_dmix):
        cp.wait_send()
    small(sr.at[ox], sr_x, sm_xs, xp).wait_send()
    small(sr_z, sr_z, sm_zs, sib).wait_send()
    rows = sr_y.at[pl.ds(1, 3)]
    small(rows, rows, sm_ys, sib).wait_send()

    @pl.when(sec == 0)
    def _():
        handed_on.wait_send()

    @pl.when(sec == 1)
    def _():
        handed_back.wait_send()

    act_done.wait()
    pltpu.make_async_copy(grad_out, grad_hbm, cot_sem).wait()
    pltpu.make_async_copy(gsum, gsum, own_sem).wait()
    for cp in small_done:
        cp.wait()
    if (taken[0], taken[1]) != (SEMAPHORES, ARRIVALS):
        raise ValueError(taken)


SEMAPHORES = 255
ARRIVALS = 372


def move(*refs):
    count = len(refs) // 3
    sems = refs[-1]
    into = [pltpu.make_async_copy(refs[k], refs[2 * count + k], sems.at[0, k]) for k in range(count)]
    out = [pltpu.make_async_copy(refs[2 * count + k], refs[count + k], sems.at[1, k]) for k in range(count)]
    for cp in into:
        cp.start()
    for k in range(count):
        into[k].wait()
        out[k].start()
    for cp in out:
        cp.wait()


def local(tokens, segment_ids, gains, biases, w_qkv, w_proj, w_fc, w_out, cotangent):
    vmem = pl.BlockSpec(memory_space=pltpu.VMEM)
    hbm = pl.BlockSpec(memory_space=pl.ANY)

    def shape(*dims, dtype=F32):
        return jax.ShapeDtypeStruct(dims, dtype)

    def v(*dims, dtype=BF16):
        return pltpu.VMEM(dims, dtype)

    scratch = [
        v(2, 4, 4, 2, 12, 16, WIDTH), v(ARRIVALS, 16, WIDTH),
        v(ROWS, WIDTH), v(ROWS, WIDTH), v(12, 16, WIDTH, dtype=F32), v(2, 16, dtype=F32), v(10, 1, 16, dtype=F32),
        v(ROWS, WIDTH), v(ROWS, WIDTH),
        v(ROWS, WIDTH, dtype=F32), v(2, ROWS, WIDTH), v(2, ROWS, WIDTH), v(2, ROWS, WIDTH), v(2, 4, ROWS, WIDTH),
        v(ROWS, 3 * WIDTH), v(16, ROWS, ROWS, dtype=F32), v(ROWS, WIDTH, dtype=F32), v(ROWS, WIDTH, dtype=F32),
        v(ROWS, 1, dtype=F32), v(ROWS, 1, dtype=F32), v(4, ROWS, WIDTH, dtype=F32), v(ROWS, WIDTH),
        v(4, ROWS, WIDTH), v(ROWS, WIDTH), v(ROWS, WIDTH), v(ROWS, 3 * WIDTH), v(ROWS, WIDTH, dtype=F32),
        v(ROWS, ROWS, dtype=F32), v(1, 3 * WIDTH, dtype=F32),
        v(16, WIDTH, dtype=F32), v(16, 16, dtype=F32), v(4, 16, 128, dtype=F32), v(2, 16, 128, dtype=F32),
        v(2, 4, 16, 128, dtype=F32), v(16, WIDTH, dtype=F32), v(2, 4, 16, 128, dtype=F32),
        v(2, 4, 16, 128, dtype=F32), v(4, 16, 128, dtype=F32), v(3, 16, 128, dtype=F32), v(4, 16, 128, dtype=F32),
        v(2, 4, 4, 2, 1, 16, ROWS), v(2, 4, 4, 2, 4, 16, ROWS), v(2, 4, 4, 2, 1, 16, ROWS), v(2, 4, 4, 2, 3, 16, ROWS),
        v(2, 4, 4, 1, 16, ROWS), v(2, 4, 4, 4, 16, ROWS), v(2, 4, 4, 1, 16, ROWS), v(2, 4, 4, 3, 16, ROWS),
        v(ROWS, WIDTH),
        pltpu.SemaphoreType.DMA((SEMAPHORES,)),
    ]
    results = (
        shape(ROWS, WIDTH, dtype=BF16), shape(ROWS, WIDTH, dtype=BF16), shape(2, 16), shape(10, 1, 16),
        shape(3, 16, WIDTH), shape(1, 16, WIDTH), shape(4, 16, WIDTH), shape(16, 4 * WIDTH),
    )
    out = pl.pallas_call(
        kernel,
        out_shape=results,
        in_specs=[vmem, vmem, vmem] + [hbm] * 6,
        out_specs=(hbm,) * 8,
        scratch_shapes=scratch,
        compiler_params=pltpu.CompilerParams(
            collective_id=0, has_side_effects=True, vmem_limit_bytes=63 * 2**20
        ),
        name="relay",
    )(
        segment_ids.reshape(1, ROWS),
        gains[0],
        biases[0],
        tokens,
        w_qkv[0].T.reshape(3, 16, WIDTH),
        w_proj[0].T.reshape(1, 16, WIDTH),
        w_fc[0].T.reshape(4, 16, WIDTH),
        w_out[0].T,
        cotangent,
    )
    out = pl.pallas_call(
        move,
        out_shape=results,
        in_specs=[hbm] * 8,
        out_specs=(hbm,) * 8,
        scratch_shapes=[pltpu.VMEM(r.shape, r.dtype) for r in results] + [pltpu.SemaphoreType.DMA((2, 8))],
        name="move",
    )(*out)
    activations, input_grads, g_gains, g_biases, g_qkv, g_proj, g_fc, g_out = out
    return (
        activations[None],
        input_grads[None],
        g_gains[None],
        g_biases.transpose(1, 0, 2),
        g_qkv.reshape(48, WIDTH).T[None],
        g_proj.reshape(16, WIDTH).T[None],
        g_fc.reshape(64, WIDTH).T[None],
        g_out.T[None],
    )


def solution(mesh):
    weight = P("section", None, "dp")
    rows = P("section", "dp", None)
    return jax.shard_map(
        local,
        mesh=mesh,
        in_specs=(P("dp", None), P("dp")) + (weight,) * 6 + (P("dp", None),),
        out_specs=(rows, rows) + (weight,) * 6,
        check_vma=False,
    )
```

time: 3970 us -> 177 us (0.04)
  waiting for transfers between devices: 3200 us -> 0 us
  matrix products: 259 us -> 0 us
  local copies, waits for them, and re-layouts: 241 us -> 0 us
  blocking collectives: 189 us -> 0 us
  Pallas kernels: 0 us -> 176 us
    unnamed x16 -> x0, waiting for transfers between devices: 3110 us -> none
    dot_general x66 -> x0, matrix products: 259 us -> none  [the longest x3 33.9 us: forward_block(): jnp.dot(act, w_out, preferred_element_type=jnp.float32) + biases[9]]
    all_gather x2 -> x0, blocking collectives: 189 us -> none  [the longest x1 99.2 us: local(): lax.all_gather(biases, 'dp', axis=2, tiled=True)]
    pallas_call x0 -> x2, Pallas kernels: none -> 176 us  [the longest x1 174 us: local(): pl.pallas_call(kernel, out_shape=results, in_specs=[vmem, vmem, vmem] + [...]
    broadcast_in_dim x4 -> x0, local copies, waits for them, and re-layouts: 113 us -> none  [the longest x1 37.4 us: local(): totals[5][None]]
    all_gather x4 -> x0, waiting for transfers between devices: 85 us -> none  [the longest x1 83.6 us: local(): lax.all_gather(w_out, 'dp', axis=2, tiled=True)]
    unnamed x306 -> x0, local copies, waits for them, and re-layouts: 48.4 us -> none
  transfers between devices with their start and end apart: 14 -> 0, of which waited for: 10 -> 0; matrix products, arithmetic and copies ran while one was open for 8% -> 0% of each run, Pallas kernels for 0% -> 0%
where the time goes in v3:
time: 177 us
  Pallas kernels  176 us (99%)
    pallas_call x1, Pallas kernels, local(): pl.pallas_call(kernel, out_shape=results, in_specs=[vmem, vmem, vmem] + [...  174 us

profile of v3, /device:TPU:0, one launch (start us, length us, event | category | flops | bytes accessed | tf_op | source)
XLA Modules:
  0.0 177.1 jit_solution(11252427128474359425)
XLA Ops:
  0.6 174.1 %relay.1 = (bf16[128,1024]{1,0:T(8,128)(2,1)}, bf16[128,1024]{1,0:T(8,128)(2,1)}, f32[2,16]{1,0:T(2,128)}, f32[10,1,16]{2,1,0:T(1,128)}, f32[3,16,1024]{2,1,0:T(...) custom-call(s32[1,128]{1,0:T(1,128)} %bitcast.48, bf16[2,16]{1,0:T(2,128)(2,1)} %bitcast.49, ...), custom_call_target="tpu_custom_call" | custom-call | tf_op jit(solution)/shard_map/relay/pallas_call | solution.py:788
  174.8 2.1 %move.1 = (bf16[128,1024]{1,0:T(8,128)(2,1)}, bf16[128,1024]{1,0:T(8,128)(2,1)}, f32[2,16]{1,0:T(2,128)}, f32[10,1,16]{2,1,0:T(1,128)}, f32[3,16,1024]{2,1,0:T(8...) custom-call(bf16[128,1024]{1,0:T(8,128)(2,1)} %get-tuple-element.24.refs_0_, ...), custom_call_target="tpu_custom_call" | custom-call | tf_op jit(solution)/shard_map/move/pallas_call | solution.py:809

commit v4 on v3

--- a/solution.py
+++ b/solution.py
@@ -19,68 +19,63 @@
 FIRST = {"Be": 0, "Ce": 2, "A1": 4, "A2": 6, "Bl": 8, "Cl": 10}
 INNER_IS_Y = {"Be": False, "Ce": True, "A1": True, "A2": False, "Bl": False, "Cl": True}
 X_FIRST = {"Be": True, "Ce": True, "A1": False, "A2": False, "Bl": True, "Cl": True}
-GROUPS = ((0, (0,)), (1, (0,)), (0, (1, 3)), (0, (2,)), (1, (1, 3)), (1, (2,)))
+GROUPS = {
+    "g0": (0, (0,)), "g1": (1, (0,)), "g2": (0, (1, 3)), "g3": (0, (2,)), "g4": (1, (1, 3)), "g5": (1, (2,)),
+    "gA": (0, (0, 1, 2, 3)), "gB": (1, (0, 1, 2, 3)),
+}
+FINE = ("g0", "g1", "g2", "g3", "g4", "g5")
+COARSE = ("gA", "gB")
+GATHER_GROUPS = {"Be": COARSE, "Ce": COARSE, "A1": FINE, "A2": FINE, "Bl": COARSE, "Cl": COARSE}
+SUM_GROUPS = {"Be": COARSE, "Ce": COARSE, "A1": COARSE, "A2": COARSE, "Bl": COARSE, "Cl": COARSE}
 STAGES = ((0,), (1, 3), (2,))
 SUM_AT = {"Be": (0, 4), "Ce": (0, 6), "A1": (0, 8), "A2": (0, 10), "Bl": (1, 8), "Cl": (1, 10)}
 
 GATHER_ONE = [
-    "Be.x.s", "A2.in0.start", "Ce.x.s", "A1.in0.start", "A1.g0.start", "Bl.in0.start", "Ce.in0.start", "Cl.in0.start",
-    "A1.X.0.0", "A2.in0.mid", "Be.x.r", "A1.in0.mid", "A2.g0.start", "Ce.g0.start", "small.1", "Bl.x.s", "Ce.x.r",
-    "A2.X.2.0", "Be.g0.start", "Cl.x.s", "A2.X.0.0", "A2.g2.start", "Ce.in0.mid", "A1.X.2.0", "Be.in0.start",
-    "A1.in0.end", "A1.g0.mid", "A1.g3.start", "Bl.in0.mid", "Cl.g0.start", "Be.in0.mid", "A1.X.3.0", "Be.g2.start",
-    "Cl.x.r", "Cl.in0.mid", "Cl.g2.start", "A2.in0.end", "A2.X.3.0", "Be.in1.start", "A2.g3.start", "Ce.in1.start",
-    "Cl.in1.start", "A1.X.0.1", "Bl.in0.end", "A2.g2.mid", "Cl.g0.mid", "A1.sib.0.0", "A1.g3.mid", "Ce.g1.start",
-    "Bl.x.r", "Bl.in1.start", "A2.g0.mid", "Be.g2.mid", "Cl.in0.end", "Cl.sib.0.0", "Be.in1.mid", "A2.X.2.1",
-    "Ce.in0.end", "Be.in0.end", "Be.g3.start", "small.2", "A1.g2.start", "A2.g3.mid", "A2.X.3.1", "Ce.g2.start",
-    "Be.g0.mid", "A2.X.0.1", "Be.g1.start", "A2.g2.end", "A2.g0.end", "Ce.sib.0.0", "Cl.g3.start", "A2.sib.0.1",
-    "Ce.in1.mid", "Be.g4.start", "A2.g3.end", "Cl.g2.mid", "Bl.g0.start", "A2.sib.0.2", "Be.g3.mid", "Bl.in1.mid",
-    "A2.sib.0.0", "Be.in1.end", "Bl.sib.0.0", "A2.XR.0", "Ce.g2.mid", "Cl.in1.mid", "A1.X.3.1", "Be.sib.0.1",
-    "Be.sib.0.0", "A2.X.2.2", "small.3", "Ce.g3.start", "A1.g2.mid", "Ce.in1.end", "Ce.g0.mid", "A2.sib.1.0",
-    "Ce.g5.start", "Cl.g3.mid", "A1.sib.0.1", "Cl.sib.0.1", "A1.X.2.1", "A2.X.3.2", "Be.g4.mid", "A2.XR.1",
-    "A1.g3.end", "Be.g5.start", "Ce.g1.mid", "Bl.in1.end", "Bl.g5.start", "Ce.g3.mid", "Cl.g2.end", "Bl.g1.start",
-    "A1.XR.0", "Ce.sib.1.0", "Cl.g0.end", "Ce.g4.start", "Be.g4.end", "A1.X.3.2", "Be.sib.1.0", "Be.g2.end",
-    "Bl.g0.mid", "small.4", "A1.g0.end", "Cl.in1.end", "A2.sib.1.1", "A2.X.0.2", "Bl.g2.start", "Ce.g2.end",
-    "Be.g0.end", "Be.g5.mid", "A1.X.0.2", "A1.g2.end", "Be.g1.mid", "Ce.sib.0.1", "Ce.g5.mid", "Cl.g5.start",
-    "Cl.sib.1.0", "Bl.sib.1.0", "Ce.g3.end", "Be.sib.1.1", "A1.sib.0.2", "Be.g3.end", "Ce.g0.end", "Cl.g3.end",
-    "Ce.sib.0.2", "Bl.g3.start", "Cl.sib.0.2", "Ce.g4.mid", "Ce.sib.1.1", "Bl.g4.start", "A1.XR.1", "Ce.g5.end",
-    "small.5", "Cl.g4.start", "Be.g5.end", "A1.X.2.2", "Ce.g1.end", "Bl.g2.mid", "Bl.g1.mid", "Be.g1.end",
-    "Bl.g0.end", "A1.sib.1.1", "Be.sib.0.2", "A1.sib.1.0", "Ce.g4.end", "Ce.sib.1.2", "Bl.g3.mid", "Cl.g1.start",
-    "Bl.g5.mid", "Be.sib.1.2", "A2.XR.2", "A2.sib.1.2", "Cl.g4.mid", "Bl.sib.0.1", "Bl.g4.mid", "Bl.sib.1.1",
-    "Cl.g5.mid", "Bl.g2.end", "Cl.g1.mid", "Bl.g1.end", "Cl.sib.1.1", "A1.XR.2", "A1.sib.1.2", "small.6",
+    "Ce.x.s", "A2.in0.start", "A1.in0.start", "A2.g0.start", "A2.X.g0.0", "Be.in0.start", "Bl.in0.start",
+    "Ce.in0.start", "A1.g0.start", "Cl.x.s", "Cl.in0.start", "A1.in0.mid", "Ce.x.r", "Bl.x.s", "small.1", "Be.x.s",
+    "A2.g0.mid", "Be.in0.mid", "A2.in0.mid", "A1.g2.start", "A2.X.g2.0", "Ce.in1.start", "A2.g2.start", "A2.X.g0.1",
+    "A1.in0.end", "Be.in0.end", "Bl.x.r", "Ce.in0.mid", "A1.sib.0.0", "Be.x.r", "Be.in1.start", "A1.g3.start",
+    "Bl.in1.start", "Ce.in1.mid", "A1.X.g2.0", "Cl.x.r", "Bl.in0.mid", "Be.gA.start", "Ce.in0.end", "A1.g0.mid",
+    "Be.in1.mid", "A1.X.g3.0", "small.2", "A1.g3.mid", "A2.in0.end", "A2.X.g3.0", "A2.g3.start", "Ce.in1.end",
+    "Ce.gA.start", "A1.g0.end", "A1.X.g0.0", "A2.sib.0.0", "Bl.in1.mid", "Cl.in1.start", "Be.in1.end", "Cl.in0.mid",
+    "Be.gB.start", "A1.g2.mid", "A1.g3.end", "A1.X.g2.1", "A1.X.g0.1", "Ce.gB.start", "A2.g3.mid", "small.3",
+    "A1.XR.0", "Be.sib.1.0", "A2.XR.0", "Be.gA.mid", "Be.sib.0.0", "A1.X.g3.1", "A2.g2.mid", "Ce.sib.0.0",
+    "A1.X.g3.2", "Cl.in0.end", "Bl.in0.end", "A2.X.g3.1", "A2.sib.0.1", "Bl.sib.0.0", "A1.sib.1.0", "Cl.in1.mid",
+    "Be.gB.mid", "Ce.gA.mid", "Be.sib.0.1", "A1.sib.0.1", "Ce.gB.mid", "small.4", "A2.X.g2.1", "A2.g2.end",
+    "A1.X.g0.2", "Bl.in1.end", "Ce.sib.1.0", "Be.sib.1.1", "Ce.sib.1.1", "Ce.sib.0.1", "Cl.gA.start", "A2.g3.end",
+    "Bl.gA.start", "A1.XR.1", "Ce.gA.end", "Ce.gB.end", "A1.g2.end", "Be.gA.end", "Be.gB.end", "A1.X.g2.2",
+    "A2.X.g2.2", "Ce.sib.0.2", "small.5", "Bl.gB.start", "Cl.in1.end", "Cl.sib.1.0", "A2.g0.end", "Be.sib.1.2",
+    "Cl.gB.start", "Ce.sib.1.2", "Cl.sib.0.0", "A2.X.g3.2", "Be.sib.0.2", "A2.sib.1.0", "A2.X.g0.2", "A1.sib.1.1",
+    "A2.XR.1", "Cl.gA.mid", "Bl.gA.mid", "Bl.sib.0.1", "A2.sib.0.2", "Bl.sib.1.0", "Cl.sib.0.1", "A2.sib.1.1",
+    "small.6",
 ]
 
 GATHER_TWO = [
-    "Cl.g4.end", "Bl.g3.end", "Cl.g1.end", "Cl.g5.end", "Cl.sib.1.2", "Bl.g5.end", "Bl.g4.end", "Bl.sib.1.2",
-    "Bl.sib.0.2",
+    "Cl.gB.mid", "A1.sib.0.2", "Cl.sib.1.1", "Bl.gB.mid", "A1.XR.2", "A1.sib.1.2", "A2.XR.2", "Bl.gA.end",
+    "A2.sib.1.2", "Cl.gA.end", "Cl.sib.0.2", "Bl.sib.1.1", "Cl.gB.end", "Cl.sib.1.2", "Bl.sib.0.2", "Bl.gB.end",
+    "Bl.sib.1.2",
 ]
 
 SUM_ONE = [
-    "comp.gout1", "Cl.g5.start", "Bl.g1.start", "comp.gout0", "Bl.g5.start", "Cl.g2.start", "Bl.g4.start",
-    "comp.gfc1", "A2.X.2", "Cl.g4.start", "Bl.g2.start", "Bl.g5.mid", "Bl.g3.start", "Cl.g3.start", "A1.X.2",
-    "Cl.g1.start", "Bl.g1.mid", "Bl.g4.mid", "Cl.g0.start", "Cl.g2.mid",
+    "comp.gout1", "comp.gout0", "Cl.gA.start", "Bl.gB.start", "Cl.gB.start", "Bl.gA.start", "comp.gfc1", "A1.X.2",
+    "A2.X.2",
 ]
 
 SUM_TWO = [
-    "Bl.g0.start", "Cl.g0.mid", "Bl.g2.mid", "Cl.g3.mid", "Cl.g4.mid",
+    "Bl.gB.mid", "Cl.gA.mid", "comp.gfc0", "Cl.gB.mid", "Bl.gA.mid",
 ]
 
 SUM_THREE = [
-    "A2.X.1", "Bl.g3.mid", "Cl.g3.end", "Cl.g5.mid", "Bl.g1.end", "Cl.g2.end", "Bl.g0.mid", "Bl.g4.end",
-    "Cl.in0.start", "Cl.g1.mid", "comp.gatt1", "Ce.g5.start", "comp.gatt0", "Be.g5.start", "Ce.g1.start",
-    "Be.g1.start", "Bl.g5.end", "Be.g2.start", "Ce.g3.start", "Cl.g5.end", "Be.g3.start", "Ce.g4.start",
-    "Be.g4.start", "Ce.g0.start", "Ce.g5.mid", "Be.g0.start", "comp.gfc0", "Ce.g1.mid", "Bl.g2.end", "A2.XR.2",
-    "A1.X.1", "A2.X.0", "Be.g5.mid", "Be.g3.mid", "Ce.g3.mid", "Be.g4.mid", "Cl.g4.end", "Be.g1.mid", "Ce.g4.mid",
-    "Ce.g2.start", "Bl.g3.end", "comp.first", "small.7", "A2.g3.start", "Ce.g5.end", "Ce.g3.end", "Cl.g0.end",
-    "Bl.in1.start", "Bl.in0.start", "Ce.g0.mid", "Be.g5.end", "Cl.in1.start", "A2.g2.start", "A2.XR.1", "Cl.g1.end",
-    "A1.XR.2", "Bl.g0.end", "Ce.in1.start", "small.8", "Ce.g4.end", "A2.g0.start", "A1.g0.start", "A1.g2.start",
-    "Ce.g2.mid", "Be.g2.mid", "Ce.in1.mid", "Be.g4.end", "A2.g3.mid", "Be.g3.end", "Ce.in0.start", "Cl.in0.mid",
-    "Be.in1.start", "Ce.g1.end", "Be.in0.start", "A1.XR.1", "small.9", "Bl.in0.mid", "A1.X.0", "Bl.in1.mid",
-    "A1.g3.start", "Cl.in1.mid", "Be.g0.mid", "A1.g2.mid", "Be.g1.end", "Ce.g2.end", "A2.g2.mid", "Be.g2.end",
-    "A1.g3.mid", "A2.XR.0", "Bl.in0.end", "Cl.in0.end", "Ce.in1.end", "small.10", "Ce.in0.mid", "Ce.g0.end",
-    "A2.g3.end", "Cl.in1.end", "A2.in0.start", "Be.in1.mid", "Be.in0.mid", "Ce.x.s", "Cl.x.s", "A1.XR.0", "A1.g3.end",
-    "A1.in0.start", "Bl.in1.end", "Bl.x.s", "A1.g0.mid", "A2.g0.mid", "small.11", "Be.in1.end", "A2.g2.end", "Be.x.s",
-    "Be.g0.end", "A2.in0.mid", "A1.g2.end", "A1.in0.mid", "Cl.x.r", "A1.g0.end", "Be.in0.end", "A2.g0.end",
-    "Ce.in0.end", "Ce.x.r", "Bl.x.r", "Be.x.r", "A2.in0.end", "A1.in0.end",
+    "A2.X.1", "Bl.gB.end", "comp.gatt1", "A1.X.1", "Ce.gB.start", "comp.gatt0", "Be.gB.start", "Ce.gA.start",
+    "Be.gA.start", "Cl.gB.end", "Ce.gB.mid", "Be.gB.mid", "Cl.in1.start", "Bl.gA.end", "A2.XR.2", "Bl.in1.start",
+    "A1.XR.2", "A1.gA.start", "A1.X.0", "Bl.in0.start", "Be.gA.mid", "Be.gB.end", "Be.in1.start", "Ce.gB.end",
+    "Ce.in1.start", "A2.gA.start", "Cl.gA.end", "A2.XR.1", "Bl.in1.mid", "A2.X.0", "Cl.in1.mid", "Cl.in0.start",
+    "Ce.gA.mid", "Be.gA.end", "A1.XR.1", "A1.gA.mid", "Ce.in1.mid", "comp.first", "small.7", "A2.gA.mid",
+    "Be.in0.start", "Be.in1.mid", "A1.XR.0", "Ce.in1.end", "Ce.x.s", "small.8", "Bl.in0.mid", "Ce.gA.end",
+    "Bl.in1.end", "Cl.in1.end", "Ce.in0.start", "A1.gA.end", "A1.in0.start", "small.9", "Cl.in0.mid", "Bl.x.s",
+    "Cl.x.s", "A2.XR.0", "A2.gA.end", "A2.in0.start", "Be.in1.end", "small.10", "Ce.in0.mid", "Be.x.s", "Be.in0.mid",
+    "A1.in0.mid", "A2.in0.mid", "Bl.in0.end", "Cl.in0.end", "small.11", "Be.in0.end", "Ce.in0.end", "Be.x.r",
+    "Bl.x.r", "Cl.x.r", "A1.in0.end", "Ce.x.r", "A2.in0.end",
 ]
 
 
@@ -93,7 +88,7 @@
 def kernel(
     seg_ref, gains_ref, bias_ref, tok_ref, qkv_ref, proj_ref, fc_ref, wout_ref, cot_ref,
     act_hbm, grad_hbm, ggain_hbm, gbias_hbm, gqkv_hbm, gproj_hbm, gfc_hbm, gwout_hbm,
-    w, rbuf, act_out, grad_out, gsum, ggain_out, gbias_out, tokv, cotv,
+    w, rbuf, act_out, grad_out, gsum, ggain_out, gbias_out, tokv, cotv, segs,
     xin, x1, x2, x3, x4, qkv, probs, xh1, xh2, rs1, rs2, dgel, gf, dpre, dbr, datt, dmix, dmid, mask, qbias,
     bf, sgb, sb_y, sb_c, sb_x, sbw, sr, sr_c, sr_x, sr_z, sr_y,
     s_out, s_fc, s_proj, s_qkv, t_out, t_fc, t_proj, t_qkv, hb, sems,
@@ -115,7 +110,9 @@
     zs = [at(x, zp[k], y, c) for k in range(4)]
     xp = at(ox, z, y, c)
     sib = at(x, z, y, oc)
-    other_section = (1 - sec, dp)
+    other_section = (1 - sec, ((lax.rem(x + c, 2) * 4 + z) * 4 + y) * 2 + c)
+    crossed = (sec == 1) & (c == 1)
+    rows_at = sec * c
 
     taken = [0, 0]
 
@@ -123,9 +120,9 @@
         taken[0] += 1
         return sems.at[taken[0] - 1]
 
-    def arrivals(pieces):
-        taken[1] += pieces
-        return taken[1] - pieces
+    def arrivals(slabs):
+        taken[1] += slabs
+        return taken[1] - slabs
 
     own = w.at[x, z, y, c]
     own_sem, tok_sem, cot_sem = sem(), sem(), sem()
@@ -135,7 +132,7 @@
     for j in range(4):
         pltpu.make_async_copy(wout_ref.at[:, pl.ds(1024 * j, 1024)], own.at[8 + j], own_sem).start()
     tok_in = pltpu.make_async_copy(tok_ref, tokv, tok_sem)
-    cot_in = pltpu.make_async_copy(cot_ref, cotv, cot_sem)
+    cot_in = pltpu.make_async_copy(cot_ref, cotv.at[0], cot_sem)
     tok_in.start()
     cot_in.start()
     barrier = pltpu.get_barrier_semaphore()
@@ -177,6 +174,14 @@
     def axes(part):
         return (yp, zp, ys, zs) if INNER_IS_Y[part] else (zp, yp, zs, ys)
 
+    def line(part, xx, o, half=None, summing=False):
+        core, base = c, FIRST[part]
+        if summing:
+            core, base = (oc if SUM_AT[part][0] else c), SUM_AT[part][1]
+        inner = slice(None) if half is None else pl.ds(2 * half, 2)
+        pz, py = (o, inner) if INNER_IS_Y[part] else (inner, o)
+        return w.at[xx, pz, py, core, pl.ds(base, 2)]
+
     def rings_of(part, summing):
         ip, op, idev, odev = axes(part)
         found = {}
@@ -187,11 +192,19 @@
         def along_outer(xx, i):
             return lambda j, half=None: slab(part, xx, ip[i], op[j], half, summing)
 
+        def along_line(xx):
+            return lambda j, half=None: line(part, xx, op[j], half, summing)
+
         for other in (0, 1) if X_FIRST[part] else (0,):
-            found[f"in{other}"] = ([along_inner(ox if other else x)], idev[3], idev[1])
-        for g, (other, offsets) in enumerate(GROUPS):
+            found[f"in{other}"] = ([along_inner(ox if other else x)], 1, idev[3], idev[1])
+        for g in (SUM_GROUPS if summing else GATHER_GROUPS)[part]:
+            other, offsets = GROUPS[g]
             if X_FIRST[part] or not other:
-                found[f"g{g}"] = ([along_outer(ox if other else x, i) for i in offsets], odev[3], odev[1])
+                xx = ox if other else x
+                if len(offsets) == 4:
+                    found[g] = ([along_line(xx)], 4, odev[3], odev[1])
+                else:
+                    found[g] = ([along_outer(xx, i) for i in offsets], 1, odev[3], odev[1])
         return found
 
     def small(src, dst, sems_of, target):
@@ -202,12 +215,6 @@
     ag_sent = {part: (sem(), sem(), sem()) for part in PARTS}
     ag_x = {part: (sem(),) if X_FIRST[part] else (sem(), sem(), sem()) for part in PARTS}
     ag_sib = {part: sem() for part in PARTS}
-
-    def line(part, xx, o):
-        core, base = c, FIRST[part]
-        if INNER_IS_Y[part]:
-            return w.at[xx, o, :, core, pl.ds(base, 2)]
-        return w.at[xx, :, o, core, pl.ds(base, 2)]
 
     def gather(step):
         part, name, *rest = step.split(".")
@@ -221,9 +228,10 @@
         elif name == "x":
             await_arrival(ag_x[part][0], 1)
         elif name == "X":
-            for i in GROUPS[int(rest[0])][1]:
-                for o in STAGES[int(rest[1])]:
-                    ref = slab(part, x, ip[i], op[o])
+            offsets = GROUPS[rest[0]][1]
+            for o in STAGES[int(rest[1])]:
+                whole = len(offsets) == 4
+                for ref in [line(part, x, op[o])] if whole else [slab(part, x, ip[i], op[o]) for i in offsets]:
                     remote(ref, ref, ag_sent[part][1], ag_x[part][int(rest[1])], xp).start()
         elif name == "XR":
             await_arrival(ag_x[part][int(rest[0])], 4 * len(STAGES[int(rest[0])]))
@@ -232,7 +240,8 @@
                 ref = line(part, ox if int(rest[0]) else x, op[o])
                 remote(ref, ref, ag_sent[part][2], ag_sib[part], sib).start()
         else:
-            views, left, right = ag_rings[part][name]
+            views, size, left, right = ag_rings[part][name]
+            count = size * len(views)
             full, half = ag_sem[part, name]
             sent = ag_sent[part][0]
             if rest[0] == "start":
@@ -240,12 +249,12 @@
                     remote(view(0), view(0), sent, full, right).start()
                     remote(view(0), view(0), sent, full, left).start()
             elif rest[0] == "mid":
-                await_arrival(full, 2 * len(views))
+                await_arrival(full, 2 * count)
                 for view in views:
                     remote(view(3, 0), view(3, 0), sent, half, right).start()
                     remote(view(1, 1), view(1, 1), sent, half, left).start()
             else:
-                await_arrival(half, len(views))
+                await_arrival(half, count)
 
     spread = (
         lax.broadcasted_iota(jnp.int32, (16, 128), 1)
@@ -253,7 +262,19 @@
     ).astype(F32)
     sm_y, sm_c, sm_z, sm_x = [(sem(), sem()) for _ in range(4)]
 
+    cross = [(sem(), sem()) for _ in range(4)]
+    seg_cross = remote(segs.at[0], segs.at[1], *cross[0], xp)
+    cot_cross = remote(cotv.at[0], cotv.at[1], *cross[1], xp)
+    act_cross = remote(act_out, act_hbm, *cross[2], xp)
+    grad_cross = remote(grad_out, grad_hbm, *cross[3], xp)
+
     def small_one():
+        segs[0] = jnp.broadcast_to(seg_ref[...].astype(F32), (8, ROWS))
+
+        @pl.when(crossed)
+        def _():
+            seg_cross.start()
+
         sgb[...] = jnp.zeros_like(sgb)
         sgb[0:2, :] = gains_ref[...].astype(F32)
         sgb[2:12, :] = bias_ref[...].astype(F32)
@@ -290,7 +311,11 @@
         return bf[k : k + 1, :]
 
     def small_six():
-        seg = jnp.broadcast_to(seg_ref[...].astype(F32), (ROWS, ROWS))
+        @pl.when(crossed)
+        def _():
+            seg_cross.wait()
+
+        seg = jnp.broadcast_to(segs[rows_at][0:1], (ROWS, ROWS))
         qi = lax.broadcasted_iota(jnp.int32, (ROWS, ROWS), 0)
         ki = lax.broadcasted_iota(jnp.int32, (ROWS, ROWS), 1)
         allowed = (seg == seg.T) & (ki <= qi) & (lax.div(qi, 64) == lax.div(ki, 64))
@@ -301,9 +326,9 @@
     for step in GATHER_ONE:
         gather(step)
 
-    handed = (sem(), sem())
-    handed_on = remote(act_out, hb, *handed, other_section)
-    handed_back = remote(grad_out, hb, *handed, other_section)
+    halves = [pl.ds(0, 512), pl.ds(512, 512)]
+    handed_on = [remote(act_out.at[:, k], hb.at[:, k], sem(), sem(), other_section) for k in halves]
+    handed_back = remote(grad_out, hb, sem(), sem(), other_section)
     tok_in.wait()
     cot_in.wait()
 
@@ -315,7 +340,13 @@
     def _():
         for step in GATHER_TWO:
             gather(step)
-        handed_on.wait_recv()
+
+        @pl.when(crossed)
+        def _():
+            cot_cross.start()
+
+        for cp in handed_on:
+            cp.wait_recv()
         xin[...] = hb[...].astype(F32)
 
     def norm(values, gain, shift):
@@ -410,17 +441,30 @@
     def wout_weights(j):
         return w[:, :, :, :, 8 + j].reshape(WIDTH, WIDTH)
 
-    result = xin[...] + row(11)
-    for j in range(4):
-        result = result + lax.dot_general(x4[0, j], wout_weights(j), NT, preferred_element_type=F32)
-    act_out[...] = result.astype(BF16)
-
-    @pl.when(sec == 0)
-    def _():
-        handed_on.start()
+    def hand_on(n):
+        @pl.when(sec == 0)
+        def _():
+            handed_on[n].start()
+
+    for n in range(2):
+        cols = slice(512 * n, 512 * (n + 1))
+        result = xin[:, cols] + row(11)[:, cols]
+        for j in range(4):
+            half = w[n, :, :, :, 8 + j].reshape(512, WIDTH)
+            result = result + lax.dot_general(x4[0, j], half, NT, preferred_element_type=F32)
+        act_out[:, cols] = result.astype(BF16)
+        hand_on(n)
 
     act_done = pltpu.make_async_copy(act_out, act_hbm, tok_sem)
-    act_done.start()
+    grad_done = pltpu.make_async_copy(grad_out, grad_hbm, cot_sem)
+
+    @pl.when(crossed)
+    def _():
+        act_cross.start()
+
+    @pl.when(~crossed)
+    def _():
+        act_done.start()
 
     for part in PARTS:
         await_sent(ag_sent[part][0], 30 if X_FIRST[part] else 15)
@@ -439,7 +483,11 @@
 
     @pl.when(sec == 1)
     def _():
-        gf[...] = cotv[...]
+        @pl.when(crossed)
+        def _():
+            cot_cross.wait()
+
+        gf[...] = cotv[rows_at]
 
     def column_sum(values):
         return jnp.sum(values.astype(F32), axis=0, keepdims=True)
@@ -517,10 +565,18 @@
     rs_sem = {(part, name): (sem(), sem()) for part in PARTS for name in rs_rings[part]}
     rs_sent = {part: (sem(), sem()) for part in PARTS}
     rs_x = {part: (sem(),) if X_FIRST[part] else (sem(), sem(), sem()) for part in PARTS}
-    rs_at = {(part, name): arrivals(6 * len(rs_rings[part][name][0])) for part in PARTS for name in rs_rings[part]}
-    rs_x_at = {part: arrivals(2 if X_FIRST[part] else 32) for part in PARTS}
+    rs_at = {
+        (part, name): arrivals(3 * rs_rings[part][name][1] * len(rs_rings[part][name][0]))
+        for part in PARTS
+        for name in rs_rings[part]
+    }
+    rs_x_at = {part: arrivals(1 if X_FIRST[part] else 16) for part in PARTS}
 
     def add(view, *terms, out=None):
+        if len(view.shape) > 3:
+            for k in range(view.shape[0]):
+                add(view.at[k], *(term.at[k] for term in terms))
+            return
         total = view[...].astype(F32)
         for term in terms:
             total = total + term[...].astype(F32)
@@ -542,47 +598,51 @@
             return
         ip, op, _, _ = axes(part)
         if name == "x" and rest[0] == "s":
-            buf = rbuf.at[pl.ds(rs_x_at[part], 2)]
+            buf = rbuf.at[rs_x_at[part]]
             remote(slab(part, ox, ip[0], op[0], None, True), buf, rs_sent[part][1], rs_x[part][0], xp).start()
         elif name == "x":
             await_arrival(rs_x[part][0], 1)
-            add(slab(part, x, ip[0], op[0], None, True), rbuf.at[pl.ds(rs_x_at[part], 2)], out=own_sum(part))
+            add(slab(part, x, ip[0], op[0], None, True), rbuf.at[rs_x_at[part]], out=own_sum(part))
         elif name in ("X", "XR"):
             stage = int(rest[0])
             if name == "XR":
                 await_arrival(rs_x[part][stage], 4 * len(STAGES[stage]))
             for o in STAGES[stage]:
-                for i in range(4):
-                    buf = rbuf.at[pl.ds(rs_x_at[part] + (o * 4 + i) * 2, 2)]
-                    if name == "X":
-                        ref = slab(part, ox, ip[i], op[o], None, True)
-                        remote(ref, buf, rs_sent[part][1], rs_x[part][stage], xp).start()
-                    else:
-                        add(slab(part, x, ip[i], op[o], None, True), buf)
+                buf = rbuf.at[pl.ds(rs_x_at[part] + 4 * o, 4)]
+                if name == "X":
+                    ref = line(part, ox, op[o], None, True)
+                    remote(ref, buf, rs_sent[part][1], rs_x[part][stage], xp).start()
+                else:
+                    add(line(part, x, op[o], None, True), buf)
         else:
-            views, left, right = rs_rings[part][name]
+            views, size, left, right = rs_rings[part][name]
+            count = size * len(views)
             half, full = rs_sem[part, name]
             sent = rs_sent[part][0]
 
-            def buf(k, offset, size):
-                return rbuf.at[pl.ds(rs_at[part, name] + 6 * k + offset, size)]
+            def arrived(k):
+                base = rs_at[part, name] + 3 * size * k
+                if size == 1:
+                    halves = [rbuf.at[base, pl.ds(0, 1)], rbuf.at[base, pl.ds(1, 1)]]
+                    return halves + [rbuf.at[base + 1], rbuf.at[base + 2]]
+                return [rbuf.at[pl.ds(base, 2)], rbuf.at[pl.ds(base + 2, 2)], rbuf.at[pl.ds(base + 4, 4)], rbuf.at[pl.ds(base + 8, 4)]]
 
             if rest[0] == "start":
                 for k, view in enumerate(views):
-                    remote(view(2, 0), buf(k, 0, 1), sent, half, right).start()
-                    remote(view(2, 1), buf(k, 1, 1), sent, half, left).start()
+                    remote(view(2, 0), arrived(k)[0], sent, half, right).start()
+                    remote(view(2, 1), arrived(k)[1], sent, half, left).start()
             elif rest[0] == "mid":
-                await_arrival(half, len(views))
+                await_arrival(half, count)
                 for k, view in enumerate(views):
-                    add(view(1, 0), buf(k, 0, 1))
-                    remote(view(1), buf(k, 2, 2), sent, full, right).start()
-                    add(view(3, 1), buf(k, 1, 1))
-                    remote(view(3), buf(k, 4, 2), sent, full, left).start()
+                    add(view(1, 0), arrived(k)[0])
+                    remote(view(1), arrived(k)[2], sent, full, right).start()
+                    add(view(3, 1), arrived(k)[1])
+                    remote(view(3), arrived(k)[3], sent, full, left).start()
             else:
-                await_arrival(full, 2 * len(views))
+                await_arrival(full, 2 * count)
                 last = name == "in0" and not X_FIRST[part]
                 for k, view in enumerate(views):
-                    add(view(0), buf(k, 2, 2), buf(k, 4, 2), out=own_sum(part) if last else None)
+                    add(view(0), arrived(k)[2], arrived(k)[3], out=own_sum(part) if last else None)
 
     sm_core, sm_xs, sm_zs, sm_ys = [(sem(), sem()) for _ in range(4)]
 
@@ -681,7 +741,14 @@
         sbw[0:1, :] = column_sum(d_first * xh1[...])
         sbw[2:3, :] = column_sum(d_first)
         grad_out[...] = (dmid[...] + norm_back(d_first, xh1[...], rs1[...], row(0))).astype(BF16)
-        pltpu.make_async_copy(grad_out, grad_hbm, cot_sem).start()
+
+        @pl.when(crossed)
+        def _():
+            grad_cross.start()
+
+        @pl.when(~crossed)
+        def _():
+            grad_done.start()
 
     @pl.when(sec == 1)
     def _():
@@ -721,14 +788,23 @@
 
     @pl.when(sec == 0)
     def _():
-        handed_on.wait_send()
+        for cp in handed_on:
+            cp.wait_send()
 
     @pl.when(sec == 1)
     def _():
         handed_back.wait_send()
 
-    act_done.wait()
-    pltpu.make_async_copy(grad_out, grad_hbm, cot_sem).wait()
+    @pl.when(crossed)
+    def _():
+        act_cross.wait()
+        grad_cross.wait()
+
+    @pl.when(~crossed)
+    def _():
+        act_done.wait()
+        grad_done.wait()
+
     pltpu.make_async_copy(gsum, gsum, own_sem).wait()
     for cp in small_done:
         cp.wait()
@@ -736,8 +812,8 @@
         raise ValueError(taken)
 
 
-SEMAPHORES = 255
-ARRIVALS = 372
+SEMAPHORES = 195
+ARRIVALS = 186
 
 
 def move(*refs):
@@ -765,9 +841,9 @@
         return pltpu.VMEM(dims, dtype)
 
     scratch = [
-        v(2, 4, 4, 2, 12, 16, WIDTH), v(ARRIVALS, 16, WIDTH),
+        v(2, 4, 4, 2, 12, 16, WIDTH), v(ARRIVALS, 2, 16, WIDTH),
         v(ROWS, WIDTH), v(ROWS, WIDTH), v(12, 16, WIDTH, dtype=F32), v(2, 16, dtype=F32), v(10, 1, 16, dtype=F32),
-        v(ROWS, WIDTH), v(ROWS, WIDTH),
+        v(ROWS, WIDTH), v(2, ROWS, WIDTH), v(2, 8, ROWS, dtype=F32),
         v(ROWS, WIDTH, dtype=F32), v(2, ROWS, WIDTH), v(2, ROWS, WIDTH), v(2, ROWS, WIDTH), v(2, 4, ROWS, WIDTH),
         v(ROWS, 3 * WIDTH), v(16, ROWS, ROWS, dtype=F32), v(ROWS, WIDTH, dtype=F32), v(ROWS, WIDTH, dtype=F32),
         v(ROWS, 1, dtype=F32), v(ROWS, 1, dtype=F32), v(4, ROWS, WIDTH, dtype=F32), v(ROWS, WIDTH),

time: 177 us -> 168 us (0.949)
  Pallas kernels: 176 us -> 167 us
    pallas_call x1, Pallas kernels: 174 us -> 165 us  [local(): pl.pallas_call(kernel, out_shape=results, in_specs=[vmem, vmem, vmem] + [...]
where the time goes in v4:
time: 168 us
  Pallas kernels  167 us (99%)
    pallas_call x1, Pallas kernels, local(): pl.pallas_call(kernel, out_shape=results, in_specs=[vmem, vmem, vmem] + [...  165 us

profile of v4, /device:TPU:0, one launch (start us, length us, event | category | flops | bytes accessed | tf_op | source)
XLA Modules:
  0.0 167.5 jit_solution(742420630998730621)
XLA Ops:
  0.6 164.6 %relay.1 = (bf16[128,1024]{1,0:T(8,128)(2,1)}, bf16[128,1024]{1,0:T(8,128)(2,1)}, f32[2,16]{1,0:T(2,128)}, f32[10,1,16]{2,1,0:T(1,128)}, f32[3,16,1024]{2,1,0:T(...) custom-call(s32[1,128]{1,0:T(1,128)} %bitcast.48, bf16[2,16]{1,0:T(2,128)(2,1)} %bitcast.49, ...), custom_call_target="tpu_custom_call" | custom-call | tf_op jit(solution)/shard_map/relay/pallas_call | solution.py:864
  165.2 2.1 %move.1 = (bf16[128,1024]{1,0:T(8,128)(2,1)}, bf16[128,1024]{1,0:T(8,128)(2,1)}, f32[2,16]{1,0:T(2,128)}, f32[10,1,16]{2,1,0:T(1,128)}, f32[3,16,1024]{2,1,0:T(8...) custom-call(bf16[128,1024]{1,0:T(8,128)(2,1)} %get-tuple-element.24.refs_0_, ...), custom_call_target="tpu_custom_call" | custom-call | tf_op jit(solution)/shard_map/move/pallas_call | solution.py:885

commit v5 on v4

--- a/solution.py
+++ b/solution.py
@@ -91,7 +91,7 @@
     w, rbuf, act_out, grad_out, gsum, ggain_out, gbias_out, tokv, cotv, segs,
     xin, x1, x2, x3, x4, qkv, probs, xh1, xh2, rs1, rs2, dgel, gf, dpre, dbr, datt, dmix, dmid, mask, qbias,
     bf, sgb, sb_y, sb_c, sb_x, sbw, sr, sr_c, sr_x, sr_z, sr_y,
-    s_out, s_fc, s_proj, s_qkv, t_out, t_fc, t_proj, t_qkv, hb, sems,
+    s_out, s_fc, s_proj, s_qkv, t_out, t_fc, t_proj, t_qkv, hb, turned, room, sems,
 ):
     sec = lax.axis_index("section")
     dp = lax.axis_index("dp")
@@ -124,6 +124,10 @@
         taken[1] += slabs
         return taken[1] - slabs
 
+    barrier = pltpu.get_barrier_semaphore()
+    partners = ys[1:] + zs[1:] + [xp, sib, other_section]
+    for target in partners:
+        pl.semaphore_signal(barrier, 1, device_id=target, device_id_type=MESH)
     own = w.at[x, z, y, c]
     own_sem, tok_sem, cot_sem = sem(), sem(), sem()
     pltpu.make_async_copy(qkv_ref, own.at[pl.ds(0, 3)], own_sem).start()
@@ -135,10 +139,6 @@
     cot_in = pltpu.make_async_copy(cot_ref, cotv.at[0], cot_sem)
     tok_in.start()
     cot_in.start()
-    barrier = pltpu.get_barrier_semaphore()
-    partners = ys[1:] + zs[1:] + [xp, sib, other_section]
-    for target in partners:
-        pl.semaphore_signal(barrier, 1, device_id=target, device_id_type=MESH)
     pl.semaphore_wait(barrier, len(partners))
     pltpu.make_async_copy(own, own, own_sem).wait()
 
@@ -326,6 +326,15 @@
     for step in GATHER_ONE:
         gather(step)
 
+    def from_sibling(part):
+        await_arrival(ag_sib[part], 32)
+
+    def fc_weights(j):
+        return w[j // 2, 2 * (j % 2) : 2 * (j % 2) + 2, :, :, 4:8].reshape(WIDTH, WIDTH)
+
+    def wout_weights(j):
+        return w[:, :, :, :, 8 + j].reshape(WIDTH, WIDTH)
+
     halves = [pl.ds(0, 512), pl.ds(512, 512)]
     handed_on = [remote(act_out.at[:, k], hb.at[:, k], sem(), sem(), other_section) for k in halves]
     handed_back = remote(grad_out, hb, sem(), sem(), other_section)
@@ -345,6 +354,13 @@
         def _():
             cot_cross.start()
 
+        for part in PARTS:
+            from_sibling(part)
+        for j in range(4):
+            rbuf[32 * j : 32 * j + 32] = wout_weights(j).T.reshape(32, 2, 16, WIDTH)
+        rbuf[128:160] = fc_weights(0).T.reshape(32, 2, 16, WIDTH)
+        for j in range(1, 4):
+            turned[j - 1] = fc_weights(j).T
         for cp in handed_on:
             cp.wait_recv()
         xin[...] = hb[...].astype(F32)
@@ -360,14 +376,14 @@
     def exchange(slot, src, dst):
         return remote(src, dst, *ex_sems[slot], sib)
 
-    def from_sibling(part):
-        await_arrival(ag_sib[part], 32)
-
     xh1[...], rs1[...], x1[0] = norm(xin[...], row(0), row(2))
     ex_first = exchange(0, x1.at[0], x1.at[1])
     ex_first.start()
-    from_sibling("Be")
-    from_sibling("Ce")
+
+    @pl.when(sec == 0)
+    def _():
+        from_sibling("Be")
+        from_sibling("Ce")
 
     def qkv_weights(k):
         return w[k, :, :, :, 0:3].reshape(1536, WIDTH)
@@ -415,45 +431,50 @@
     ex_second = exchange(2, x3.at[0], x3.at[1])
     ex_second.start()
 
-    @pl.when(sec == 0)
-    def _():
-        for step in GATHER_TWO:
-            gather(step)
-
-    from_sibling("A1")
-    from_sibling("A2")
-
-    def fc_weights(j):
-        return w[j // 2, 2 * (j % 2) : 2 * (j % 2) + 2, :, :, 4:8].reshape(WIDTH, WIDTH)
-
-    for j in range(4):
-        pre = lax.dot_general(x3[0], fc_weights(j), NT, preferred_element_type=F32) + row(7 + j)
+    def up(j, pre):
+        pre = pre + row(7 + j)
         square = pre * pre
         t = jnp.tanh(GC * (pre + 0.044715 * (square * pre)))
         half = 0.5 * (1.0 + t)
         x4[0, j] = (pre * half).astype(BF16)
         dgel[j] = half + (0.5 * GC) * pre * (1.0 - t * t) * (1.0 + 0.134145 * square)
+
     ex_act = exchange(3, x4.at[0], x4.at[1])
-    ex_act.start()
-    from_sibling("Bl")
-    from_sibling("Cl")
-
-    def wout_weights(j):
-        return w[:, :, :, :, 8 + j].reshape(WIDTH, WIDTH)
-
-    def hand_on(n):
-        @pl.when(sec == 0)
-        def _():
+
+    @pl.when(sec == 0)
+    def _():
+        for step in GATHER_TWO:
+            gather(step)
+        from_sibling("A1")
+        from_sibling("A2")
+        for j in range(4):
+            up(j, lax.dot_general(x3[0], fc_weights(j), NT, preferred_element_type=F32))
+        ex_act.start()
+        from_sibling("Bl")
+        from_sibling("Cl")
+        for n in range(2):
+            cols = slice(512 * n, 512 * (n + 1))
+            result = xin[:, cols] + row(11)[:, cols]
+            for j in range(4):
+                half = w[n, :, :, :, 8 + j].reshape(512, WIDTH)
+                result = result + lax.dot_general(x4[0, j], half, NT, preferred_element_type=F32)
+            act_out[:, cols] = result.astype(BF16)
             handed_on[n].start()
 
-    for n in range(2):
-        cols = slice(512 * n, 512 * (n + 1))
-        result = xin[:, cols] + row(11)[:, cols]
+    @pl.when(sec == 1)
+    def _():
         for j in range(4):
-            half = w[n, :, :, :, 8 + j].reshape(512, WIDTH)
-            result = result + lax.dot_general(x4[0, j], half, NT, preferred_element_type=F32)
-        act_out[:, cols] = result.astype(BF16)
-        hand_on(n)
+            right = rbuf[128:160].reshape(WIDTH, WIDTH) if j == 0 else turned[j - 1]
+            up(j, jnp.dot(x3[0], right, preferred_element_type=F32))
+        ex_act.start()
+        result = xin[...] + row(11)
+        for j in range(4):
+            right = rbuf[32 * j : 32 * j + 32].reshape(WIDTH, WIDTH)
+            result = result + jnp.dot(x4[0, j], right, preferred_element_type=F32)
+        act_out[...] = result.astype(BF16)
+
+    for target in (ys[1], ys[3], zs[1], zs[3], xp):
+        pl.semaphore_signal(room, 1, device_id=target, device_id_type=MESH)
 
     act_done = pltpu.make_async_copy(act_out, act_hbm, tok_sem)
     grad_done = pltpu.make_async_copy(grad_out, grad_hbm, cot_sem)
@@ -585,6 +606,19 @@
         else:
             out[...] = total
 
+    def leave(part):
+        first = FIRST[part]
+        for piece in (first, first + 1):
+            if piece < 3:
+                target = gqkv_hbm.at[piece]
+            elif piece == 3:
+                target = gproj_hbm.at[0]
+            elif piece < 8:
+                target = gfc_hbm.at[piece - 4]
+            else:
+                target = gwout_hbm.at[:, pl.ds(1024 * (piece - 8), 1024)]
+            pltpu.make_async_copy(gsum.at[piece], target, own_sem).start()
+
     def own_sum(part):
         return gsum.at[pl.ds(FIRST[part], 2)]
 
@@ -603,6 +637,7 @@
         elif name == "x":
             await_arrival(rs_x[part][0], 1)
             add(slab(part, x, ip[0], op[0], None, True), rbuf.at[rs_x_at[part]], out=own_sum(part))
+            leave(part)
         elif name in ("X", "XR"):
             stage = int(rest[0])
             if name == "XR":
@@ -643,6 +678,8 @@
                 last = name == "in0" and not X_FIRST[part]
                 for k, view in enumerate(views):
                     add(view(0), arrived(k)[2], arrived(k)[3], out=own_sum(part) if last else None)
+                if last:
+                    leave(part)
 
     sm_core, sm_xs, sm_zs, sm_ys = [(sem(), sem()) for _ in range(4)]
 
@@ -678,6 +715,8 @@
             gbias_out[k] = picked[2 + k : 3 + k, :]
 
     small_steps.update({7: small_seven, 8: small_eight, 9: small_nine, 10: small_ten, 11: small_eleven})
+
+    pl.semaphore_wait(room, 5)
 
     @pl.when(sec == 0)
     def _():
@@ -760,15 +799,6 @@
     for step in SUM_THREE:
         summing(step)
 
-    done = [
-        pltpu.make_async_copy(gsum.at[pl.ds(0, 3)], gqkv_hbm, own_sem),
-        pltpu.make_async_copy(gsum.at[pl.ds(3, 1)], gproj_hbm, own_sem),
-        pltpu.make_async_copy(gsum.at[pl.ds(4, 4)], gfc_hbm, own_sem),
-    ] + [
-        pltpu.make_async_copy(gsum.at[8 + j], gwout_hbm.at[:, pl.ds(1024 * j, 1024)], own_sem) for j in range(4)
-    ]
-    for cp in done:
-        cp.start()
     small_done = [
         pltpu.make_async_copy(ggain_out, ggain_hbm, sem()),
         pltpu.make_async_copy(gbias_out, gbias_hbm, sem()),
@@ -854,8 +884,8 @@
         v(2, 4, 16, 128, dtype=F32), v(4, 16, 128, dtype=F32), v(3, 16, 128, dtype=F32), v(4, 16, 128, dtype=F32),
         v(2, 4, 4, 2, 1, 16, ROWS), v(2, 4, 4, 2, 4, 16, ROWS), v(2, 4, 4, 2, 1, 16, ROWS), v(2, 4, 4, 2, 3, 16, ROWS),
         v(2, 4, 4, 1, 16, ROWS), v(2, 4, 4, 4, 16, ROWS), v(2, 4, 4, 1, 16, ROWS), v(2, 4, 4, 3, 16, ROWS),
-        v(ROWS, WIDTH),
-        pltpu.SemaphoreType.DMA((SEMAPHORES,)),
+        v(ROWS, WIDTH), v(3, WIDTH, WIDTH),
+        pltpu.SemaphoreType.REGULAR, pltpu.SemaphoreType.DMA((SEMAPHORES,)),
     ]
     results = (
         shape(ROWS, WIDTH, dtype=BF16), shape(ROWS, WIDTH, dtype=BF16), shape(2, 16), shape(10, 1, 16),

time: 168 us -> 165 us (0.982)
  Pallas kernels: 167 us -> 164 us
    pallas_call x1, Pallas kernels: 165 us -> 162 us  [local(): pl.pallas_call(kernel, out_shape=results, in_specs=[vmem, vmem, vmem] + [...]
where the time goes in v5:
time: 165 us
  Pallas kernels  164 us (99%)
    pallas_call x1, Pallas kernels, local(): pl.pallas_call(kernel, out_shape=results, in_specs=[vmem, vmem, vmem] + [...  162 us

profile of v5, /device:TPU:0, one launch (start us, length us, event | category | flops | bytes accessed | tf_op | source)
XLA Modules:
  0.0 164.9 jit_solution(18054522865659071483)
XLA Ops:
  0.6 161.9 %relay.1 = (bf16[128,1024]{1,0:T(8,128)(2,1)}, bf16[128,1024]{1,0:T(8,128)(2,1)}, f32[2,16]{1,0:T(2,128)}, f32[10,1,16]{2,1,0:T(1,128)}, f32[3,16,1024]{2,1,0:T(...) custom-call(s32[1,128]{1,0:T(1,128)} %bitcast.48, bf16[2,16]{1,0:T(2,128)(2,1)} %bitcast.49, ...), custom_call_target="tpu_custom_call" | custom-call | tf_op jit(solution)/shard_map/relay/pallas_call | solution.py:894
  162.6 2.1 %move.1 = (bf16[128,1024]{1,0:T(8,128)(2,1)}, bf16[128,1024]{1,0:T(8,128)(2,1)}, f32[2,16]{1,0:T(2,128)}, f32[10,1,16]{2,1,0:T(1,128)}, f32[3,16,1024]{2,1,0:T(8...) custom-call(bf16[128,1024]{1,0:T(8,128)(2,1)} %get-tuple-element.24.refs_0_, ...), custom_call_target="tpu_custom_call" | custom-call | tf_op jit(solution)/shard_map/move/pallas_call | solution.py:915

commit v6 on v5

--- a/solution.py
+++ b/solution.py
@@ -15,67 +15,80 @@
 GC = 0.7978845608028654
 NT = (((1,), (1,)), ((), ()))
 
-PARTS = ("Be", "Ce", "A1", "A2", "Bl", "Cl")
-FIRST = {"Be": 0, "Ce": 2, "A1": 4, "A2": 6, "Bl": 8, "Cl": 10}
-INNER_IS_Y = {"Be": False, "Ce": True, "A1": True, "A2": False, "Bl": False, "Cl": True}
-X_FIRST = {"Be": True, "Ce": True, "A1": False, "A2": False, "Bl": True, "Cl": True}
+PARTS = ("Be", "Ce", "A1", "Bm", "Cm", "A2", "Bl", "Cl")
+FIRST = {"Be": 0, "Ce": 2, "A1": 4, "Bm": 6, "Cm": 7, "A2": 8, "Bl": 10, "Cl": 11}
+SIZE = {"Be": 2, "Ce": 2, "A1": 2, "Bm": 1, "Cm": 1, "A2": 2, "Bl": 1, "Cl": 1}
+INNER_IS_Y = {part: part[0] == "C" or part == "A1" for part in PARTS}
+X_FIRST = {part: part[0] != "A" for part in PARTS}
 GROUPS = {
     "g0": (0, (0,)), "g1": (1, (0,)), "g2": (0, (1, 3)), "g3": (0, (2,)), "g4": (1, (1, 3)), "g5": (1, (2,)),
     "gA": (0, (0, 1, 2, 3)), "gB": (1, (0, 1, 2, 3)),
 }
 FINE = ("g0", "g1", "g2", "g3", "g4", "g5")
 COARSE = ("gA", "gB")
-GATHER_GROUPS = {"Be": COARSE, "Ce": COARSE, "A1": FINE, "A2": FINE, "Bl": COARSE, "Cl": COARSE}
-SUM_GROUPS = {"Be": COARSE, "Ce": COARSE, "A1": COARSE, "A2": COARSE, "Bl": COARSE, "Cl": COARSE}
+GATHER_GROUPS = {"Be": COARSE, "Ce": COARSE, "A1": FINE, "Bm": COARSE, "Cm": COARSE, "A2": FINE, "Bl": COARSE, "Cl": COARSE}
+SUM_GROUPS = {"Be": COARSE, "Ce": COARSE, "A1": COARSE, "Bm": COARSE, "Cm": COARSE, "A2": COARSE, "Bl": COARSE, "Cl": COARSE}
 STAGES = ((0,), (1, 3), (2,))
-SUM_AT = {"Be": (0, 4), "Ce": (0, 6), "A1": (0, 8), "A2": (0, 10), "Bl": (1, 8), "Cl": (1, 10)}
+SUM_AT = {part: (0, FIRST[part] + 4) if FIRST[part] < 8 else (1, FIRST[part]) for part in PARTS}
+BESIDE = {"Bm": 0, "Cm": 1, "Bl": 0, "Cl": 1}
 
 GATHER_ONE = [
-    "Ce.x.s", "A2.in0.start", "A1.in0.start", "A2.g0.start", "A2.X.g0.0", "Be.in0.start", "Bl.in0.start",
-    "Ce.in0.start", "A1.g0.start", "Cl.x.s", "Cl.in0.start", "A1.in0.mid", "Ce.x.r", "Bl.x.s", "small.1", "Be.x.s",
-    "A2.g0.mid", "Be.in0.mid", "A2.in0.mid", "A1.g2.start", "A2.X.g2.0", "Ce.in1.start", "A2.g2.start", "A2.X.g0.1",
-    "A1.in0.end", "Be.in0.end", "Bl.x.r", "Ce.in0.mid", "A1.sib.0.0", "Be.x.r", "Be.in1.start", "A1.g3.start",
-    "Bl.in1.start", "Ce.in1.mid", "A1.X.g2.0", "Cl.x.r", "Bl.in0.mid", "Be.gA.start", "Ce.in0.end", "A1.g0.mid",
-    "Be.in1.mid", "A1.X.g3.0", "small.2", "A1.g3.mid", "A2.in0.end", "A2.X.g3.0", "A2.g3.start", "Ce.in1.end",
-    "Ce.gA.start", "A1.g0.end", "A1.X.g0.0", "A2.sib.0.0", "Bl.in1.mid", "Cl.in1.start", "Be.in1.end", "Cl.in0.mid",
-    "Be.gB.start", "A1.g2.mid", "A1.g3.end", "A1.X.g2.1", "A1.X.g0.1", "Ce.gB.start", "A2.g3.mid", "small.3",
-    "A1.XR.0", "Be.sib.1.0", "A2.XR.0", "Be.gA.mid", "Be.sib.0.0", "A1.X.g3.1", "A2.g2.mid", "Ce.sib.0.0",
-    "A1.X.g3.2", "Cl.in0.end", "Bl.in0.end", "A2.X.g3.1", "A2.sib.0.1", "Bl.sib.0.0", "A1.sib.1.0", "Cl.in1.mid",
-    "Be.gB.mid", "Ce.gA.mid", "Be.sib.0.1", "A1.sib.0.1", "Ce.gB.mid", "small.4", "A2.X.g2.1", "A2.g2.end",
-    "A1.X.g0.2", "Bl.in1.end", "Ce.sib.1.0", "Be.sib.1.1", "Ce.sib.1.1", "Ce.sib.0.1", "Cl.gA.start", "A2.g3.end",
-    "Bl.gA.start", "A1.XR.1", "Ce.gA.end", "Ce.gB.end", "A1.g2.end", "Be.gA.end", "Be.gB.end", "A1.X.g2.2",
-    "A2.X.g2.2", "Ce.sib.0.2", "small.5", "Bl.gB.start", "Cl.in1.end", "Cl.sib.1.0", "A2.g0.end", "Be.sib.1.2",
-    "Cl.gB.start", "Ce.sib.1.2", "Cl.sib.0.0", "A2.X.g3.2", "Be.sib.0.2", "A2.sib.1.0", "A2.X.g0.2", "A1.sib.1.1",
-    "A2.XR.1", "Cl.gA.mid", "Bl.gA.mid", "Bl.sib.0.1", "A2.sib.0.2", "Bl.sib.1.0", "Cl.sib.0.1", "A2.sib.1.1",
-    "small.6",
+    "A2.in0.start", "A1.in0.start", "A2.X.g0.0", "Be.x.s", "Ce.in0.start", "A1.g0.start", "Be.in0.start",
+    "Bl.in0.start", "Cm.x.s", "A2.g0.start", "Bl.x.s", "Cl.x.s", "A1.in0.mid", "Cm.in0.start", "small.1",
+    "A2.in0.mid", "A2.g2.start", "A2.X.g2.0", "Be.x.r", "A1.g0.mid", "Be.in1.start", "A1.g2.start", "Ce.x.s",
+    "Cm.x.r", "Cl.in0.start", "A2.g0.mid", "Bm.x.s", "A1.X.g0.1", "Cl.x.r", "Cm.in0.mid", "A1.X.g2.0", "A2.in0.end",
+    "A2.g3.start", "Bm.in0.start", "Ce.in0.mid", "Be.in0.mid", "Bl.in0.mid", "Be.in1.mid", "Ce.x.r", "A2.g2.mid",
+    "Ce.in1.start", "A1.in0.end", "A1.g2.mid", "A1.g3.start", "A2.g0.end", "Be.in0.end", "Be.sib.0.0", "A2.X.g0.1",
+    "Cm.in0.end", "Cm.gA.start", "A1.X.g3.0", "A1.X.g0.0", "small.2", "Ce.in0.end", "Cl.in1.start", "Cm.in1.start",
+    "Be.gA.start", "Cl.in0.mid", "Bl.x.r", "Bm.x.r", "Bm.in0.mid", "A2.sib.0.0", "Bm.in1.start", "Be.in1.end",
+    "A2.X.g3.0", "Ce.gA.start", "A1.g3.mid", "A1.X.g2.1", "Cm.gA.mid", "A1.sib.0.1", "A1.sib.0.0", "Ce.in1.mid",
+    "Cm.in1.mid", "Be.gB.start", "Ce.in1.end", "Be.gA.mid", "Bm.in1.mid", "Ce.sib.1.0", "small.3", "Bl.in0.end",
+    "Bl.sib.0.0", "Be.sib.0.1", "A2.XR.0", "A1.X.g3.1", "A1.g2.end", "Ce.gB.start", "Ce.sib.0.0", "A2.g2.end",
+    "Be.sib.1.0", "Bm.in0.end", "A2.g3.mid", "A1.XR.0", "Cl.in0.end", "Cm.sib.0.0", "A2.sib.0.1", "Cm.gA.end",
+    "Ce.gA.mid", "Ce.sib.0.1", "A2.X.g2.1", "Bm.in1.end", "Be.gB.mid", "A1.g0.end", "A2.X.g3.1", "A1.g3.end",
+    "Cm.sib.0.1", "small.4", "A2.sib.1.0", "Cl.in1.mid", "Cm.in1.end", "A2.X.g0.2", "Bm.gB.start", "A1.XR.1",
+    "A1.sib.1.1", "Bm.gA.start", "Cl.sib.0.0", "Be.sib.1.1", "A1.sib.0.2", "A1.X.g2.2", "Bl.in1.start", "Ce.gB.mid",
+    "A1.X.g0.2", "Cm.sib.1.0", "A2.g3.end", "Ce.sib.1.1", "Cl.in1.end", "Bl.gA.start", "Bl.in1.mid", "A2.sib.0.2",
+    "Cm.gB.start", "Be.gB.end", "Be.sib.1.2", "small.5", "Cl.gA.start", "Ce.gA.end", "Ce.sib.0.2", "Be.gA.end",
+    "Be.sib.0.2", "A1.X.g3.2", "A1.sib.1.0", "Ce.gB.end", "Bl.in1.end", "Bl.gB.start", "Ce.sib.1.2", "Cm.sib.0.2",
+    "Bl.sib.1.0", "Bm.gB.mid", "A2.X.g2.2", "A2.XR.1", "Cl.sib.1.0", "Bm.sib.0.0", "A2.sib.1.1", "Cl.gB.start",
+    "Bm.gA.mid", "Bm.sib.1.0", "Bm.sib.1.1", "Bm.sib.0.1", "Cm.gB.mid", "Cm.sib.1.1", "small.6",
 ]
 
 GATHER_TWO = [
-    "Cl.gB.mid", "A1.sib.0.2", "Cl.sib.1.1", "Bl.gB.mid", "A1.XR.2", "A1.sib.1.2", "A2.XR.2", "Bl.gA.end",
-    "A2.sib.1.2", "Cl.gA.end", "Cl.sib.0.2", "Bl.sib.1.1", "Cl.gB.end", "Cl.sib.1.2", "Bl.sib.0.2", "Bl.gB.end",
-    "Bl.sib.1.2",
+    "A1.XR.2", "A1.sib.1.2", "Cl.gA.mid", "Bl.gB.mid", "Bl.sib.1.1", "A2.X.g3.2", "Cl.sib.0.1", "Cl.gB.mid",
+    "Bl.gA.mid", "Bl.sib.0.1", "Cm.gB.end", "Cm.sib.1.2", "Bm.gA.end", "Bm.gB.end", "Bm.sib.1.2", "Bm.sib.0.2",
+    "Cl.sib.1.1", "Bl.gB.end", "A2.XR.2", "A2.sib.1.2", "Cl.gA.end", "Cl.sib.0.2", "Bl.sib.1.2", "Cl.gB.end",
+    "Cl.sib.1.2", "Bl.gA.end", "Bl.sib.0.2",
 ]
 
+GATHER_THREE = [
+
+]
+
 SUM_ONE = [
-    "comp.gout1", "comp.gout0", "Cl.gA.start", "Bl.gB.start", "Cl.gB.start", "Bl.gA.start", "comp.gfc1", "A1.X.2",
-    "A2.X.2",
+    "comp.gout1", "A2.X.2", "Bl.gB.start", "Cl.gB.start", "comp.gout0", "Cl.gA.start", "Bl.gA.start", "comp.gfc1",
+    "Cm.gB.start", "Bm.gB.start", "Cl.gB.mid", "Bl.gB.mid", "A1.X.2",
 ]
 
 SUM_TWO = [
-    "Bl.gB.mid", "Cl.gA.mid", "comp.gfc0", "Cl.gB.mid", "Bl.gA.mid",
+    "Cl.gA.mid", "Bm.gB.mid",
 ]
 
 SUM_THREE = [
-    "A2.X.1", "Bl.gB.end", "comp.gatt1", "A1.X.1", "Ce.gB.start", "comp.gatt0", "Be.gB.start", "Ce.gA.start",
-    "Be.gA.start", "Cl.gB.end", "Ce.gB.mid", "Be.gB.mid", "Cl.in1.start", "Bl.gA.end", "A2.XR.2", "Bl.in1.start",
-    "A1.XR.2", "A1.gA.start", "A1.X.0", "Bl.in0.start", "Be.gA.mid", "Be.gB.end", "Be.in1.start", "Ce.gB.end",
-    "Ce.in1.start", "A2.gA.start", "Cl.gA.end", "A2.XR.1", "Bl.in1.mid", "A2.X.0", "Cl.in1.mid", "Cl.in0.start",
-    "Ce.gA.mid", "Be.gA.end", "A1.XR.1", "A1.gA.mid", "Ce.in1.mid", "comp.first", "small.7", "A2.gA.mid",
-    "Be.in0.start", "Be.in1.mid", "A1.XR.0", "Ce.in1.end", "Ce.x.s", "small.8", "Bl.in0.mid", "Ce.gA.end",
-    "Bl.in1.end", "Cl.in1.end", "Ce.in0.start", "A1.gA.end", "A1.in0.start", "small.9", "Cl.in0.mid", "Bl.x.s",
-    "Cl.x.s", "A2.XR.0", "A2.gA.end", "A2.in0.start", "Be.in1.end", "small.10", "Ce.in0.mid", "Be.x.s", "Be.in0.mid",
-    "A1.in0.mid", "A2.in0.mid", "Bl.in0.end", "Cl.in0.end", "small.11", "Be.in0.end", "Ce.in0.end", "Be.x.r",
-    "Bl.x.r", "Cl.x.r", "A1.in0.end", "Ce.x.r", "A2.in0.end",
+    "Cm.gB.mid", "Cl.gB.end", "Cl.in1.start", "A2.XR.2", "A2.gA.start", "A2.X.1", "comp.gfc0", "Cm.gA.start",
+    "Bm.gA.start", "comp.gatt1", "Ce.gB.start", "Cl.gA.end", "Cl.in1.mid", "Be.gB.start", "A1.X.1", "comp.gatt0",
+    "Cm.gB.end", "comp.first", "small.7", "Bm.gB.end", "Ce.gA.start", "Be.gA.start", "Cl.in1.end", "Ce.gB.mid",
+    "Be.gB.mid", "Bl.gA.mid", "A1.XR.2", "A1.X.0", "Ce.gA.mid", "A1.gA.start", "Ce.gB.end", "Bl.gB.end", "Be.gA.mid",
+    "Be.gB.end", "small.8", "Bl.gA.end", "Cm.gA.mid", "Cm.in1.start", "Ce.in1.start", "Bm.in1.start", "A2.X.0",
+    "Bm.gA.mid", "Bl.in1.start", "A1.XR.1", "A1.gA.mid", "Be.in1.start", "Be.gA.end", "Ce.gA.end", "A2.XR.1",
+    "A2.gA.mid", "A1.XR.0", "Cl.x.s", "small.9", "Bl.in0.start", "Bm.gA.end", "Bm.in1.mid", "Bl.in1.mid",
+    "Be.in0.start", "Cm.gA.end", "Cm.in0.start", "Ce.in0.start", "Cl.in0.start", "Cm.in1.mid", "A1.gA.end",
+    "A1.in0.start", "Ce.in1.mid", "Be.in1.mid", "Bm.in0.start", "A2.XR.0", "small.10", "A2.gA.end", "A2.in0.start",
+    "Bm.in1.end", "Bm.x.s", "Bl.in0.mid", "Bl.in1.end", "Ce.in0.mid", "Bl.x.s", "Cl.in0.mid", "Cm.in1.end", "Cm.x.s",
+    "Be.in0.mid", "Be.in1.end", "Be.x.s", "Cm.in0.mid", "Bm.in0.mid", "A1.in0.mid", "small.11", "Ce.in1.end",
+    "Ce.x.s", "A2.in0.mid", "Bl.in0.end", "Ce.in0.end", "Bl.x.r", "Bm.in0.end", "Cm.in0.end", "Be.in0.end", "Be.x.r",
+    "Bm.x.r", "Cm.x.r", "Cl.in0.end", "Cl.x.r", "Ce.x.r", "A2.in0.end", "A1.in0.end",
 ]
 
 
@@ -88,7 +101,7 @@
 def kernel(
     seg_ref, gains_ref, bias_ref, tok_ref, qkv_ref, proj_ref, fc_ref, wout_ref, cot_ref,
     act_hbm, grad_hbm, ggain_hbm, gbias_hbm, gqkv_hbm, gproj_hbm, gfc_hbm, gwout_hbm,
-    w, rbuf, act_out, grad_out, gsum, ggain_out, gbias_out, tokv, cotv, segs,
+    w, rbuf, act_out, grad_out, gsum, ggain_out, gbias_out, cotv, segs,
     xin, x1, x2, x3, x4, qkv, probs, xh1, xh2, rs1, rs2, dgel, gf, dpre, dbr, datt, dmix, dmid, mask, qbias,
     bf, sgb, sb_y, sb_c, sb_x, sbw, sr, sr_c, sr_x, sr_z, sr_y,
     s_out, s_fc, s_proj, s_qkv, t_out, t_fc, t_proj, t_qkv, hb, turned, room, sems,
@@ -135,7 +148,7 @@
     pltpu.make_async_copy(fc_ref, own.at[pl.ds(4, 4)], own_sem).start()
     for j in range(4):
         pltpu.make_async_copy(wout_ref.at[:, pl.ds(1024 * j, 1024)], own.at[8 + j], own_sem).start()
-    tok_in = pltpu.make_async_copy(tok_ref, tokv, tok_sem)
+    tok_in = pltpu.make_async_copy(tok_ref, datt, tok_sem)
     cot_in = pltpu.make_async_copy(cot_ref, cotv.at[0], cot_sem)
     tok_in.start()
     cot_in.start()
@@ -146,22 +159,20 @@
         core, base = c, FIRST[part]
         if summing:
             core, base = (oc if SUM_AT[part][0] else c), SUM_AT[part][1]
-        pieces = pl.ds(base, 2) if half is None else pl.ds(base + half, 1)
         pz, py = (o, i) if INNER_IS_Y[part] else (i, o)
-        return w.at[xx, pz, py, core, pieces]
-
-    def bytes_of(count):
-        two = pl.ds(0, 2)
-        return {
-            1: w.at[0, 0, 0, 0, two],
-            2: w.at[0, 0, two, 0, two],
-            4: w.at[0, 0, :, 0, two],
-            8: w.at[0, two, :, 0, two],
-            15: w.at[0, 0, pl.ds(0, 3), 0, pl.ds(0, 10)],
-            16: w.at[0, :, :, 0, two],
-            30: w.at[0, two, pl.ds(0, 3), 0, pl.ds(0, 10)],
-            32: w.at[:, :, :, 0, two],
-        }[count]
+        if half is None:
+            return w.at[xx, pz, py, core, pl.ds(base, SIZE[part])]
+        if SIZE[part] == 2:
+            return w.at[xx, pz, py, core, pl.ds(base + half, 1)]
+        return w.at[xx, pz, py, core, pl.ds(base, 1), :, pl.ds(512 * half, 512)]
+
+    def bytes_of(pieces):
+        for xs in (1, 2):
+            for a in (1, 2, 3, 4):
+                for b in (1, 2, 3, 4):
+                    k = pieces // (xs * a * b)
+                    if k <= 12 and xs * a * b * k == pieces:
+                        return w.at[pl.ds(0, xs), pl.ds(0, a), pl.ds(0, b), 0, pl.ds(0, k)]
 
     def await_arrival(which, count):
         ref = bytes_of(count)
@@ -180,7 +191,7 @@
             core, base = (oc if SUM_AT[part][0] else c), SUM_AT[part][1]
         inner = slice(None) if half is None else pl.ds(2 * half, 2)
         pz, py = (o, inner) if INNER_IS_Y[part] else (inner, o)
-        return w.at[xx, pz, py, core, pl.ds(base, 2)]
+        return w.at[xx, pz, py, core, pl.ds(base, SIZE[part])]
 
     def rings_of(part, summing):
         ip, op, idev, odev = axes(part)
@@ -226,7 +237,7 @@
             ref = slab(part, x, ip[0], op[0])
             remote(ref, ref, ag_sent[part][1], ag_x[part][0], xp).start()
         elif name == "x":
-            await_arrival(ag_x[part][0], 1)
+            await_arrival(ag_x[part][0], SIZE[part])
         elif name == "X":
             offsets = GROUPS[rest[0]][1]
             for o in STAGES[int(rest[1])]:
@@ -234,14 +245,14 @@
                 for ref in [line(part, x, op[o])] if whole else [slab(part, x, ip[i], op[o]) for i in offsets]:
                     remote(ref, ref, ag_sent[part][1], ag_x[part][int(rest[1])], xp).start()
         elif name == "XR":
-            await_arrival(ag_x[part][int(rest[0])], 4 * len(STAGES[int(rest[0])]))
+            await_arrival(ag_x[part][int(rest[0])], 4 * SIZE[part] * len(STAGES[int(rest[0])]))
         elif name == "sib":
             for o in STAGES[int(rest[1])]:
                 ref = line(part, ox if int(rest[0]) else x, op[o])
                 remote(ref, ref, ag_sent[part][2], ag_sib[part], sib).start()
         else:
             views, size, left, right = ag_rings[part][name]
-            count = size * len(views)
+            count = size * len(views) * SIZE[part]
             full, half = ag_sem[part, name]
             sent = ag_sent[part][0]
             if rest[0] == "start":
@@ -327,7 +338,7 @@
         gather(step)
 
     def from_sibling(part):
-        await_arrival(ag_sib[part], 32)
+        await_arrival(ag_sib[part], 32 * SIZE[part])
 
     def fc_weights(j):
         return w[j // 2, 2 * (j % 2) : 2 * (j % 2) + 2, :, :, 4:8].reshape(WIDTH, WIDTH)
@@ -343,11 +354,11 @@
 
     @pl.when(sec == 0)
     def _():
-        xin[...] = tokv[...].astype(F32)
+        xin[...] = datt[...].astype(F32)
 
     @pl.when(sec == 1)
     def _():
-        for step in GATHER_TWO:
+        for step in GATHER_TWO + GATHER_THREE:
             gather(step)
 
         @pl.when(crossed)
@@ -445,13 +456,15 @@
     def _():
         for step in GATHER_TWO:
             gather(step)
-        from_sibling("A1")
-        from_sibling("A2")
+        for part in ("A1", "Bm", "Cm"):
+            from_sibling(part)
         for j in range(4):
             up(j, lax.dot_general(x3[0], fc_weights(j), NT, preferred_element_type=F32))
         ex_act.start()
-        from_sibling("Bl")
-        from_sibling("Cl")
+        for step in GATHER_THREE:
+            gather(step)
+        for part in ("A2", "Bl", "Cl"):
+            from_sibling(part)
         for n in range(2):
             cols = slice(512 * n, 512 * (n + 1))
             result = xin[:, cols] + row(11)[:, cols]
@@ -488,9 +501,9 @@
         act_done.start()
 
     for part in PARTS:
-        await_sent(ag_sent[part][0], 30 if X_FIRST[part] else 15)
-        await_sent(ag_sent[part][1], 1 if X_FIRST[part] else 16)
-        await_sent(ag_sent[part][2], 32)
+        await_sent(ag_sent[part][0], (30 if X_FIRST[part] else 15) * SIZE[part])
+        await_sent(ag_sent[part][1], (1 if X_FIRST[part] else 16) * SIZE[part])
+        await_sent(ag_sent[part][2], 32 * SIZE[part])
     rows = sb_y.at[pl.ds(1, 3)]
     small(rows, rows, sm_y, sib).wait_send()
     small(sb_c.at[0], sb_c.at[1], sm_c, sib).wait_send()
@@ -586,12 +599,16 @@
     rs_sem = {(part, name): (sem(), sem()) for part in PARTS for name in rs_rings[part]}
     rs_sent = {part: (sem(), sem()) for part in PARTS}
     rs_x = {part: (sem(),) if X_FIRST[part] else (sem(), sem(), sem()) for part in PARTS}
-    rs_at = {
-        (part, name): arrivals(3 * rs_rings[part][name][1] * len(rs_rings[part][name][0]))
-        for part in PARTS
-        for name in rs_rings[part]
-    }
-    rs_x_at = {part: arrivals(1 if X_FIRST[part] else 16) for part in PARTS}
+    rs_at, rs_x_at = {}, {}
+    for part in PARTS:
+        twin = "B" + part[1]
+        for name, (views, size, _, _) in rs_rings[part].items():
+            rs_at[part, name] = rs_at[twin, name] if BESIDE.get(part) else arrivals(3 * size * len(views))
+        rs_x_at[part] = rs_x_at[twin] if BESIDE.get(part) else arrivals(1 if X_FIRST[part] else 16)
+
+    def room_for(part, base, count=None):
+        slabs = base if count is None else pl.ds(base, count)
+        return rbuf.at[slabs] if SIZE[part] == 2 else rbuf.at[slabs, pl.ds(BESIDE[part], 1)]
 
     def add(view, *terms, out=None):
         if len(view.shape) > 3:
@@ -608,7 +625,7 @@
 
     def leave(part):
         first = FIRST[part]
-        for piece in (first, first + 1):
+        for piece in range(first, first + SIZE[part]):
             if piece < 3:
                 target = gqkv_hbm.at[piece]
             elif piece == 3:
@@ -620,7 +637,7 @@
             pltpu.make_async_copy(gsum.at[piece], target, own_sem).start()
 
     def own_sum(part):
-        return gsum.at[pl.ds(FIRST[part], 2)]
+        return gsum.at[pl.ds(FIRST[part], SIZE[part])]
 
     def summing(step):
         part, name, *rest = step.split(".")
@@ -632,18 +649,18 @@
             return
         ip, op, _, _ = axes(part)
         if name == "x" and rest[0] == "s":
-            buf = rbuf.at[rs_x_at[part]]
+            buf = room_for(part, rs_x_at[part])
             remote(slab(part, ox, ip[0], op[0], None, True), buf, rs_sent[part][1], rs_x[part][0], xp).start()
         elif name == "x":
-            await_arrival(rs_x[part][0], 1)
-            add(slab(part, x, ip[0], op[0], None, True), rbuf.at[rs_x_at[part]], out=own_sum(part))
+            await_arrival(rs_x[part][0], SIZE[part])
+            add(slab(part, x, ip[0], op[0], None, True), room_for(part, rs_x_at[part]), out=own_sum(part))
             leave(part)
         elif name in ("X", "XR"):
             stage = int(rest[0])
             if name == "XR":
-                await_arrival(rs_x[part][stage], 4 * len(STAGES[stage]))
+                await_arrival(rs_x[part][stage], 4 * SIZE[part] * len(STAGES[stage]))
             for o in STAGES[stage]:
-                buf = rbuf.at[pl.ds(rs_x_at[part] + 4 * o, 4)]
+                buf = room_for(part, rs_x_at[part] + 4 * o, 4)
                 if name == "X":
                     ref = line(part, ox, op[o], None, True)
                     remote(ref, buf, rs_sent[part][1], rs_x[part][stage], xp).start()
@@ -651,16 +668,19 @@
                     add(line(part, x, op[o], None, True), buf)
         else:
             views, size, left, right = rs_rings[part][name]
-            count = size * len(views)
+            count = size * len(views) * SIZE[part]
             half, full = rs_sem[part, name]
             sent = rs_sent[part][0]
 
             def arrived(k):
                 base = rs_at[part, name] + 3 * size * k
                 if size == 1:
-                    halves = [rbuf.at[base, pl.ds(0, 1)], rbuf.at[base, pl.ds(1, 1)]]
-                    return halves + [rbuf.at[base + 1], rbuf.at[base + 2]]
-                return [rbuf.at[pl.ds(base, 2)], rbuf.at[pl.ds(base + 2, 2)], rbuf.at[pl.ds(base + 4, 4)], rbuf.at[pl.ds(base + 8, 4)]]
+                    fulls = [room_for(part, base + 1), room_for(part, base + 2)]
+                    if SIZE[part] == 2:
+                        return [rbuf.at[base, pl.ds(0, 1)], rbuf.at[base, pl.ds(1, 1)]] + fulls
+                    piece = pl.ds(BESIDE[part], 1)
+                    return [rbuf.at[base, piece, :, pl.ds(512 * k, 512)] for k in (0, 1)] + fulls
+                return [room_for(part, base + 2 * k, 2) for k in (0, 1)] + [room_for(part, base + 4 * k, 4) for k in (1, 2)]
 
             if rest[0] == "start":
                 for k, view in enumerate(views):
@@ -807,8 +827,8 @@
         cp.start()
 
     for part in PARTS:
-        await_sent(rs_sent[part][0], 30 if X_FIRST[part] else 15)
-        await_sent(rs_sent[part][1], 1 if X_FIRST[part] else 16)
+        await_sent(rs_sent[part][0], (30 if X_FIRST[part] else 15) * SIZE[part])
+        await_sent(rs_sent[part][1], (1 if X_FIRST[part] else 16) * SIZE[part])
     for cp in (ex_first, ex_att, ex_second, ex_act, ex_gf, ex_dpre, ex_dbr, ex_dmix):
         cp.wait_send()
     small(sr.at[ox], sr_x, sm_xs, xp).wait_send()
@@ -842,7 +862,7 @@
         raise ValueError(taken)
 
 
-SEMAPHORES = 195
+SEMAPHORES = 243
 ARRIVALS = 186
 
 
@@ -873,7 +893,7 @@
     scratch = [
         v(2, 4, 4, 2, 12, 16, WIDTH), v(ARRIVALS, 2, 16, WIDTH),
         v(ROWS, WIDTH), v(ROWS, WIDTH), v(12, 16, WIDTH, dtype=F32), v(2, 16, dtype=F32), v(10, 1, 16, dtype=F32),
-        v(ROWS, WIDTH), v(2, ROWS, WIDTH), v(2, 8, ROWS, dtype=F32),
+        v(2, ROWS, WIDTH), v(2, 8, ROWS, dtype=F32),
         v(ROWS, WIDTH, dtype=F32), v(2, ROWS, WIDTH), v(2, ROWS, WIDTH), v(2, ROWS, WIDTH), v(2, 4, ROWS, WIDTH),
         v(ROWS, 3 * WIDTH), v(16, ROWS, ROWS, dtype=F32), v(ROWS, WIDTH, dtype=F32), v(ROWS, WIDTH, dtype=F32),
         v(ROWS, 1, dtype=F32), v(ROWS, 1, dtype=F32), v(4, ROWS, WIDTH, dtype=F32), v(ROWS, WIDTH),
@@ -898,7 +918,7 @@
         out_specs=(hbm,) * 8,
         scratch_shapes=scratch,
         compiler_params=pltpu.CompilerParams(
-            collective_id=0, has_side_effects=True, vmem_limit_bytes=63 * 2**20
+            collective_id=0, has_side_effects=True, vmem_limit_bytes=127 * 2**19
         ),
         name="relay",
     )(

time: 165 us -> 163 us (0.988)
  Pallas kernels: 164 us -> 162 us
    pallas_call x1, Pallas kernels: 162 us -> 160 us  [local(): pl.pallas_call(kernel, out_shape=results, in_specs=[vmem, vmem, vmem] + [...]
where the time goes in v6:
time: 163 us
  Pallas kernels  162 us (99%)
    pallas_call x1, Pallas kernels, local(): pl.pallas_call(kernel, out_shape=results, in_specs=[vmem, vmem, vmem] + [...  160 us

profile of v6, /device:TPU:0, one launch (start us, length us, event | category | flops | bytes accessed | tf_op | source)
XLA Modules:
  0.0 162.9 jit_solution(9217176602124684521)
XLA Ops:
  0.6 159.9 %relay.1 = (bf16[128,1024]{1,0:T(8,128)(2,1)}, bf16[128,1024]{1,0:T(8,128)(2,1)}, f32[2,16]{1,0:T(2,128)}, f32[10,1,16]{2,1,0:T(1,128)}, f32[3,16,1024]{2,1,0:T(...) custom-call(s32[1,128]{1,0:T(1,128)} %bitcast.48, bf16[2,16]{1,0:T(2,128)(2,1)} %bitcast.49, ...), custom_call_target="tpu_custom_call" | custom-call | tf_op jit(solution)/shard_map/relay/pallas_call | solution.py:914
  160.5 2.1 %move.1 = (bf16[128,1024]{1,0:T(8,128)(2,1)}, bf16[128,1024]{1,0:T(8,128)(2,1)}, f32[2,16]{1,0:T(2,128)}, f32[10,1,16]{2,1,0:T(1,128)}, f32[3,16,1024]{2,1,0:T(8...) custom-call(bf16[128,1024]{1,0:T(8,128)(2,1)} %get-tuple-element.24.refs_0_, ...), custom_call_target="tpu_custom_call" | custom-call | tf_op jit(solution)/shard_map/move/pallas_call | solution.py:935

commit v7 on v6

--- a/solution.py
+++ b/solution.py
@@ -223,7 +223,8 @@
 
     ag_rings = {part: rings_of(part, False) for part in PARTS}
     ag_sem = {(part, name): (sem(), sem()) for part in PARTS for name in ag_rings[part]}
-    ag_sent = {part: (sem(), sem(), sem()) for part in PARTS}
+    ag_rings_sent, ag_x_sent, ag_sib_sent = (sem(), sem()), sem(), sem()
+    ag_sent = {part: (ag_rings_sent[X_FIRST[part]], ag_x_sent, ag_sib_sent) for part in PARTS}
     ag_x = {part: (sem(),) if X_FIRST[part] else (sem(), sem(), sem()) for part in PARTS}
     ag_sib = {part: sem() for part in PARTS}
 
@@ -500,10 +501,11 @@
     def _():
         act_done.start()
 
-    for part in PARTS:
-        await_sent(ag_sent[part][0], (30 if X_FIRST[part] else 15) * SIZE[part])
-        await_sent(ag_sent[part][1], (1 if X_FIRST[part] else 16) * SIZE[part])
-        await_sent(ag_sent[part][2], 32 * SIZE[part])
+    by_x = [sum(SIZE[part] for part in PARTS if X_FIRST[part] == first) for first in (False, True)]
+    await_sent(ag_rings_sent[0], 15 * by_x[0])
+    await_sent(ag_rings_sent[1], 30 * by_x[1])
+    await_sent(ag_x_sent, 16 * by_x[0] + by_x[1])
+    await_sent(ag_sib_sent, 32 * 12)
     rows = sb_y.at[pl.ds(1, 3)]
     small(rows, rows, sm_y, sib).wait_send()
     small(sb_c.at[0], sb_c.at[1], sm_c, sib).wait_send()
@@ -593,11 +595,15 @@
         elif name == "gatt0":
             grads_att(x)
         elif name == "first":
-            pl.when(sec == 0)(back_first)
+
+            @pl.when(sec == 0)
+            def _():
+                back_first(grad_done.start)
 
     rs_rings = {part: rings_of(part, True) for part in PARTS}
     rs_sem = {(part, name): (sem(), sem()) for part in PARTS for name in rs_rings[part]}
-    rs_sent = {part: (sem(), sem()) for part in PARTS}
+    rs_rings_sent, rs_x_sent = (sem(), sem()), sem()
+    rs_sent = {part: (rs_rings_sent[X_FIRST[part]], rs_x_sent) for part in PARTS}
     rs_x = {part: (sem(),) if X_FIRST[part] else (sem(), sem(), sem()) for part in PARTS}
     rs_at, rs_x_at = {}, {}
     for part in PARTS:
@@ -794,12 +800,19 @@
     sbw[3:4, :] = column_sum(dmix[:, 0:WIDTH])
     sbw[4:5, :] = column_sum(dmix[:, 2 * WIDTH :])
 
-    def back_first():
+    def back_first(then):
         d_first = jnp.dot(dmix[:, 0:1536], qkv_weights(0), preferred_element_type=F32)
         d_first = d_first + jnp.dot(dmix[:, 1536:], qkv_weights(1), preferred_element_type=F32)
+        grad_out[...] = (dmid[...] + norm_back(d_first, xh1[...], rs1[...], row(0))).astype(BF16)
+        then()
         sbw[0:1, :] = column_sum(d_first * xh1[...])
         sbw[2:3, :] = column_sum(d_first)
-        grad_out[...] = (dmid[...] + norm_back(d_first, xh1[...], rs1[...], row(0))).astype(BF16)
+
+    @pl.when(sec == 1)
+    def _():
+        back_first(handed_back.start)
+        summing(SUM_ONE[0])
+        handed_back.wait_send()
 
         @pl.when(crossed)
         def _():
@@ -809,11 +822,7 @@
         def _():
             grad_done.start()
 
-    @pl.when(sec == 1)
-    def _():
-        back_first()
-        handed_back.start()
-        for step in SUM_ONE + SUM_TWO:
+        for step in SUM_ONE[1:] + SUM_TWO:
             summing(step)
 
     for step in SUM_THREE:
@@ -826,9 +835,9 @@
     for cp in small_done:
         cp.start()
 
-    for part in PARTS:
-        await_sent(rs_sent[part][0], (30 if X_FIRST[part] else 15) * SIZE[part])
-        await_sent(rs_sent[part][1], (1 if X_FIRST[part] else 16) * SIZE[part])
+    await_sent(rs_rings_sent[0], 15 * by_x[0])
+    await_sent(rs_rings_sent[1], 30 * by_x[1])
+    await_sent(rs_x_sent, 16 * by_x[0] + by_x[1])
     for cp in (ex_first, ex_att, ex_second, ex_act, ex_gf, ex_dpre, ex_dbr, ex_dmix):
         cp.wait_send()
     small(sr.at[ox], sr_x, sm_xs, xp).wait_send()
@@ -841,10 +850,6 @@
         for cp in handed_on:
             cp.wait_send()
 
-    @pl.when(sec == 1)
-    def _():
-        handed_back.wait_send()
-
     @pl.when(crossed)
     def _():
         act_cross.wait()
@@ -862,7 +867,7 @@
         raise ValueError(taken)
 
 
-SEMAPHORES = 243
+SEMAPHORES = 210
 ARRIVALS = 186
 
 

time: 163 us -> 162 us (level)
  no operation moved by 1% of the time
where the time goes in v7:
time: 162 us
  Pallas kernels  161 us (99%)
    pallas_call x1, Pallas kernels, local(): pl.pallas_call(kernel, out_shape=results, in_specs=[vmem, vmem, vmem] + [...  159 us

profile of v7, /device:TPU:0, one launch (start us, length us, event | category | flops | bytes accessed | tf_op | source)
XLA Modules:
  0.0 162.1 jit_solution(4404091649371498769)
XLA Ops:
  0.6 159.1 %relay.1 = (bf16[128,1024]{1,0:T(8,128)(2,1)}, bf16[128,1024]{1,0:T(8,128)(2,1)}, f32[2,16]{1,0:T(2,128)}, f32[10,1,16]{2,1,0:T(1,128)}, f32[3,16,1024]{2,1,0:T(...) custom-call(s32[1,128]{1,0:T(1,128)} %bitcast.48, bf16[2,16]{1,0:T(2,128)(2,1)} %bitcast.49, ...), custom_call_target="tpu_custom_call" | custom-call | tf_op jit(solution)/shard_map/relay/pallas_call | solution.py:919
  159.7 2.1 %move.1 = (bf16[128,1024]{1,0:T(8,128)(2,1)}, bf16[128,1024]{1,0:T(8,128)(2,1)}, f32[2,16]{1,0:T(2,128)}, f32[10,1,16]{2,1,0:T(1,128)}, f32[3,16,1024]{2,1,0:T(8...) custom-call(bf16[128,1024]{1,0:T(8,128)(2,1)} %get-tuple-element.24.refs_0_, ...), custom_call_target="tpu_custom_call" | custom-call | tf_op jit(solution)/shard_map/move/pallas_call | solution.py:940

commit v8 on v7

--- a/solution.py
+++ b/solution.py
@@ -338,6 +338,38 @@
     for step in GATHER_ONE:
         gather(step)
 
+    by_x = [sum(SIZE[part] for part in PARTS if X_FIRST[part] == first) for first in (False, True)]
+
+    def gather_sent():
+        await_sent(ag_rings_sent[0], 15 * by_x[0])
+        await_sent(ag_rings_sent[1], 30 * by_x[1])
+        await_sent(ag_x_sent, 16 * by_x[0] + by_x[1])
+        await_sent(ag_sib_sent, 32 * 12)
+        rows = sb_y.at[pl.ds(1, 3)]
+        small(rows, rows, sm_y, sib).wait_send()
+        small(sb_c.at[0], sb_c.at[1], sm_c, sib).wait_send()
+        small(rows, rows, sm_z, sib).wait_send()
+        small(sb_x.at[x], sb_x.at[x], sm_x, xp).wait_send()
+
+    def column_sum(values):
+        return jnp.sum(values.astype(F32), axis=0, keepdims=True)
+
+    ex_sems = [(sem(), sem()) for _ in range(8)]
+
+    def exchange(slot, src, dst):
+        return remote(src, dst, *ex_sems[slot], sib)
+
+    def swap(slot, src, dst):
+        return exchange(slot, src.at[:, :, :, oc], dst)
+
+    ex_gf = swap(4, s_out, t_out)
+
+    def start_back():
+        sbw[...] = jnp.zeros_like(sbw)
+        sbw[11:12, :] = column_sum(gf[...])
+        s_out[...] = gf[...].T.reshape(2, 4, 4, 2, 1, 16, ROWS)
+        ex_gf.start()
+
     def from_sibling(part):
         await_arrival(ag_sib[part], 32 * SIZE[part])
 
@@ -373,6 +405,13 @@
         rbuf[128:160] = fc_weights(0).T.reshape(32, 2, 16, WIDTH)
         for j in range(1, 4):
             turned[j - 1] = fc_weights(j).T
+        @pl.when(crossed)
+        def _():
+            cot_cross.wait()
+
+        gf[...] = cotv[rows_at]
+        start_back()
+        gather_sent()
         for cp in handed_on:
             cp.wait_recv()
         xin[...] = hb[...].astype(F32)
@@ -382,11 +421,6 @@
         rs = lax.rsqrt(jnp.mean(centre * centre, axis=-1, keepdims=True) + EPS)
         hat = centre * rs
         return hat, rs, (hat * gain + shift).astype(BF16)
-
-    ex_sems = [(sem(), sem()) for _ in range(8)]
-
-    def exchange(slot, src, dst):
-        return remote(src, dst, *ex_sems[slot], sib)
 
     xh1[...], rs1[...], x1[0] = norm(xin[...], row(0), row(2))
     ex_first = exchange(0, x1.at[0], x1.at[1])
@@ -501,42 +535,16 @@
     def _():
         act_done.start()
 
-    by_x = [sum(SIZE[part] for part in PARTS if X_FIRST[part] == first) for first in (False, True)]
-    await_sent(ag_rings_sent[0], 15 * by_x[0])
-    await_sent(ag_rings_sent[1], 30 * by_x[1])
-    await_sent(ag_x_sent, 16 * by_x[0] + by_x[1])
-    await_sent(ag_sib_sent, 32 * 12)
-    rows = sb_y.at[pl.ds(1, 3)]
-    small(rows, rows, sm_y, sib).wait_send()
-    small(sb_c.at[0], sb_c.at[1], sm_c, sib).wait_send()
-    small(rows, rows, sm_z, sib).wait_send()
-    small(sb_x.at[x], sb_x.at[x], sm_x, xp).wait_send()
+    @pl.when(sec == 0)
+    def _():
+        gather_sent()
 
     @pl.when(sec == 0)
     def _():
         handed_back.wait_recv()
         gf[...] = hb[...]
-
-    @pl.when(sec == 1)
-    def _():
-        @pl.when(crossed)
-        def _():
-            cot_cross.wait()
-
-        gf[...] = cotv[rows_at]
-
-    def column_sum(values):
-        return jnp.sum(values.astype(F32), axis=0, keepdims=True)
-
-    sbw[...] = jnp.zeros_like(sbw)
-    sbw[11:12, :] = column_sum(gf[...])
-    s_out[...] = gf[...].T.reshape(2, 4, 4, 2, 1, 16, ROWS)
-
-    def swap(slot, src, dst):
-        return exchange(slot, src.at[:, :, :, oc], dst)
-
-    ex_gf = swap(4, s_out, t_out)
-    ex_gf.start()
+        start_back()
+
     for j in range(4):
         d_act = jnp.dot(gf[...], wout_weights(j), preferred_element_type=F32)
         d_pre = (dgel[j] * d_act).astype(BF16)

time: 162 us -> 162 us (level)
  no operation moved by 1% of the time
where the time goes in v8:
time: 162 us
  Pallas kernels  161 us (99%)
    pallas_call x1, Pallas kernels, local(): pl.pallas_call(kernel, out_shape=results, in_specs=[vmem, vmem, vmem] + [...  159 us

profile of v8, /device:TPU:0, one launch (start us, length us, event | category | flops | bytes accessed | tf_op | source)
XLA Modules:
  0.0 162.0 jit_solution(5170737643160853955)
XLA Ops:
  0.6 159.0 %relay.1 = (bf16[128,1024]{1,0:T(8,128)(2,1)}, bf16[128,1024]{1,0:T(8,128)(2,1)}, f32[2,16]{1,0:T(2,128)}, f32[10,1,16]{2,1,0:T(1,128)}, f32[3,16,1024]{2,1,0:T(...) custom-call(s32[1,128]{1,0:T(1,128)} %bitcast.48, bf16[2,16]{1,0:T(2,128)(2,1)} %bitcast.49, ...), custom_call_target="tpu_custom_call" | custom-call | tf_op jit(solution)/shard_map/relay/pallas_call | solution.py:927
  159.7 2.1 %move.1 = (bf16[128,1024]{1,0:T(8,128)(2,1)}, bf16[128,1024]{1,0:T(8,128)(2,1)}, f32[2,16]{1,0:T(2,128)}, f32[10,1,16]{2,1,0:T(1,128)}, f32[3,16,1024]{2,1,0:T(8...) custom-call(bf16[128,1024]{1,0:T(8,128)(2,1)} %get-tuple-element.24.refs_0_, ...), custom_call_target="tpu_custom_call" | custom-call | tf_op jit(solution)/shard_map/move/pallas_call | solution.py:948
